TPU v7x, 128 devices: a whole 4x4x4 slice. The times are simulated.
128 devices in a mesh: slab: 16 (over y, x), mp: 8 (over z, core), dp: 1.
Axes of the slice: x: 4, y: 4, z: 4, core: 2. Of those that a mesh axis runs over, the one named last changes fastest.
Arguments:
- enc_feat: bfloat16 [64, 512, 256], P(('dp', 'slab'), 'mp'), may hold values from -120 to 120
- gn_gain: float32 [512], P('mp'), may hold values from 0.1 to 1.9
- gn_bias: float32 [512], P('mp'), may hold values from -3 to 3
- conv_w: bfloat16 [512, 432], P('mp'), may hold values from -0.0546875 to 0.0546875
- clip_frames: int32 [4], P('dp'), may hold values from 1 to 32, 64 in all
- clip_res: int32 [4, 2], P('dp'), may hold values from 8 to 16, as said below
- token_place: int32 [4096], P(('dp', 'slab')), may hold values from 0 to 4095, each once
- embed_w: bfloat16 [64, 3072], replicated, may hold values from -0.75 to 0.75
- embed_b: float32 [3072], replicated, may hold values from -3 to 3
- mod_shift: float32 [3072], P('dp'), may hold values from -3 to 3
- mod_scale: float32 [3072], P('dp'), may hold values from -2 to 2
- mod_gate: float32 [3072], P('dp'), may hold values from -4 to 4
- w_qkv: bfloat16 [3072, 6144], P(None, 'mp'), may hold values from -0.109375 to 0.109375
- q_gain: float32 [128], replicated, may hold values from 0.1 to 1.9
- k_gain: float32 [128], replicated, may hold values from 0.1 to 1.9
- w_out: bfloat16 [2048, 3072], P('mp'), may hold values from -0.125 to 0.125
- grad_out: bfloat16 [4096, 3072], P(('dp', 'slab'), 'mp'), may hold values from -6 to 6
Outputs:
- latents: float32 [64, 16, 256], P(('dp', 'slab'))
- block_out: bfloat16 [4096, 3072], P(('dp', 'slab'), 'mp')
- g_qkv: float32 [3072, 6144], P(('dp', 'slab'), 'mp')
- g_out: float32 [2048, 3072], P(('dp', 'mp'), 'slab')
- g_embed: float32 [64, 3072], P('dp', 'mp')
Inputs may be any that keep to these rules, and one draw needn't show every extreme that they name: `clip_frames`: frames of each clip; they sum to 64 and the longest has exactly 32. `clip_res`: even latent heights and widths; some clip has the full 16 x 16 grid. `token_place`: a permutation of the 4096 positions.
All inputs are finite; a program needn't handle non-finite values.
Results may differ from a plain program's by a relative error of at most 0.024.
Values may be sent and summed in bfloat16 or wider, within the bound.
No kernel may reach another device: no remote copies, remote signals or barrier semaphores. Data moves between devices by JAX's collectives and lax.ppermute only.
A program may use at most 128 MiB of HBM per device.

v0:
```python
import jax
import jax.numpy as jnp
from jax import lax
from jax.sharding import PartitionSpec as P

D = 3072
HD = 128
LAT = 16
CLIPS = 4
SIDE = 16
PSIDE = 8
CELLS = 256
GS = 16


EPSILON = 1e-06
HIGHEST = lax.Precision.HIGHEST


def shifted(value, axis, by):
    devices = lax.axis_size(axis)
    pairs = [(i, i + by) for i in range(devices) if 0 <= i + by < devices]
    return lax.ppermute(value, axis, pairs)


def rms_scale(values):
    return lax.rsqrt(jnp.mean(values * values, axis=-1, keepdims=True) + EPSILON)


def rms_back(grad_hat, normed, inverse, weight):
    scaled = grad_hat * weight
    return inverse * (scaled - normed * jnp.mean(scaled * normed, axis=-1, keepdims=True))


def head_weights(scores, log_total, allowed):
    return jnp.exp(jnp.where(allowed, scores - log_total[:, None], -1e30))


def body(
    enc_feat,
    gn_gain,
    gn_bias,
    conv_w,
    clip_frames,
    clip_res,
    token_place,
    embed_w,
    embed_b,
    mod_shift,
    mod_scale,
    mod_gate,
    w_qkv,
    q_gain,
    k_gain,
    w_out,
    grad_out,
):
    slabs = lax.axis_size("slab")
    slab_pos = lax.axis_index("slab")
    mp_size = lax.axis_size("mp")
    mp_pos = lax.axis_index("mp")
    frames_dev = enc_feat.shape[0]
    channels = enc_feat.shape[1]
    clip_ends = jnp.cumsum(clip_frames)
    clip_starts = clip_ends - clip_frames
    first_frame = slab_pos * frames_dev
    frame_id = first_frame + jnp.arange(frames_dev, dtype=jnp.int32)
    clip_of = jnp.sum((frame_id[:, None] >= clip_ends[None, :]).astype(jnp.int32), axis=1)
    member_int = (clip_of[:, None] == jnp.arange(CLIPS, dtype=jnp.int32)[None, :]).astype(jnp.int32)
    member = member_int.astype(jnp.float32)
    height = jnp.sum(member_int * clip_res[None, :, 0], axis=1)
    width_of = jnp.sum(member_int * clip_res[None, :, 1], axis=1)
    start_of = jnp.sum(member_int * clip_starts[None, :], axis=1)
    cell_id = jnp.arange(CELLS, dtype=jnp.int32)
    valid = (
        (cell_id[None, :] // SIDE < height[:, None]) & (cell_id[None, :] % SIDE < width_of[:, None])
    ).astype(jnp.float32)
    groups_dev = channels // GS
    features = enc_feat.astype(jnp.float32).reshape(frames_dev, groups_dev, GS, CELLS)
    masked = features * valid[:, None, None, :]
    group_sum, group_sq = lax.psum(
        (
            jnp.dot(member.T, jnp.sum(masked, axis=(2, 3)), precision=HIGHEST),
            jnp.dot(member.T, jnp.sum(masked * features, axis=(2, 3)), precision=HIGHEST),
        ),
        "slab",
    )
    counts = (clip_frames * clip_res[:, 0] * clip_res[:, 1] * GS).astype(jnp.float32)
    group_mean = group_sum / counts[:, None]
    group_rstd = lax.rsqrt(group_sq / counts[:, None] - group_mean * group_mean + EPSILON)
    frame_mean = jnp.dot(member, group_mean, precision=HIGHEST)
    frame_rstd = jnp.dot(member, group_rstd, precision=HIGHEST)
    normed = (features - frame_mean[:, :, None, None]) * frame_rstd[:, :, None, None]
    activated = (
        jax.nn.silu(
            normed.reshape(frames_dev, channels, CELLS) * gn_gain[None, :, None]
            + gn_bias[None, :, None]
        )
        * valid[:, None, :]
    )
    activated = activated.astype(jnp.bfloat16)
    rim_frames = shifted(activated[frames_dev - 2 :], "slab", 1)
    extended = jnp.concatenate([rim_frames, activated], axis=0)
    projected = jnp.einsum("fin,ik->fkn", extended, conv_w, preferred_element_type=jnp.float32)
    tap_table = projected.reshape(frames_dev + 2, 3, 3, 3, LAT, SIDE, SIDE)
    conv_sum = jnp.zeros((frames_dev, LAT, SIDE, SIDE), jnp.float32)
    for step_t in range(3):
        source = jnp.maximum(frame_id - 2 + step_t, start_of) - first_frame + 2
        chosen = jnp.take(tap_table[:, step_t], source, axis=0)
        padded = jnp.pad(chosen, ((0, 0), (0, 0), (0, 0), (0, 0), (1, 1), (1, 1)))
        for step_y in range(3):
            for step_x in range(3):
                conv_sum = (
                    conv_sum
                    + padded[:, step_y, step_x, :, step_y : step_y + SIDE, step_x : step_x + SIDE]
                )
    latents = lax.psum(conv_sum.reshape(frames_dev, LAT, CELLS).astype(jnp.bfloat16), "mp").astype(
        jnp.float32
    )
    shard_rows = frames_dev * PSIDE * PSIDE
    patches = (
        latents.reshape(frames_dev, LAT, PSIDE, 2, PSIDE, 2)
        .transpose(0, 2, 4, 1, 3, 5)
        .reshape(shard_rows, 4 * LAT)
        .astype(jnp.bfloat16)
    )
    patch_id = jnp.arange(PSIDE, dtype=jnp.int32)
    tok_valid = (
        (
            (2 * patch_id[None, :, None] < height[:, None, None])
            & (2 * patch_id[None, None, :] < width_of[:, None, None])
        )
        .astype(jnp.int32)
        .reshape(shard_rows)
    )
    tok_code = (jnp.repeat(clip_of, PSIDE * PSIDE) + 1) * 2 + tok_valid
    target = token_place // shard_rows
    slot_pos = token_place % shard_rows
    send_rows = (
        jnp.zeros((slabs, shard_rows, 4 * LAT), jnp.bfloat16).at[target, slot_pos].set(patches)
    )
    send_code = jnp.zeros((slabs, shard_rows), jnp.int32).at[target, slot_pos].set(tok_code)
    got_rows, got_code = (
        lax.all_to_all(send_rows, "slab", split_axis=0, concat_axis=0, tiled=True),
        lax.all_to_all(send_code, "slab", split_axis=0, concat_axis=0, tiled=True),
    )
    sequence = jnp.sum(got_rows, axis=0)
    seq_code = jnp.sum(got_code, axis=0).astype(jnp.int32)
    hidden = (jnp.dot(sequence, embed_w, preferred_element_type=jnp.float32) + embed_b).astype(
        jnp.bfloat16
    )
    hidden_f = hidden.astype(jnp.float32)
    centered = hidden_f - jnp.mean(hidden_f, axis=-1, keepdims=True)
    ln_rstd = lax.rsqrt(jnp.mean(centered * centered, axis=-1, keepdims=True) + EPSILON)
    xnorm = centered * ln_rstd
    modded = (xnorm * (1.0 + mod_scale) + mod_shift).astype(jnp.bfloat16)
    heads_dev = w_out.shape[0] // HD
    qkv_out = jnp.dot(modded, w_qkv, preferred_element_type=jnp.float32).reshape(
        shard_rows, heads_dev, 3, HD
    )
    q_inv = rms_scale(qkv_out[:, :, 0])
    q_norm = qkv_out[:, :, 0] * q_inv
    k_inv = rms_scale(qkv_out[:, :, 1])
    k_norm = qkv_out[:, :, 1] * k_inv
    queries = (q_norm * q_gain).astype(jnp.bfloat16)
    keys_dev = (k_norm * k_gain).astype(jnp.bfloat16)
    values_dev = qkv_out[:, :, 2].astype(jnp.bfloat16)
    keys_all, values_all, code_all = (
        lax.all_gather(keys_dev, "slab", axis=0, tiled=True),
        lax.all_gather(values_dev, "slab", axis=0, tiled=True),
        lax.all_gather(seq_code, "slab", axis=0, tiled=True),
    )
    allowed = (code_all[None, :] // 2 == seq_code[:, None] // 2) & (code_all[None, :] % 2 == 1)
    score_scale = HD ** (-0.5)
    out_list = []
    lse_list = []
    for head_num in range(heads_dev):
        scores = (
            jnp.einsum(
                "qe,ke->qk",
                queries[:, head_num],
                keys_all[:, head_num],
                preferred_element_type=jnp.float32,
            )
            * score_scale
        )
        masked_s = jnp.where(allowed, scores, -1e30)
        row_top = jnp.max(masked_s, axis=-1, keepdims=True)
        log_total = row_top[:, 0] + jnp.log(jnp.sum(jnp.exp(masked_s - row_top), axis=-1))
        weights = head_weights(scores, log_total, allowed)
        out_list.append(
            jnp.dot(
                weights.astype(jnp.bfloat16),
                values_all[:, head_num],
                preferred_element_type=jnp.float32,
            ).astype(jnp.bfloat16)
        )
        lse_list.append(log_total)
    attended = jnp.stack(out_list, axis=1)
    lse_rows = jnp.stack(lse_list, axis=1)
    flat_heads = attended.reshape(shard_rows, heads_dev * HD)
    attn_cols = lax.psum_scatter(
        jnp.dot(flat_heads, w_out, preferred_element_type=jnp.float32).astype(jnp.bfloat16),
        "mp",
        scatter_dimension=1,
        tiled=True,
    ).astype(jnp.float32)
    cols_dev = D // mp_size
    col_first = mp_pos * cols_dev
    hidden_cols = lax.dynamic_slice_in_dim(hidden_f, col_first, cols_dev, 1)
    gate_cols = lax.dynamic_slice_in_dim(mod_gate, col_first, cols_dev, 0)
    block_out = (hidden_cols + gate_cols * attn_cols).astype(jnp.bfloat16)
    cotangent = lax.all_gather(grad_out, "mp", axis=1, tiled=True)
    d_attn = (mod_gate * cotangent.astype(jnp.float32)).astype(jnp.bfloat16)
    g_out = lax.psum_scatter(
        jnp.dot(flat_heads.T, d_attn, preferred_element_type=jnp.float32).astype(jnp.bfloat16),
        "slab",
        scatter_dimension=1,
        tiled=True,
    ).astype(jnp.float32)
    d_out = (
        jnp.dot(d_attn, w_out.T, preferred_element_type=jnp.float32)
        .astype(jnp.bfloat16)
        .reshape(shard_rows, heads_dev, HD)
    )
    delta_rows = jnp.sum(d_out.astype(jnp.float32) * attended.astype(jnp.float32), axis=-1)
    grad_q_list = []
    score_list = []
    prob_list = []
    for head_num in range(heads_dev):
        scores = (
            jnp.einsum(
                "qe,ke->qk",
                queries[:, head_num],
                keys_all[:, head_num],
                preferred_element_type=jnp.float32,
            )
            * score_scale
        )
        weights = head_weights(scores, lse_rows[:, head_num], allowed)
        d_prob = jnp.einsum(
            "qe,ke->qk",
            d_out[:, head_num],
            values_all[:, head_num],
            preferred_element_type=jnp.float32,
        )
        d_score = (weights * (d_prob - delta_rows[:, head_num, None])).astype(jnp.bfloat16)
        grad_q_list.append(
            jnp.dot(d_score, keys_all[:, head_num], preferred_element_type=jnp.float32)
            * score_scale
        )
        score_list.append(d_score)
        prob_list.append(weights.astype(jnp.bfloat16))
    score_all = jnp.stack(score_list, axis=0)
    prob_all = jnp.stack(prob_list, axis=0)
    grad_keys = (
        jnp.einsum("hqk,qhe->khe", score_all, queries, preferred_element_type=jnp.float32)
        * score_scale
    )
    grad_values = jnp.einsum("hqk,qhe->khe", prob_all, d_out, preferred_element_type=jnp.float32)
    own_grads = (
        lax.psum_scatter(
            jnp.stack([grad_keys, grad_values], axis=2)
            .reshape(shard_rows * lax.axis_size("slab"), heads_dev * 2 * HD)
            .astype(jnp.bfloat16),
            "slab",
            scatter_dimension=0,
            tiled=True,
        )
        .astype(jnp.float32)
        .reshape(shard_rows, heads_dev, 2, HD)
    )
    grad_k = own_grads[:, :, 0]
    grad_v = own_grads[:, :, 1]
    dq_raw = rms_back(jnp.stack(grad_q_list, axis=1), q_norm, q_inv, q_gain)
    dk_raw = rms_back(grad_k, k_norm, k_inv, k_gain)
    d_qkv = (
        jnp.stack([dq_raw, dk_raw, grad_v], axis=2)
        .reshape(shard_rows, heads_dev * 3 * HD)
        .astype(jnp.bfloat16)
    )
    g_qkv = lax.psum_scatter(
        jnp.dot(modded.T, d_qkv, preferred_element_type=jnp.float32).astype(jnp.bfloat16),
        "slab",
        scatter_dimension=0,
        tiled=True,
    ).astype(jnp.float32)
    d_mod_part = jnp.dot(d_qkv, w_qkv.T, preferred_element_type=jnp.float32)
    xnorm_cols = lax.dynamic_slice_in_dim(xnorm, col_first, cols_dev, 1)
    d_mod = lax.psum(d_mod_part.astype(jnp.bfloat16), "mp").astype(jnp.float32)
    d_norm = d_mod * (1.0 + mod_scale)
    mean_one = jnp.mean(d_norm, axis=-1, keepdims=True)
    mean_two = jnp.mean(d_norm * xnorm, axis=-1, keepdims=True)
    d_norm_cols = lax.dynamic_slice_in_dim(d_norm, col_first, cols_dev, 1)
    d_hidden = grad_out.astype(jnp.float32) + ln_rstd * (
        d_norm_cols - mean_one - xnorm_cols * mean_two
    )
    g_embed = lax.psum(
        jnp.dot(sequence.astype(jnp.float32).T, d_hidden, precision=HIGHEST).astype(jnp.bfloat16),
        "slab",
    ).astype(jnp.float32)
    return (latents, block_out, g_qkv, g_out, g_embed)


def solution(mesh):
    in_specs = (
        P(("dp", "slab"), "mp", None),
        P("mp"),
        P("mp"),
        P("mp", None),
        P("dp"),
        P("dp", None),
        P(("dp", "slab")),
        P(),
        P(),
        P("dp"),
        P("dp"),
        P("dp"),
        P(None, "mp"),
        P(),
        P(),
        P("mp", None),
        P(("dp", "slab"), "mp"),
    )
    out_specs = (
        P(("dp", "slab"), None, None),
        P(("dp", "slab"), "mp"),
        P(("dp", "slab"), "mp"),
        P(("dp", "mp"), "slab"),
        P("dp", "mp"),
    )
    return jax.shard_map(body, mesh=mesh, in_specs=in_specs, out_specs=out_specs, check_vma=False)
```

profile of v0, /device:TPU:0, one launch (start us, length us, event | category | flops | bytes accessed | tf_op | source)
XLA Modules:
  0.0 688.5 jit_solution(7059284607434209081)
XLA Ops:
  12.7 40.8 %all-reduce.3 = (f32[4,4]{1,0:T(4,128)S(1)}, f32[4,4]{1,0:T(4,128)S(1)}) all-reduce(f32[4,4]{1,0:T(4,128)S(1)} %fusion.92, f32[4,4]{1,0:T(4,128)S(1)} %fusion.96), channel_id=1, replica_groups=mesh['slab'=16,'mp'=8,'dp'=1] {'slab'}, use_global_device_ids=true, to_apply=%region_9.10 | all-reduce | flops 32 | bytes 256 | tf_op jit(solution)/shard_map/psum | solution.py:81
  58.5 2.9 convolution_bitcast_fusion
  61.4 12.8 %reshape.503 = f32[6,3,3,3,16,16,16]{6,5,4,3,2,1,0:T(8,128)} reshape(f32[6,432,256]{2,1,0:T(8,128)} %convolution_bitcast_fusion) | data formatting | bytes 5308416 | tf_op jit(solution)/shard_map/reshape | solution.py:105
  74.2 15.1 %slice_bitcast_fusion.2 = (f32[6,3,3,16,16,16]{5,4,3,2,1,0:T(8,128)}, f32[6,3,3,16,16,16]{5,4,3,2,1,0:T(8,128)}, f32[6,3,3,16,16,16]{5,4,3,2,1,0:T(8,128)}) fusion(f32[6,3,3,3,16,16,16]{6,5,4,3,2,1,0:T(8,128)} %reshape.503), kind=kLoop, calls=%fused_computation.31 | loop fusion | bytes 5308416 | tf_op jit(solution)/shard_map/squeeze | solution.py:109
  89.4 6.0 gather_fusion.1
  95.4 5.2 broadcast_select_fusion.1
  100.6 6.0 gather_fusion
  106.6 3.2 broadcast_select_fusion.2
  112.6 6.0 gather_fusion.2
  118.5 3.1 broadcast_select_fusion
  121.6 3.1 pad_slice_fusion.7
  126.0 2.1 copy.118
  128.1 2.1 copy.119
  134.3 2.1 copy.122
  136.4 2.1 copy.123
  138.4 2.1 copy.124
  142.6 2.5 add_convert_fusion.1
  145.1 27.9 %psum.37 = bf16[4,16,256]{1,2,0:T(8,128)(2,1)S(1)} all-reduce(bf16[4,16,256]{1,2,0:T(8,128)(2,1)S(1)} %add_convert_fusion.1), channel_id=1, replica_groups=mesh['slab'=16,'mp'=8,'dp'=1] {'mp'}, use_global_device_ids=true, to_apply=%region_11.13 | all-reduce | flops 16384 | bytes 65536 | tf_op jit(solution)/shard_map/psum | solution.py:117
  175.1 12.2 %scatter_fusion = bf16[16,256,64]{2,1,0:T(8,128)(2,1)S(1)} fusion(bf16[16,256,64]{2,1,0:T(8,128)(2,1)S(1)} %broadcast_in_dim.27, s32[256]{0:T(256)S(1)} %bitcast.182, bf16[256,64]{1,0:T(8,128)(2,1)S(1)} %copy.127), kind=kCustom, calls=%fused_computation.3 | custom fusion | bytes 100352 | tf_op jit(solution)/shard_map/scatter | solution.py:140
  188.4 4.1 all-to-all-start
  192.6 10.1 %all-to-all-done = bf16[16,256,64]{1,2,0:T(8,128)(2,1)S(1)} async-done(((bf16[16,256,64]{1,2,0:T(8,128)(2,1)}), bf16[16,256,64]{1,2,0:T(8,128)(2,1)S(1)}, u32[]{:S(2)}, u32[]{:S(2)}) %all-to-all-start) | async-done | bytes 524320 | tf_op jit(solution)/shard_map/all_to_all | solution.py:144
  206.2 2.1 fusion.42
  210.4 13.1 %scatter_fusion.1 = s32[16,256]{1,0:T(8,128)S(1)} fusion(s32[16,256]{1,0:T(8,128)S(1)} %broadcast_in_dim.30, s32[256]{0:T(256)S(1)} %bitcast.183, s32[256]{0:T(256)S(1)} %add.357), kind=kCustom, calls=%fused_computation.4 | custom fusion | bytes 5120 | tf_op jit(solution)/shard_map/scatter | solution.py:142
  224.1 3.5 all-to-all-start.1
  228.4 6.7 all-to-all-done.1
  235.2 21.4 %all-gather.1 = s32[16,1,256]{2,1,0:T(1,128)S(1)} all-gather(s32[1,1,256]{2,1,0:T(1,128)S(1)} %bitcast.226), channel_id=1, replica_groups=mesh['slab'=16,'mp'=8,'dp'=1] {'slab'}, dimensions={0}, use_global_device_ids=true | all-gather | bytes 17408 | tf_op jit(solution)/shard_map/all_gather | solution.py:171
  256.7 2.8 fusion.17
  261.4 4.4 exponential_reduce_fusion.1
  265.8 37.4 %all-gather.10.cloned.1.call-done = bf16[4096,2,1,128]{0,3,2,1:T(8,128)(2,1)} async-done(((bf16[256,2,1,128]{0,3,2,1:T(8,128)(2,1)}), bf16[4096,2,1,128]{0,3,2,1:T(8,128)(2,1)}) %all-gather.10.cloned.1.call-update) | async-done | bytes 2097168 | tf_op jit(solution)/shard_map/all_gather | solution.py:170
  303.2 4.2 copy.133
  307.5 3.7 exponential_reduce_fusion
  311.3 3.8 fusion.19
  318.1 11.2 %all-gather.8.cloned.1.call-done = bf16[256,3072]{1,0:T(8,128)(2,1)} async-done(((bf16[256,384]{1,0:T(8,128)(2,1)}), bf16[256,3072]{1,0:T(8,128)(2,1)}) %all-gather.8.cloned.1.call-update) | async-done | bytes 1572880 | tf_op jit(solution)/shard_map/all_gather | solution.py:213
  329.3 2.2 multiply_reduce_fusion.2
  331.5 4.2 fusion.3
  341.9 2.2 copy.134
  346.0 2.6 copy.140
  348.8 3.3 convolution_convert_fusion.3
  352.2 2.9 convolution_multiply_fusion.4
  355.1 2.7 convolution_multiply_fusion.3
  357.8 63.9 %reduce-scatter.7.cloned.1.call-done = bf16[256,512]{0,1:T(8,128)(2,1)} async-done(((bf16[4096,512]{0,1:T(8,128)(2,1)}), bf16[256,512]{0,1:T(8,128)(2,1)}) %reduce-scatter.7.cloned.1.call-update) | async-done | bytes 262160 | tf_op jit(solution)/shard_map/reduce_scatter | solution.py:262
  424.9 5.0 convolution_convert_fusion.2
  429.9 5.5 convolution_convert_fusion.1
  436.2 20.2 %reduce-scatter.13.cloned.1.call-done = bf16[384,256]{1,0:T(8,128)(2,1)} async-done(((bf16[3072,256]{1,0:T(8,128)(2,1)}), bf16[384,256]{1,0:T(8,128)(2,1)}) %reduce-scatter.13.cloned.1.call-update) | async-done | bytes 196624
  457.5 74.5 %reduce-scatter.11.cloned.1.call-done = bf16[256,192]{0,1:T(8,128)(2,1)} async-done(((bf16[256,3072]{0,1:T(8,128)(2,1)}), bf16[256,192]{0,1:T(8,128)(2,1)}) %reduce-scatter.11.cloned.1.call-update) | async-done | bytes 98320 | tf_op jit(solution)/shard_map/reduce_scatter | solution.py:215
  535.3 62.9 %all-reduce.6.cloned.1.call-done = bf16[256,3072]{1,0:T(8,128)(2,1)} async-done(((bf16[256,3072]{1,0:T(8,128)(2,1)}), bf16[256,3072]{1,0:T(8,128)(2,1)}) %all-reduce.6.cloned.1.call-update) | async-done | bytes 1572880 | tf_op jit(solution)/shard_map/psum | solution.py:290
  598.2 3.2 fusion.22
  602.8 74.6 %psum.39 = bf16[64,384]{1,0:T(8,128)(2,1)S(1)} all-reduce(bf16[64,384]{1,0:T(8,128)(2,1)S(1)} %convolution_convert_fusion.7), channel_id=1, replica_groups=mesh['slab'=16,'mp'=8,'dp'=1] {'slab'}, use_global_device_ids=true, to_apply=%region_34.36 | all-reduce | flops 24576 | bytes 98304 | tf_op jit(solution)/shard_map/psum | solution.py:298
  (167 shorter events, 58.0 us)
Async XLA Ops:
  7.2 322.1 %copy-start = (bf16[256,3072]{1,0:T(8,128)(2,1)S(1)}, bf16[256,3072]{1,0:T(8,128)(2,1)}, u32[]{:S(2)}) copy-start(bf16[256,3072]{1,0:T(8,128)(2,1)} %param.34) | copy-start | bytes 4718596
  55.4 3.2 collective-permute-start
  106.6 3.8 copy-start.3
  145.1 47.5 %copy-start.18 = (f32[3072]{0:T(1024)S(1)}, f32[3072]{0:T(1024)}, u32[]{:S(2)}) copy-start(f32[3072]{0:T(1024)} %param.29) | copy-start | bytes 36868
  145.1 57.6 %copy-start.17 = (f32[3072]{0:T(1024)S(1)}, f32[3072]{0:T(1024)}, u32[]{:S(2)}) copy-start(f32[3072]{0:T(1024)} %param.27) | copy-start | bytes 36868
  173.0 29.7 %copy-start.14 = (bf16[64,3072]{1,0:T(8,128)(2,1)S(1)}, bf16[64,3072]{1,0:T(8,128)(2,1)}, u32[]{:S(2)}) copy-start(bf16[64,3072]{1,0:T(8,128)(2,1)} %param.26) | copy-start | bytes 1179652
  188.4 14.2 %all-to-all-start = ((bf16[16,256,64]{1,2,0:T(8,128)(2,1)}), bf16[16,256,64]{1,2,0:T(8,128)(2,1)S(1)}, u32[]{:S(2)}, u32[]{:S(2)}) async-start(bf16[16,256,64]{1,2,0:T(8,128)(2,1)} %copy.128), calls=%async_computation | async-start | bytes 1048576 | tf_op jit(solution)/shard_map/all_to_all | solution.py:144
  192.5 64.1 %all-gather.6.cloned.1.call-start = ((), (), s32[]{:S(2)}) async-start(), calls=%async_computation.6 | async-start | bytes 2228224 | tf_op jit(solution)/shard_map/all_gather | solution.py:169
  202.8 3.3 slice-start
  203.4 1.8 copy-start.1
  203.5 2.6 copy-start.15
  203.5 2.7 slice-start.1
  206.2 2.1 copy-start.2
  206.2 2.2 copy-start.19
  206.2 2.2 copy-start.20
  209.2 94.0 %all-gather.10.cloned.1.call-start = ((), (), s32[]{:S(2)}) async-start(), calls=%async_computation.12 | async-start | bytes 2228224 | tf_op jit(solution)/shard_map/all_gather | solution.py:170
  224.1 11.0 %all-to-all-start.1 = ((s32[16,1,256]{2,1,0:T(1,128)}), s32[16,1,256]{2,1,0:T(1,128)S(1)}, u32[]{:S(2)}, u32[]{:S(2)}) async-start(s32[16,1,256]{2,1,0:T(1,128)} %copy.129), calls=%async_computation.1 | async-start | bytes 32768 | tf_op jit(solution)/shard_map/all_to_all | solution.py:145
  227.6 101.6 %all-gather.8.cloned.1.call-start = ((), (), s32[]{:S(2)}) async-start(), calls=%async_computation.7 | async-start | bytes 1769472 | tf_op jit(solution)/shard_map/all_gather | solution.py:213
  228.4 193.3 %reduce-scatter.7.cloned.1.call-start = ((), (), s32[]{:S(2)}) async-start(), calls=%async_computation.8 | async-start | bytes 4456448 | tf_op jit(solution)/shard_map/reduce_scatter | solution.py:262
  256.7 4.8 copy-start.21
  259.4 2.0 copy-start.12
  307.5 3.8 copy-start.8
  311.3 5.1 copy-start.10
  315.1 1.3 copy-start.4
  315.1 2.1 copy-start.6
  315.1 14.1 %copy-start.16 = (f32[3072]{0:T(1024)S(1)}, f32[3072]{0:T(1024)}, u32[]{:S(2)}) copy-start(f32[3072]{0:T(1024)} %param.30) | copy-start | bytes 36868
  329.3 2.2 copy-start.11
  331.5 4.3 copy-start.9
  335.7 2.0 copy-start.22
  337.7 1.3 copy-start.23
  337.7 2.3 copy-start.5
  337.7 3.0 copy-start.7
  344.1 112.3 %reduce-scatter.13.cloned.1.call-start = ((), (), s32[]{:S(2)}) async-start(), calls=%async_computation.13 | async-start | bytes 1769472
  348.6 183.4 %reduce-scatter.11.cloned.1.call-start = ((), (), s32[]{:S(2)}) async-start(), calls=%async_computation.10 | async-start | bytes 1671168 | tf_op jit(solution)/shard_map/reduce_scatter | solution.py:215
  352.2 246.0 %all-reduce.6.cloned.1.call-start = ((), (), s32[]{:S(2)}) async-start(), calls=%async_computation.11 | async-start | bytes 3145728 | tf_op jit(solution)/shard_map/psum | solution.py:290
  429.8 249.7 %reduce-scatter.9.cloned.1.call-start = ((), (), s32[]{:S(2)}) async-start(), calls=%async_computation.9 | async-start | bytes 5013504 | tf_op jit(solution)/shard_map/reduce_scatter | solution.py:282
  533.6 67.8 %copy-start.13 = (bf16[256,384]{1,0:T(8,128)(2,1)S(1)}, bf16[256,384]{1,0:T(8,128)(2,1)}, u32[]{:S(2)}) copy-start(bf16[256,384]{1,0:T(8,128)(2,1)} %param.35) | copy-start | bytes 589828
Sparse Core Ops, SparseCore 0:
  209.4 44.0 all-gather.5
  256.1 47.0 all-gather.9
  304.9 24.2 all-gather.7
  344.3 77.3 reduce-scatter.6
  424.1 32.2 reduce-scatter.12
  459.8 72.1 reduce-scatter.10
  534.5 63.6 all-reduce.5
  601.9 77.6 reduce-scatter.8
where the time goes:
time: 698 us; the launch traced here: 688 us
  waiting for transfers between devices  291 us (42%)
  blocking collectives  165 us (24%)
  local copies, waits for them, and re-layouts  118 us (17%)
  matrix products  48 us (7%)
  other arithmetic  42 us (6%)
  between operations  15 us (2%)
  starting transfers between devices  9.42 us (1%)
    psum x1, blocking collectives, body(): lax.psum(jnp.dot(sequence.astype(jnp.float32).T, d_hidden, precision=HIGH...  74.6 us
    reduce_scatter x1, waiting for transfers between devices, body(): lax.psum_scatter(jnp.dot(flat_heads.T, d_attn, preferred_element_type=jnp...  74.5 us
    reduce_scatter x1, waiting for transfers between devices, body(): lax.psum_scatter(jnp.stack([grad_keys, grad_values], axis=2).reshape(shar...  63.9 us
    psum x1, waiting for transfers between devices, body(): d_mod = lax.psum(d_mod_part.astype(jnp.bfloat16), 'mp').astype(jnp.float32)  62.9 us
    psum x1, blocking collectives, body(): lax.psum((jnp.dot(member.T, jnp.sum(masked, axis=(2, 3)), precision=HIGHE...  40.8 us
    all_gather x1, waiting for transfers between devices, body(): lax.all_gather(values_dev, 'slab', axis=0, tiled=True)  37.4 us
    psum x1, blocking collectives, body(): lax.psum(conv_sum.reshape(frames_dev, LAT, CELLS).astype(jnp.bfloat16), '...  27.9 us
    all_gather x1, blocking collectives, body(): lax.all_gather(seq_code, 'slab', axis=0, tiled=True)  21.4 us
  transfers between devices with their start and end apart: 11, of which 10 were waited for; matrix products, arithmetic and copies ran while one was open for 11% of the time, Pallas kernels for 0%

commit v1 on v0

v1 whole, which is shorter than its diff:
```python
import functools

import jax
import jax.numpy as jnp
from jax import lax
from jax.experimental import pallas as pl
from jax.experimental.pallas import tpu as pltpu
from jax.sharding import PartitionSpec as P

D = 3072
HD = 128
LAT = 16
CLIPS = 4
SIDE = 16
PSIDE = 8
CELLS = 256
GS = 16
HEADS = 2
ROWS = 256
FRAMES = 4
FEAT = 64
AUG = 80
EXT = 144
EPSILON = 1e-06
HIGHEST = lax.Precision.HIGHEST
LOG2E = 1.4426950408889634
OFF = -1e30
F32 = jnp.float32
BF16 = jnp.bfloat16
VMEM_BYTES = 50 * 1024 * 1024


def nn(a, b):
    return lax.dot_general(a, b, (((1,), (0,)), ((), ())), preferred_element_type=F32)


def nt(a, b):
    return lax.dot_general(a, b, (((1,), (1,)), ((), ())), preferred_element_type=F32)


def tn(a, b):
    return lax.dot_general(a, b, (((0,), (0,)), ((), ())), preferred_element_type=F32)


def hi_lo(value):
    hi = value.astype(BF16)
    return hi, (value - hi.astype(F32)).astype(BF16)


def clip_number(meta, frame):
    one = meta[0]
    two = one + meta[1]
    three = two + meta[2]
    return (
        jnp.where(frame >= one, 1, 0) + jnp.where(frame >= two, 1, 0) + jnp.where(frame >= three, 1, 0)
    )


def frame_facts(meta, frame):
    clip = clip_number(meta, frame)
    one = meta[0]
    two = one + meta[1]
    three = two + meta[2]
    start = jnp.where(
        clip == 0, 0, jnp.where(clip == 1, one, jnp.where(clip == 2, two, three))
    )
    return clip, start, meta[4 + 2 * clip], meta[5 + 2 * clip]


def cell_valid(height, width):
    cell = lax.broadcasted_iota(jnp.int32, (1, CELLS), 1)
    return ((cell >> 4) < height) & ((cell & 15) < width)


def stats_kernel(meta, enc, place, out):
    lane = lax.broadcasted_iota(jnp.int32, (FEAT, 128), 1)
    total = jnp.zeros((FEAT, 128), F32)
    for f in range(FRAMES):
        clip, _, height, width = frame_facts(meta, meta[12] * FRAMES + f)
        kept = jnp.where(cell_valid(height, width), enc[f].astype(F32), 0.0)
        sums = jnp.sum(kept, axis=1, keepdims=True)
        squares = jnp.sum(kept * kept, axis=1, keepdims=True)
        total = total + jnp.where(lane == clip, sums, 0.0) + jnp.where(lane == clip + 4, squares, 0.0)
    for g in range(4):
        out[g : g + 1, :] = jnp.sum(total[g * GS : (g + 1) * GS], axis=0, keepdims=True)
    out[4:6, :] = place[...].astype(F32)
    out[6:8, :] = jnp.zeros((2, 128), F32)


def conv_kernel(meta, enc, rim, sums, gain, bias, taps, spread, out, proj):
    totals = jnp.sum(sums[...], axis=0)
    lane = lax.broadcasted_iota(jnp.int32, (8, 128), 1)
    first = meta[12] * FRAMES
    cell = lax.broadcasted_iota(jnp.int32, (1, CELLS), 1)
    row, col = cell >> 4, cell & 15
    for j in range(FRAMES + 2):
        clip, _, height, width = frame_facts(meta, jnp.maximum(first - 2 + j, 0))
        count = (meta[clip] * height * width * GS).astype(F32)
        mean = jnp.sum(jnp.where(lane == clip, totals, 0.0), axis=1, keepdims=True) / count
        square = jnp.sum(jnp.where(lane == clip + 4, totals, 0.0), axis=1, keepdims=True) / count
        rstd = lax.rsqrt(square - mean * mean + EPSILON)
        mean_c = jnp.concatenate([jnp.broadcast_to(mean[g : g + 1], (GS, 1)) for g in range(4)], axis=0)
        rstd_c = jnp.concatenate([jnp.broadcast_to(rstd[g : g + 1], (GS, 1)) for g in range(4)], axis=0)
        value = rim[j] if j < 2 else enc[j - 2]
        pre = (value.astype(F32) - mean_c) * rstd_c * gain[...] + bias[...]
        act = jnp.where(cell_valid(height, width), pre / (1.0 + jnp.exp(-pre)), 0.0)
        proj[j] = nn(taps[...], act.astype(BF16))
    frames = []
    for f in range(FRAMES):
        _, start, _, _ = frame_facts(meta, first + f)
        source = [jnp.maximum(first + f - 2 + dt, start) - first + 2 for dt in range(3)]
        planes = [proj[source[dt], dt * 144 : (dt + 1) * 144, :] for dt in range(3)]
        joint = planes[0] + planes[1] + planes[2]
        result = jnp.zeros((LAT, CELLS), F32)
        for dx in range(3):
            part = jnp.zeros((LAT, CELLS), F32)
            for dy in range(3):
                tap = (dy * 3 + dx) * LAT
                piece = joint[tap : tap + LAT]
                if dy != 1:
                    piece = pltpu.roll(piece, (-(dy - 1) * SIDE) % CELLS, 1)
                    inside = (row >= 1) if dy == 0 else (row <= SIDE - 2)
                    piece = jnp.where(inside, piece, 0.0)
                part = part + piece
            if dx != 1:
                part = pltpu.roll(part, (-(dx - 1)) % CELLS, 1)
                inside = (col >= 1) if dx == 0 else (col <= SIDE - 2)
                part = jnp.where(inside, part, 0.0)
            result = result + part
        frames.append(result.astype(BF16))
    sorted_cells = nn(jnp.concatenate(frames, axis=0), spread[...]).astype(BF16)
    for ab in range(4):
        out[ab * LAT : (ab + 1) * LAT, :] = jnp.concatenate(
            [
                sorted_cells[f * LAT : (f + 1) * LAT, ab * 64 : (ab + 1) * 64]
                for f in range(FRAMES)
            ],
            axis=1,
        )


def shift_row(m_hi, m_lo, part):
    unit = jnp.where(lax.broadcasted_iota(jnp.int32, (16, AUG), 1) == FEAT + 1, 1.0, 0.0).astype(BF16)
    return (nt(unit, m_hi[part, :]) + nt(unit, m_lo[part, :]))[0:1]


def attn_kernel(
    meta,
    patches,
    place,
    gram_hi,
    gram_lo,
    m_cat,
    m_hi,
    m_lo,
    d_out,
    q_gain,
    k_gain,
    grad_out,
    sums,
    attended,
    own,
    k_t,
    v_t,
    s_t,
    kn_t,
    rk_t,
    prob,
):
    blocks = patches.shape[0]
    row_aug = lax.broadcasted_iota(jnp.int32, (AUG, ROWS), 0)
    row16 = lax.broadcasted_iota(jnp.int32, (16, ROWS), 0)
    token = lax.broadcasted_iota(jnp.int32, (1, ROWS), 1)
    position = lax.broadcasted_iota(jnp.int32, (ROWS, ROWS), 0).astype(F32)
    base = (meta[12] * ROWS).astype(F32)
    one_row = jnp.where(row16 == 0, 1.0, 0.0).astype(BF16)
    two_rows = jnp.where(row16 <= 1, 1.0, 0.0).astype(BF16)

    def lanes(j):
        return pl.ds(pl.multiple_of(j * ROWS, ROWS), ROWS)

    def prepare(j, carry):
        x_q, clip_q = carry
        block = lanes(j)
        raw = patches[j]
        x_aug = jnp.concatenate([raw, one_row], axis=0)
        x_f = x_aug.astype(F32)
        gx = nn(gram_hi[...], x_aug) + nn(gram_lo[...], x_aug)
        rstd = lax.rsqrt(jnp.sum(gx * x_f, axis=0, keepdims=True) + EPSILON)
        s = jnp.where(row_aug == FEAT + 1, 1.0, x_f * rstd)
        s_hi, s_lo = hi_lo(s)
        s_t[:, block] = s_hi
        s_cat = jnp.concatenate([s_hi, s_lo, s_hi], axis=0)
        frame = j * FRAMES + (token >> 6)
        clip = clip_number(meta, frame)
        height = jnp.zeros((1, ROWS), jnp.int32)
        width = jnp.zeros((1, ROWS), jnp.int32)
        for c in range(CLIPS):
            height = jnp.where(clip == c, meta[4 + 2 * c], height)
            width = jnp.where(clip == c, meta[5 + 2 * c], width)
        valid = (2 * ((token >> 3) & 7) < height) & (2 * (token & 7) < width)
        member = row16 == clip
        mask = jnp.where((row16 < CLIPS) & ~(member & valid), OFF, 0.0).astype(BF16)
        for h in range(HEADS):
            kv = nn(m_cat[h * 384 + 128 : h * 384 + 384, :], s_cat)
            k = kv[:HD]
            rk = lax.rsqrt(jnp.mean(k * k, axis=0, keepdims=True) + EPSILON)
            kn = k * rk
            kn_t[h, :, block] = kn
            rk_t[h, :, block] = jnp.broadcast_to(rk, (8, ROWS))
            k_t[h, :HD, block] = (kn * k_gain[...]).astype(BF16)
            k_t[h, HD:, block] = mask
            v_t[h, :HD, block] = kv[HD:].astype(BF16)
            v_t[h, HD:, block] = two_rows
        spot = jnp.concatenate([place[j, 4:5, :], place[j, 5:6, :]], axis=1)
        chosen = jnp.where(spot == position + base, 1.0, 0.0).astype(BF16)
        x_q = x_q + nt(chosen, x_aug)
        clip_q = clip_q + nt(chosen, jnp.where(member, 1.0, 0.0).astype(BF16))
        return x_q, clip_q

    x_q, clip_q = lax.fori_loop(
        0, blocks, prepare, (jnp.zeros((ROWS, AUG), F32), jnp.zeros((ROWS, 16), F32))
    )
    x_qb = x_q.astype(BF16)
    own[...] = x_qb
    sums[:, 896:1280] = tn(x_qb, grad_out[...])
    gx_q = nn(x_qb, gram_hi[...]) + nn(x_qb, gram_lo[...])
    rstd_q = lax.rsqrt(jnp.sum(gx_q * x_q, axis=1, keepdims=True) + EPSILON)
    lane_aug = lax.broadcasted_iota(jnp.int32, (ROWS, AUG), 1)
    s_q = jnp.where(lane_aug == FEAT + 1, 1.0, x_q * rstd_q)
    s_qhi, s_qlo = hi_lo(s_q)
    lane16 = lax.broadcasted_iota(jnp.int32, (ROWS, 16), 1)

    q_ext, q_ext_t, do_ext, do_ext_t, q_keep = [], [], [], [], []
    for h in range(HEADS):
        mine = slice(h * 384, h * 384 + 128)
        q = nt(s_qhi, m_hi[mine, :]) + nt(s_qlo, m_hi[mine, :]) + nt(s_qhi, m_lo[mine, :])
        rq = lax.rsqrt(jnp.mean(q * q, axis=1, keepdims=True) + EPSILON)
        qn = q * rq
        qb = (qn * (q_gain[...] * (HD**-0.5 * LOG2E))).astype(BF16)
        q_keep.append((q, rq, qn))
        q_ext.append(jnp.concatenate([qb, clip_q.astype(BF16)], axis=1))
        ones = jnp.where(lane16 == 0, 1.0, 0.0)
        q_ext_t.append(jnp.concatenate([qb.astype(F32), ones], axis=1).T.astype(BF16))

        def forward(j, total, h=h):
            block = lanes(j)
            p = jnp.exp2(nn(q_ext[h], k_t[h, :, block])).astype(BF16)
            prob[h, :, block] = p
            return total + nt(p, v_t[h, :, block])

        total = lax.fori_loop(0, blocks, forward, jnp.zeros((ROWS, EXT), F32))
        inv_l = 1.0 / total[:, HD : HD + 1]
        att = (total[:, :HD] * inv_l).astype(BF16)
        attended[:, h * HD : (h + 1) * HD] = att
        do = d_out[:, h * HD : (h + 1) * HD].astype(F32)
        delta = jnp.sum(do * att.astype(F32), axis=1, keepdims=True)
        shift_v = shift_row(m_hi, m_lo, slice(h * 384 + 256, h * 384 + 384))
        weight = (delta - jnp.sum(do * shift_v, axis=1, keepdims=True)) * inv_l
        scaled = (do * inv_l).astype(BF16)
        d_hi, d_lo = hi_lo(-delta * inv_l)
        extra = jnp.where(lane16 == 0, d_hi.astype(F32), jnp.where(lane16 == 1, d_lo.astype(F32), 0.0))
        do_ext.append(jnp.concatenate([scaled, extra.astype(BF16)], axis=1))
        w_hi, w_lo = hi_lo(weight)
        extra = jnp.where(lane16 == 0, w_hi.astype(F32), jnp.where(lane16 == 1, w_lo.astype(F32), 0.0))
        do_ext_t.append(jnp.concatenate([scaled.astype(F32), extra], axis=1).T.astype(BF16))

    def backward(j, carry):
        quad, per_head = carry
        block = lanes(j)
        s_block = s_t[:, block]
        m2 = jnp.zeros((1, ROWS), F32)
        done = []
        for h in range(HEADS):
            grad_q, p_k, p_v = per_head[h]
            pb = prob[h, :, block]
            d_score = (pb.astype(F32) * nn(do_ext[h], v_t[h, :, block])).astype(BF16)
            grad_q = grad_q + nt(d_score, k_t[h, :HD, block])
            gk = nn(q_ext_t[h], d_score)
            gv = nn(do_ext_t[h], pb)
            kn = kn_t[h, :, block]
            rk = rk_t[h, 0:1, block]
            scaled = gk[:HD] * (k_gain[...] * (1.0 / LOG2E))
            dk = rk * (scaled - kn * jnp.mean(scaled * kn, axis=0, keepdims=True))
            shift_k = m_hi[h * 384 + 128 : h * 384 + 256, FEAT + 1 : FEAT + 2].astype(F32) + m_lo[
                h * 384 + 128 : h * 384 + 256, FEAT + 1 : FEAT + 2
            ].astype(F32)
            m2 = m2 + jnp.sum(dk * (kn * (1.0 / rk) - shift_k), axis=0, keepdims=True)
            m2 = m2 + gk[HD : HD + 1] + gv[HD : HD + 1] + gv[HD + 1 : HD + 2]
            p_k = p_k + nt(s_block, dk.astype(BF16))
            p_v = p_v + nt(s_block, gv[:HD].astype(BF16))
            done.append((grad_q, p_k, p_v))
        quad = quad + nt((s_block.astype(F32) * m2).astype(BF16), s_block)
        return quad, tuple(done)

    zero = (jnp.zeros((ROWS, HD), F32), jnp.zeros((AUG, HD), F32), jnp.zeros((AUG, HD), F32))
    quad, per_head = lax.fori_loop(
        0, blocks, backward, (jnp.zeros((AUG, AUG), F32), (zero,) * HEADS)
    )
    m2_q = jnp.zeros((ROWS, 1), F32)
    for h in range(HEADS):
        grad_q, p_k, p_v = per_head[h]
        q, rq, qn = q_keep[h]
        scaled = grad_q * (q_gain[...] * HD**-0.5)
        dq = rq * (scaled - qn * jnp.mean(scaled * qn, axis=1, keepdims=True))
        mine = slice(h * 384, h * 384 + 128)
        shift_q = shift_row(m_hi, m_lo, mine)
        m2_q = m2_q + jnp.sum(dq * (q - shift_q), axis=1, keepdims=True)
        sums[:, h * 384 : h * 384 + 128] = tn(s_qhi, dq.astype(BF16))
        sums[:, h * 384 + 128 : h * 384 + 256] = p_k
        sums[:, h * 384 + 256 : h * 384 + 384] = p_v
    quad = (quad + tn((s_q * m2_q).astype(BF16), s_qhi)) * (1.0 / D)
    sums[:, 768:896] = jnp.concatenate([quad, jnp.zeros((AUG, 128 - AUG), F32)], axis=1)


VMEM = pl.BlockSpec(memory_space=pltpu.VMEM)
SMEM = pl.BlockSpec(memory_space=pltpu.SMEM)


def call(kernel, inputs, outputs, scratch, flops):
    return pl.pallas_call(
        kernel,
        out_shape=outputs,
        in_specs=[SMEM] + [VMEM] * (len(inputs) - 1),
        out_specs=jax.tree.map(lambda _: VMEM, outputs),
        scratch_shapes=scratch,
        compiler_params=pltpu.CompilerParams(vmem_limit_bytes=VMEM_BYTES),
        cost_estimate=pl.CostEstimate(flops=flops, bytes_accessed=1 << 20, transcendentals=0),
    )(*inputs)


def shift_by(value, axis, move):
    return lax.ppermute(value, axis, [(i, move(i)) for i in range(lax.axis_size(axis))])


def along_x(k):
    return lambda i: (i // 4) * 4 + (i % 4 + k) % 4


def along_y(k):
    return lambda i: ((i // 4 + k) % 4) * 4 + i % 4


def along_z(k):
    return lambda i: ((i // 2 + k) % 4) * 2 + i % 2


def sum_of_four(value, axis, move, kind):
    sent = value.astype(kind)
    one, two, three = (shift_by(sent, axis, move(k)).astype(F32) for k in (1, 2, 3))
    return (sent.astype(F32) + two) + (one + three)


def body(
    enc_feat,
    gn_gain,
    gn_bias,
    conv_w,
    clip_frames,
    clip_res,
    token_place,
    embed_w,
    embed_b,
    mod_shift,
    mod_scale,
    mod_gate,
    w_qkv,
    q_gain,
    k_gain,
    w_out,
    grad_out,
):
    slabs = lax.axis_size("slab")
    slab_pos = lax.axis_index("slab").astype(jnp.int32)
    mp_size = lax.axis_size("mp")
    mp_pos = lax.axis_index("mp")
    cols_dev = D // mp_size
    col_first = mp_pos * cols_dev
    row_cols = D // slabs

    meta = jnp.concatenate(
        [clip_frames, clip_res.reshape(-1), slab_pos[None], jnp.zeros((3,), jnp.int32)]
    )
    rim = shift_by(enc_feat[FRAMES - 2 :], "slab", lambda i: (i + 1) % slabs)
    stats = call(
        stats_kernel,
        (meta, enc_feat, token_place.reshape(2, 128)),
        jax.ShapeDtypeStruct((8, 128), F32),
        [],
        1 << 20,
    )
    all_stats = lax.all_to_all(
        jnp.broadcast_to(stats, (slabs, 8, 128)), "slab", split_axis=0, concat_axis=0, tiled=True
    )
    cell = jnp.arange(CELLS, dtype=jnp.int32)
    row, col = cell // SIDE, cell % SIDE
    sorted_place = ((row % 2) * 2 + col % 2) * 64 + (row // 2) * PSIDE + col // 2
    spread = (sorted_place[:, None] == cell[None, :]).astype(BF16)
    partial = call(
        conv_kernel,
        (
            meta,
            enc_feat,
            rim,
            all_stats,
            gn_gain[:, None],
            gn_bias[:, None],
            conv_w.T,
            spread,
        ),
        jax.ShapeDtypeStruct((FEAT, CELLS), BF16),
        [pltpu.VMEM((FRAMES + 2, 432, CELLS), F32)],
        1 << 28,
    )
    other = shift_by(partial, "mp", lambda i: i ^ 1)
    pair = partial.astype(F32) + other.astype(F32)
    lat_sorted = sum_of_four(pair, "mp", along_z, BF16)
    patches = lat_sorted.astype(BF16)
    all_patches = lax.all_to_all(
        jnp.broadcast_to(patches, (slabs, FEAT, CELLS)), "slab", split_axis=0, concat_axis=0, tiled=True
    )
    latents = (
        lat_sorted.reshape(2, 2, LAT, FRAMES, PSIDE, PSIDE)
        .transpose(3, 2, 4, 0, 5, 1)
        .reshape(FRAMES, LAT, CELLS)
    )

    embed_f = embed_w.astype(F32).reshape(LAT, 4, D).transpose(1, 0, 2).reshape(FEAT, D)
    embed_aug = jnp.concatenate([embed_f, embed_b[None]], axis=0)
    centered = embed_aug - jnp.mean(embed_aug, axis=1, keepdims=True)
    gram = lax.dot_general(centered, centered, (((1,), (1,)), ((), ())), precision=HIGHEST) / D
    gram_hi, gram_lo = hi_lo(jnp.pad(gram, ((0, AUG - 65), (0, AUG - 65))))
    modulated = jnp.concatenate(
        [centered * (1.0 + mod_scale), mod_shift[None], jnp.zeros((AUG - 66, D), F32)], axis=0
    )
    mod_hi, mod_lo = hi_lo(modulated)
    both = lax.dot_general(
        w_qkv,
        jnp.concatenate([mod_hi, mod_lo], axis=0),
        (((0,), (1,)), ((), ())),
        preferred_element_type=F32,
    )
    m_hi, m_lo = hi_lo(both[:, :AUG] + both[:, AUG:])
    m_cat = jnp.concatenate([m_hi, m_hi, m_lo], axis=1)

    cotangent = lax.all_gather(grad_out, "mp", axis=1, tiled=True)
    d_attn = (mod_gate * cotangent.astype(F32)).astype(BF16)
    d_out = nt(d_attn, w_out).astype(BF16)

    sums, attended, own = call(
        attn_kernel,
        (
            meta,
            all_patches,
            all_stats,
            gram_hi,
            gram_lo,
            m_cat,
            m_hi,
            m_lo,
            d_out,
            q_gain[None, :],
            k_gain[:, None],
            grad_out,
        ),
        (
            jax.ShapeDtypeStruct((AUG, 1280), F32),
            jax.ShapeDtypeStruct((ROWS, HEADS * HD), BF16),
            jax.ShapeDtypeStruct((ROWS, AUG), BF16),
        ),
        [
            pltpu.VMEM((HEADS, EXT, 4096), BF16),
            pltpu.VMEM((HEADS, EXT, 4096), BF16),
            pltpu.VMEM((AUG, 4096), BF16),
            pltpu.VMEM((HEADS, HD, 4096), F32),
            pltpu.VMEM((HEADS, 8, 4096), F32),
            pltpu.VMEM((HEADS, ROWS, 4096), BF16),
        ],
        1 << 33,
    )

    total = sum_of_four(sums, "slab", along_x, F32)
    total = sum_of_four(total, "slab", along_y, F32)
    own_rows = lax.dynamic_slice_in_dim(modulated, slab_pos * row_cols, row_cols, 1)
    g_qkv = lax.dot_general(
        own_rows[:66], total[:66, :768], (((0,), (0,)), ((), ())), precision=HIGHEST
    )
    back = nt(total[:FEAT, :768].astype(BF16), w_qkv) * (1.0 + mod_scale)
    back = back - jnp.mean(back, axis=1, keepdims=True)
    back = back - jnp.dot(total[:FEAT, 768 : 768 + 65], centered, precision=HIGHEST)
    pieces = back.astype(BF16).reshape(FEAT, mp_size, cols_dev).transpose(1, 0, 2)
    got = lax.all_to_all(pieces, "mp", split_axis=0, concat_axis=0, tiled=True)
    g_embed = jnp.sum(got.astype(F32), axis=0) + total[:FEAT, 896:1280]
    g_embed = g_embed.reshape(4, LAT, cols_dev).transpose(1, 0, 2).reshape(FEAT, cols_dev)

    attn_part = jnp.dot(attended, w_out, preferred_element_type=F32).astype(BF16)
    attn_got = lax.all_to_all(
        attn_part.reshape(ROWS, mp_size, cols_dev).transpose(1, 0, 2),
        "mp",
        split_axis=0,
        concat_axis=0,
        tiled=True,
    )
    attn_cols = jnp.sum(attn_got.astype(F32), axis=0)
    hidden_cols = (
        jnp.dot(
            own[:, :FEAT],
            lax.dynamic_slice_in_dim(embed_f.astype(BF16), col_first, cols_dev, 1),
            preferred_element_type=F32,
        )
        + lax.dynamic_slice_in_dim(embed_b, col_first, cols_dev, 0)
    ).astype(BF16)
    gate_cols = lax.dynamic_slice_in_dim(mod_gate, col_first, cols_dev, 0)
    block_out = (hidden_cols.astype(F32) + gate_cols * attn_cols).astype(BF16)
    g_part = tn(attended, d_attn).astype(BF16)
    g_got = lax.all_to_all(
        g_part.reshape(HEADS * HD, slabs, row_cols).transpose(1, 0, 2),
        "slab",
        split_axis=0,
        concat_axis=0,
        tiled=True,
    )
    g_out = jnp.sum(g_got.astype(F32), axis=0)
    return (latents, block_out, g_qkv, g_out, g_embed)


def solution(mesh):
    in_specs = (
        P(("dp", "slab"), "mp", None),
        P("mp"),
        P("mp"),
        P("mp", None),
        P("dp"),
        P("dp", None),
        P(("dp", "slab")),
        P(),
        P(),
        P("dp"),
        P("dp"),
        P("dp"),
        P(None, "mp"),
        P(),
        P(),
        P("mp", None),
        P(("dp", "slab"), "mp"),
    )
    out_specs = (
        P(("dp", "slab"), None, None),
        P(("dp", "slab"), "mp"),
        P(("dp", "slab"), "mp"),
        P(("dp", "mp"), "slab"),
        P("dp", "mp"),
    )
    return jax.shard_map(body, mesh=mesh, in_specs=in_specs, out_specs=out_specs, check_vma=False)
```

time: 698 us -> 224 us (0.32); the launches traced: 688 us -> 223 us
  waiting for transfers between devices: 291 us -> 79 us
  blocking collectives: 165 us -> 0 us
  local copies, waits for them, and re-layouts: 118 us -> 20.6 us
  Pallas kernels: 0 us -> 41.3 us
  other arithmetic: 42 us -> 7.65 us
  starting transfers between devices: 9.42 us -> 41.4 us
  matrix products: 48 us -> 18.7 us
    psum x3 -> x0, blocking collectives: 143 us -> none  [the longest x1 74.6 us: body(): lax.psum(jnp.dot(sequence.astype(jnp.float32).T, d_hidden, precision=HIGH...]
    reduce_scatter x3 -> x0, waiting for transfers between devices: 140 us -> none  [the longest x1 74.5 us: body(): lax.psum_scatter(jnp.dot(flat_heads.T, d_attn, preferred_element_type=jnp...]
    psum x1 -> x0, waiting for transfers between devices: 62.9 us -> none  [body(): d_mod = lax.psum(d_mod_part.astype(jnp.bfloat16), 'mp').astype(jnp.float32)]
    pallas_call x0 -> x3, Pallas kernels: none -> 41.3 us  [call(): pl.pallas_call(kernel, out_shape=outputs, in_specs=[SMEM] + [VMEM] * (len...]
    all_gather x2 -> x0, waiting for transfers between devices: 37.4 us -> none  [the longest x1 37.4 us: body(): lax.all_gather(values_dev, 'slab', axis=0, tiled=True)]
    ppermute x1 -> x11, waiting for transfers between devices: 1.82 us -> 37.4 us  [shift_by(): lax.ppermute(value, axis, [(i, move(i)) for i in range(lax.axis_size(axis...]
    dot_general x23 -> x9, matrix products: 48 us -> 18.7 us  [the longest x2 6.83 us: nt(): lax.dot_general(a, b, (((1,), (1,)), ((), ())), preferred_element_type=F32)]
    scatter x3 -> x0, local copies, waits for them, and re-layouts: 26.4 us -> none  [the longest x2 13.4 us: body(): jnp.zeros((slabs, shard_rows, 4 * LAT), jnp.bfloat16).at[target, slot_pos]]
  transfers between devices with their start and end apart: 11 -> 17, of which waited for: 10 -> 12; matrix products, arithmetic and copies ran while one was open for 11% -> 15% of each run, Pallas kernels for 0% -> 1%
where the time goes in v1:
time: 224 us; the launch traced here: 223 us
  waiting for transfers between devices  79 us (35%)
  starting transfers between devices  41.4 us (18%)
  Pallas kernels  41.3 us (18%)
  local copies, waits for them, and re-layouts  20.6 us (9%)
  matrix products  18.7 us (8%)
  between operations  14.4 us (6%)
  other arithmetic  7.65 us (3%)
    pallas_call x3, Pallas kernels, call(): pl.pallas_call(kernel, out_shape=outputs, in_specs=[SMEM] + [VMEM] * (len...  41.3 us
    ppermute x11, waiting for transfers between devices, shift_by(): lax.ppermute(value, axis, [(i, move(i)) for i in range(lax.axis_size(axis...  37.4 us
    ppermute x11, starting transfers between devices, shift_by(): lax.ppermute(value, axis, [(i, move(i)) for i in range(lax.axis_size(axis...  16.2 us
    all_to_all x1, waiting for transfers between devices, body(): lax.all_to_all(attn_part.reshape(ROWS, mp_size, cols_dev).transpose(1, 0,...  15.8 us
    all_to_all x1, waiting for transfers between devices, body(): lax.all_to_all(g_part.reshape(HEADS * HD, slabs, row_cols).transpose(1, 0...  10.6 us
    all_to_all x1, waiting for transfers between devices, body(): lax.all_to_all(jnp.broadcast_to(patches, (slabs, FEAT, CELLS)), 'slab', s...  7.74 us
    unnamed x47, local copies, waits for them, and re-layouts  7.65 us
    all_to_all x1, starting transfers between devices, body(): lax.all_to_all(jnp.broadcast_to(stats, (slabs, 8, 128)), 'slab', split_ax...  7.12 us
  transfers between devices with their start and end apart: 17, of which 12 were waited for; matrix products, arithmetic and copies ran while one was open for 15% of the time, Pallas kernels for 1%

profile of v1, /device:TPU:0, one launch (start us, length us, event | category | flops | bytes accessed | tf_op | source)
XLA Modules:
  0.0 223.1 jit_solution(12519983771427568765)
XLA Ops:
  7.2 0.9 copy.53
  8.9 0.9 copy-done.1
  11.8 7.1 %all-to-all-start = ((f32[16,8,128]{2,1,0:T(8,128)}), f32[16,8,128]{2,1,0:T(8,128)S(1)}, u32[]{:S(2)}, u32[]{:S(2)}) async-start(f32[16,8,128]{2,1,0:T(8,128)} %broadcast_in_dim.40), calls=%async_computation | async-start | bytes 131072 | tf_op jit(solution)/shard_map/all_to_all | solution.py:392
  19.9 1.9 collective-permute-start
  21.8 1.1 reshape.141
  24.1 1.1 maximum_maximum_fusion
  25.3 1.1 copy-done.9
  26.4 1.9 convolution_bitcast_fusion
  29.0 1.8 shard_map.201
  30.9 1.0 convolution_multiply_fusion.1
  32.1 4.0 %collective-permute-start.2 = (bf16[64,256]{1,0:T(8,128)(2,1)S(1)}, bf16[64,256]{1,0:T(8,128)(2,1)S(1)}, u32[]{:S(2)}, u32[]{:S(2)}) collective-permute-start(bf16[64,256]{1,0:T(8,128)(2,1)S(1)} %add_convert_fusion), channel_id=1, source_target_pairs={{0,4},{1,5},{2,6},{3,7},{4,0},{5,1},{6,2},{7,3},{8,12},{9,13},{10,... | collective-permute-start | bytes 98312 | tf_op jit(solution)/shard_map/ppermute | solution.py:333
  36.0 1.0 collective-permute-start.3
  37.0 2.2 collective-permute-start.4
  39.4 1.8 collective-permute-done.3
  42.0 6.6 %all-to-all-start.1 = ((bf16[16,64,256]{2,1,0:T(8,128)(2,1)}), bf16[16,64,256]{2,1,0:T(8,128)(2,1)S(1)}, u32[]{:S(2)}, u32[]{:S(2)}) async-start(bf16[16,64,256]{2,1,0:T(8,128)(2,1)} %broadcast_in_dim.43), calls=%async_computation.1 | async-start | bytes 1048576 | tf_op jit(solution)/shard_map/all_to_all | solution.py:419
  49.5 2.7 %fusion.6.d_out = bf16[256,256]{1,0:T(8,128)(2,1)} fusion(bf16[256,3072]{1,0:T(8,128)(2,1)S(1)} %copy-done, bf16[256,3072]{1,0:T(8,128)(2,1)} %all-gather.2.cloned.1.call-done, f32[3072]{0:T(1024)S(1)} %copy-done.16), kind=kOutput, calls=%fused_computation.16 | convolution fusion | flops 405078016 | bytes 3289088 | tf_op jit(solution)/shard_map/dot_general | solution.py:38
  52.1 7.7 %all-to-all-done.1.patches = bf16[16,64,256]{2,1,0:T(8,128)(2,1)S(1)} async-done(((bf16[16,64,256]{2,1,0:T(8,128)(2,1)}), bf16[16,64,256]{2,1,0:T(8,128)(2,1)S(1)}, u32[]{:S(2)}, u32[]{:S(2)}) %all-to-all-start.1) | async-done | bytes 524320 | tf_op jit(solution)/shard_map/all_to_all | solution.py:419
  59.9 0.9 copy-done.6
  60.8 38.8 %shard_map.202 = (f32[80,1280]{1,0:T(8,128)S(1)}, bf16[256,256]{1,0:T(8,128)(2,1)S(1)}, bf16[256,80]{1,0:T(8,128)(2,1)S(1)}) custom-call(s32[16]{0:T(128)S(1)} %pad_add_fusion.meta, bf16[16,64,256]{2,1,0:T(8,128)(2,1)S(1)} %all-to-all-done.1.patches, f32[16,8,128]{2,1,0:T(8,128)S(1)} %all-to-all-done.sums.place, bf16[80,80]{1,0:T(8,128)(2,1)S(1)} %pad_convert_fusion.gram_hi, ...), custom_call_target="tpu_custom_call" | custom-call | flops 8589934592 | bytes 1048576 | tf_op jit(solution)/shard_map/pallas_call | solution.py:321
  99.6 0.9 collective-permute-start.5
  101.0 2.7 %collective-permute-start.7 = (f32[80,1280]{1,0:T(8,128)S(1)}, f32[80,1280]{1,0:T(8,128)S(1)}, u32[]{:S(2)}, u32[]{:S(2)}) collective-permute-start(f32[80,1280]{1,0:T(8,128)S(1)} %get-tuple-element.10), channel_id=1, source_target_pairs={{0,24},{8,0},{16,8},{24,16},{32,56},{40,32},{48,40},{56,48},{64,88... | collective-permute-start | bytes 1228808 | tf_op jit(solution)/shard_map/ppermute | solution.py:333
  103.7 9.9 %collective-permute-done.5 = f32[80,1280]{1,0:T(8,128)S(1)} collective-permute-done((f32[80,1280]{1,0:T(8,128)S(1)}, f32[80,1280]{1,0:T(8,128)S(1)}, u32[]{:S(2)}, u32[]{:S(2)}) %collective-permute-start.5) | collective-permute-done | bytes 409632 | tf_op jit(solution)/shard_map/ppermute | solution.py:333
  113.6 5.9 %collective-permute-done.6 = f32[80,1280]{1,0:T(8,128)S(1)} collective-permute-done((f32[80,1280]{1,0:T(8,128)S(1)}, f32[80,1280]{1,0:T(8,128)S(1)}, u32[]{:S(2)}, u32[]{:S(2)}) %collective-permute-start.6) | collective-permute-done | bytes 409632 | tf_op jit(solution)/shard_map/ppermute | solution.py:333
  119.6 1.2 collective-permute-start.10
  121.6 0.9 collective-permute-start.9
  122.5 9.5 %collective-permute-done.10 = f32[80,1280]{1,0:T(8,128)S(1)} collective-permute-done((f32[80,1280]{1,0:T(8,128)S(1)}, f32[80,1280]{1,0:T(8,128)S(1)}, u32[]{:S(2)}, u32[]{:S(2)}) %collective-permute-start.10) | collective-permute-done | bytes 409632 | tf_op jit(solution)/shard_map/ppermute | solution.py:333
  132.0 2.7 %collective-permute-done.8 = f32[80,1280]{1,0:T(8,128)S(1)} collective-permute-done((f32[80,1280]{1,0:T(8,128)S(1)}, f32[80,1280]{1,0:T(8,128)S(1)}, u32[]{:S(2)}, u32[]{:S(2)}) %collective-permute-start.8) | collective-permute-done | bytes 409632 | tf_op jit(solution)/shard_map/ppermute | solution.py:333
  134.7 7.5 %collective-permute-done.9 = f32[80,1280]{1,0:T(8,128)S(1)} collective-permute-done((f32[80,1280]{1,0:T(8,128)S(1)}, f32[80,1280]{1,0:T(8,128)S(1)}, u32[]{:S(2)}, u32[]{:S(2)}) %collective-permute-start.9) | collective-permute-done | bytes 409632 | tf_op jit(solution)/shard_map/ppermute | solution.py:333
  142.2 4.1 %fusion.36 = (f32[64]{0:T(128)S(1)}, f32[64,3072]{1,0:T(8,128)S(1)}) fusion(f32[3072]{0:T(1024)S(1)} %broadcast_add_fusion, bf16[3072,768]{1,0:T(8,128)(2,1)} %param.29, f32[80,1280]{1,0:T(8,128)S(1)} %add_add_fusion), kind=kOutput, calls=%fused_computation.84 | convolution fusion | flops 302383040 | bytes 5615872 | tf_op jit(solution)/shard_map/dot_general | solution.py:38
  146.4 0.9 fusion
  148.1 3.5 %all-to-all-start.4 = ((bf16[8,64,384]{2,1,0:T(8,128)(2,1)}), bf16[8,64,384]{2,1,0:T(8,128)(2,1)S(1)}, u32[]{:S(2)}, u32[]{:S(2)}) async-start(bf16[8,64,384]{2,1,0:T(8,128)(2,1)} %bitcast.43), calls=%async_computation.4 | async-start | bytes 786432 | tf_op jit(solution)/shard_map/all_to_all | solution.py:492
  152.1 1.3 copy.72
  153.5 6.9 %all-to-all-done.4 = bf16[8,64,384]{2,1,0:T(8,128)(2,1)S(1)} async-done(((bf16[8,64,384]{2,1,0:T(8,128)(2,1)}), bf16[8,64,384]{2,1,0:T(8,128)(2,1)S(1)}, u32[]{:S(2)}, u32[]{:S(2)}) %all-to-all-start.4) | async-done | bytes 393248 | tf_op jit(solution)/shard_map/all_to_all | solution.py:492
  161.2 4.3 %all-to-all-start.2 = ((bf16[8,256,384]{2,1,0:T(8,128)(2,1)}), bf16[8,256,384]{2,1,0:T(8,128)(2,1)}, u32[]{:S(2)}, u32[]{:S(2)}) async-start(bf16[8,256,384]{2,1,0:T(8,128)(2,1)} %bitcast.47), calls=%async_computation.2 | async-start | bytes 3145728 | tf_op jit(solution)/shard_map/all_to_all | solution.py:497
  165.5 3.2 %convolution_convert_fusion = bf16[256,3072]{1,0:T(8,128)(2,1)} fusion(bf16[256,256]{1,0:T(8,128)(2,1)S(1)} %get-tuple-element.9, bf16[256,3072]{1,0:T(8,128)(2,1)} %all-gather.2.cloned.1.call-done, f32[3072]{0:T(1024)S(1)} %copy-done.17), kind=kOutput, calls=%fused_computation | convolution fusion | flops 405798912 | bytes 3289088 | tf_op jit(solution)/shard_map/dot_general | solution.py:42
  168.7 2.6 %copy.63 = bf16[256,3072]{0,1:T(8,128)(2,1)} copy(bf16[256,3072]{1,0:T(8,128)(2,1)} %convolution_convert_fusion) | data formatting | bytes 3145728 | tf_op jit(solution)/shard_map/convert_element_type | solution.py:515
  171.3 15.8 %all-to-all-done.2 = bf16[8,256,384]{2,1,0:T(8,128)(2,1)} async-done(((bf16[8,256,384]{2,1,0:T(8,128)(2,1)}), bf16[8,256,384]{2,1,0:T(8,128)(2,1)}, u32[]{:S(2)}, u32[]{:S(2)}) %all-to-all-start.2) | async-done | bytes 1572896 | tf_op jit(solution)/shard_map/all_to_all | solution.py:497
  187.1 3.7 %all-to-all-start.3 = ((bf16[16,256,192]{1,2,0:T(8,128)(2,1)}), bf16[16,256,192]{1,2,0:T(8,128)(2,1)S(1)}, u32[]{:S(2)}, u32[]{:S(2)}) async-start(bf16[16,256,192]{1,2,0:T(8,128)(2,1)} %bitcast.16), calls=%async_computation.3 | async-start | bytes 3145728 | tf_op jit(solution)/shard_map/all_to_all | solution.py:516
  191.0 1.2 reshape.139
  192.3 2.0 copy.58
  194.3 1.8 copy.66
  196.1 2.6 %fusion.16 = f32[192,768]{1,0:T(8,128)} fusion(f32[80,1280]{1,0:T(8,128)} %copy-done.10, f32[80,3072]{1,0:T(8,128)} %get-tuple-element.30, s32[]{:T(128)S(6)} %select_n.65), kind=kOutput, calls=%fused_computation.39 | convolution fusion | flops 116785152 | bytes 884740 | tf_op jit(solution)/shard_map/dot_general | solution.py:485
  198.7 1.1 convert_reduce_fusion.2
  199.8 0.9 slice_add_fusion.1
  201.4 1.7 convert_reduce_fusion.1
  203.1 1.7 fusion.5
  204.7 10.6 %all-to-all-done.3 = bf16[16,256,192]{1,2,0:T(8,128)(2,1)S(1)} async-done(((bf16[16,256,192]{1,2,0:T(8,128)(2,1)}), bf16[16,256,192]{1,2,0:T(8,128)(2,1)S(1)}, u32[]{:S(2)}, u32[]{:S(2)}) %all-to-all-start.3) | async-done | bytes 1572896 | tf_op jit(solution)/shard_map/all_to_all | solution.py:516
  215.3 0.9 convert_reduce_fusion
  (91 shorter events, 12.2 us)
Async XLA Ops:
  7.2 42.3 %copy-start = (bf16[256,3072]{1,0:T(8,128)(2,1)S(1)}, bf16[256,3072]{1,0:T(8,128)(2,1)}, u32[]{:S(2)}) copy-start(bf16[256,3072]{1,0:T(8,128)(2,1)} %param.32) | copy-start | bytes 4718596
  8.9 0.9 copy-start.1
  9.8 0.7 copy-start.4
  11.8 17.2 %all-to-all-start = ((f32[16,8,128]{2,1,0:T(8,128)}), f32[16,8,128]{2,1,0:T(8,128)S(1)}, u32[]{:S(2)}, u32[]{:S(2)}) async-start(f32[16,8,128]{2,1,0:T(8,128)} %broadcast_in_dim.40), calls=%async_computation | async-start | bytes 131072 | tf_op jit(solution)/shard_map/all_to_all | solution.py:392
  18.9 4.3 %copy-start.13 = (f32[3072]{0:T(1024)S(1)}, f32[3072]{0:T(1024)}, u32[]{:S(2)}) copy-start(f32[3072]{0:T(1024)} %param.25) | copy-start | bytes 36868
  19.0 30.5 %all-gather.2.cloned.1.call-start = ((), (), s32[]{:S(2)}) async-start(), calls=%async_computation.5 | async-start | bytes 1769472 | tf_op jit(solution)/shard_map/all_gather | solution.py:446
  19.9 9.1 %collective-permute-start = (bf16[2,64,256]{2,1,0:T(8,128)(2,1)S(1)}, bf16[2,64,256]{2,1,0:T(8,128)(2,1)S(1)}, u32[]{:S(2)}, u32[]{:S(2)}) collective-permute-start(bf16[2,64,256]{2,1,0:T(8,128)(2,1)S(1)} %slice.28), channel_id=1, source_target_pairs={{0,8},{8,16},{16,24},{24,32},{32,40},{40,48},{48,56},{56,64},{64,7... | collective-permute-start | bytes 196616 | tf_op jit(solution)/shard_map/ppermute | solution.py:333
  23.0 0.7 copy-start.18
  23.1 0.8 copy-start.11
  23.1 0.9 copy-start.15
  23.2 7.7 %copy-start.7 = (f32[64,3072]{1,0:T(8,128)}, f32[64,3072]{1,0:T(8,128)S(1)}, u32[]{:S(2)}) copy-start(f32[64,3072]{1,0:T(8,128)S(1)} %bitcast_convert_fusion) | copy-start | bytes 2359300
  23.7 2.7 %copy-start.9 = (bf16[3072,768]{1,0:T(8,128)(2,1)S(1)}, bf16[3072,768]{1,0:T(8,128)(2,1)}, u32[]{:S(2)}) copy-start(bf16[3072,768]{1,0:T(8,128)(2,1)} %param.29) | copy-start | bytes 14155780
  26.4 2.3 %copy-start.14 = (bf16[64,432]{1,0:T(8,128)(2,1)S(1)}, bf16[64,432]{1,0:T(8,128)(2,1)}, u32[]{:S(2)}) copy-start(bf16[64,432]{1,0:T(8,128)(2,1)} %param.20) | copy-start | bytes 165892
  26.4 2.4 %copy-start.19 = (f32[64]{0:T(128)S(1)}, f32[64]{0:T(128)}, u32[]{:S(2)}) copy-start(f32[64]{0:T(128)} %param.18) | copy-start | bytes 772
  26.4 2.5 %copy-start.20 = (f32[64]{0:T(128)S(1)}, f32[64]{0:T(128)}, u32[]{:S(2)}) copy-start(f32[64]{0:T(128)} %param.19) | copy-start | bytes 772
  26.4 2.6 %copy-start.2 = (bf16[4,64,256]{2,1,0:T(8,128)(2,1)S(1)}, bf16[4,64,256]{2,1,0:T(8,128)(2,1)}, u32[]{:S(2)}) copy-start(bf16[4,64,256]{2,1,0:T(8,128)(2,1)} %enc.3) | copy-start | bytes 393220
  28.5 10.8 %copy-start.21 = (f32[128]{0:T(128)S(1)}, f32[128]{0:T(128)}, u32[]{:S(2)}) copy-start(f32[128]{0:T(128)} %param.31) | copy-start | bytes 1540
  30.8 1.3 collective-permute-start.1
  31.9 17.6 %copy-start.16 = (f32[3072]{0:T(1024)S(1)}, f32[3072]{0:T(1024)}, u32[]{:S(2)}) copy-start(f32[3072]{0:T(1024)} %param.28) | copy-start | bytes 36868
  32.1 7.3 %collective-permute-start.2 = (bf16[64,256]{1,0:T(8,128)(2,1)S(1)}, bf16[64,256]{1,0:T(8,128)(2,1)S(1)}, u32[]{:S(2)}, u32[]{:S(2)}) collective-permute-start(bf16[64,256]{1,0:T(8,128)(2,1)S(1)} %add_convert_fusion), channel_id=1, source_target_pairs={{0,4},{1,5},{2,6},{3,7},{4,0},{5,1},{6,2},{7,3},{8,12},{9,13},{10,... | collective-permute-start | bytes 98312 | tf_op jit(solution)/shard_map/ppermute | solution.py:333
  36.0 5.1 %collective-permute-start.3 = (bf16[64,256]{1,0:T(8,128)(2,1)S(1)}, bf16[64,256]{1,0:T(8,128)(2,1)S(1)}, u32[]{:S(2)}, u32[]{:S(2)}) collective-permute-start(bf16[64,256]{1,0:T(8,128)(2,1)S(1)} %add_convert_fusion), channel_id=1, source_target_pairs={{0,2},{1,3},{2,4},{3,5},{4,6},{5,7},{6,0},{7,1},{8,10},{9,11},{10,... | collective-permute-start | bytes 98312 | tf_op jit(solution)/shard_map/ppermute | solution.py:333
  37.0 4.1 %collective-permute-start.4 = (bf16[64,256]{1,0:T(8,128)(2,1)S(1)}, bf16[64,256]{1,0:T(8,128)(2,1)S(1)}, u32[]{:S(2)}, u32[]{:S(2)}) collective-permute-start(bf16[64,256]{1,0:T(8,128)(2,1)S(1)} %add_convert_fusion), channel_id=1, source_target_pairs={{0,6},{1,7},{2,0},{3,1},{4,2},{5,3},{6,4},{7,5},{8,14},{9,15},{10,... | collective-permute-start | bytes 98312 | tf_op jit(solution)/shard_map/ppermute | solution.py:333
  42.0 17.9 %all-to-all-start.1 = ((bf16[16,64,256]{2,1,0:T(8,128)(2,1)}), bf16[16,64,256]{2,1,0:T(8,128)(2,1)S(1)}, u32[]{:S(2)}, u32[]{:S(2)}) async-start(bf16[16,64,256]{2,1,0:T(8,128)(2,1)} %broadcast_in_dim.43), calls=%async_computation.1 | async-start | bytes 1048576 | tf_op jit(solution)/shard_map/all_to_all | solution.py:419
  48.9 11.0 %copy-start.3 = (bf16[256,384]{1,0:T(8,128)(2,1)S(1)}, bf16[256,384]{1,0:T(8,128)(2,1)}, u32[]{:S(2)}) copy-start(bf16[256,384]{1,0:T(8,128)(2,1)} %grad_out.1) | copy-start | bytes 589828
  48.9 11.0 %copy-start.5 = (f32[128]{0:T(128)S(1)}, f32[128]{0:T(128)}, u32[]{:S(2)}) copy-start(f32[128]{0:T(128)} %param.30) | copy-start | bytes 1540
  59.9 0.9 copy-start.6
  99.6 14.0 %collective-permute-start.5 = (f32[80,1280]{1,0:T(8,128)S(1)}, f32[80,1280]{1,0:T(8,128)S(1)}, u32[]{:S(2)}, u32[]{:S(2)}) collective-permute-start(f32[80,1280]{1,0:T(8,128)S(1)} %get-tuple-element.10), channel_id=1, source_target_pairs={{0,16},{8,24},{16,0},{24,8},{32,48},{40,56},{48,32},{56,40},{64,80... | collective-permute-start | bytes 1228808 | tf_op jit(solution)/shard_map/ppermute | solution.py:333
  100.5 19.0 %collective-permute-start.6 = (f32[80,1280]{1,0:T(8,128)S(1)}, f32[80,1280]{1,0:T(8,128)S(1)}, u32[]{:S(2)}, u32[]{:S(2)}) collective-permute-start(f32[80,1280]{1,0:T(8,128)S(1)} %get-tuple-element.10), channel_id=1, source_target_pairs={{0,8},{8,16},{16,24},{24,0},{32,40},{40,48},{48,56},{56,32},{64,72... | collective-permute-start | bytes 1228808 | tf_op jit(solution)/shard_map/ppermute | solution.py:333
  101.0 18.5 %collective-permute-start.7 = (f32[80,1280]{1,0:T(8,128)S(1)}, f32[80,1280]{1,0:T(8,128)S(1)}, u32[]{:S(2)}, u32[]{:S(2)}) collective-permute-start(f32[80,1280]{1,0:T(8,128)S(1)} %get-tuple-element.10), channel_id=1, source_target_pairs={{0,24},{8,0},{16,8},{24,16},{32,56},{40,32},{48,40},{56,48},{64,88... | collective-permute-start | bytes 1228808 | tf_op jit(solution)/shard_map/ppermute | solution.py:333
  119.6 12.4 %collective-permute-start.10 = (f32[80,1280]{1,0:T(8,128)S(1)}, f32[80,1280]{1,0:T(8,128)S(1)}, u32[]{:S(2)}, u32[]{:S(2)}) collective-permute-start(f32[80,1280]{1,0:T(8,128)S(1)} %add_add_fusion.1), channel_id=1, source_target_pairs={{0,96},{8,104},{16,112},{24,120},{32,0},{40,8},{48,16},{56,24},{64... | collective-permute-start | bytes 1228808 | tf_op jit(solution)/shard_map/ppermute | solution.py:333
  120.7 13.9 %collective-permute-start.8 = (f32[80,1280]{1,0:T(8,128)S(1)}, f32[80,1280]{1,0:T(8,128)S(1)}, u32[]{:S(2)}, u32[]{:S(2)}) collective-permute-start(f32[80,1280]{1,0:T(8,128)S(1)} %add_add_fusion.1), channel_id=1, source_target_pairs={{0,64},{8,72},{16,80},{24,88},{32,96},{40,104},{48,112},{56,120},{... | collective-permute-start | bytes 1228808 | tf_op jit(solution)/shard_map/ppermute | solution.py:333
  121.6 20.5 %collective-permute-start.9 = (f32[80,1280]{1,0:T(8,128)S(1)}, f32[80,1280]{1,0:T(8,128)S(1)}, u32[]{:S(2)}, u32[]{:S(2)}) collective-permute-start(f32[80,1280]{1,0:T(8,128)S(1)} %add_add_fusion.1), channel_id=1, source_target_pairs={{0,32},{8,40},{16,48},{24,56},{32,64},{40,72},{48,80},{56,88},{64,... | collective-permute-start | bytes 1228808 | tf_op jit(solution)/shard_map/ppermute | solution.py:333
  142.2 4.2 %copy-start.10 = (f32[80,1280]{1,0:T(8,128)}, f32[80,1280]{1,0:T(8,128)S(1)}, u32[]{:S(2)}) copy-start(f32[80,1280]{1,0:T(8,128)S(1)} %add_add_fusion) | copy-start | bytes 1228804
  142.2 4.2 %copy-start.8 = (f32[64,3072]{1,0:T(8,128)S(1)}, f32[64,3072]{1,0:T(8,128)}, u32[]{:S(2)}) copy-start(f32[64,3072]{1,0:T(8,128)} %copy-done.7) | copy-start | bytes 2359300
  148.1 12.3 %all-to-all-start.4 = ((bf16[8,64,384]{2,1,0:T(8,128)(2,1)}), bf16[8,64,384]{2,1,0:T(8,128)(2,1)S(1)}, u32[]{:S(2)}, u32[]{:S(2)}) async-start(bf16[8,64,384]{2,1,0:T(8,128)(2,1)} %bitcast.43), calls=%async_computation.4 | async-start | bytes 786432 | tf_op jit(solution)/shard_map/all_to_all | solution.py:492
  160.4 0.8 copy-start.12
  160.4 5.1 %copy-start.17 = (f32[3072]{0:T(1024)S(1)}, f32[3072]{0:T(1024)}, u32[]{:S(2)}) copy-start(f32[3072]{0:T(1024)} %param.28) | copy-start | bytes 36868
  161.2 25.9 %all-to-all-start.2 = ((bf16[8,256,384]{2,1,0:T(8,128)(2,1)}), bf16[8,256,384]{2,1,0:T(8,128)(2,1)}, u32[]{:S(2)}, u32[]{:S(2)}) async-start(bf16[8,256,384]{2,1,0:T(8,128)(2,1)} %bitcast.47), calls=%async_computation.2 | async-start | bytes 3145728 | tf_op jit(solution)/shard_map/all_to_all | solution.py:497
  187.1 28.3 %all-to-all-start.3 = ((bf16[16,256,192]{1,2,0:T(8,128)(2,1)}), bf16[16,256,192]{1,2,0:T(8,128)(2,1)S(1)}, u32[]{:S(2)}, u32[]{:S(2)}) async-start(bf16[16,256,192]{1,2,0:T(8,128)(2,1)} %bitcast.16), calls=%async_computation.3 | async-start | bytes 3145728 | tf_op jit(solution)/shard_map/all_to_all | solution.py:516
Sparse Core Ops, SparseCore 0:
  21.9 27.4 all-gather.1

commit v2 on v1

v2 whole, which is shorter than its diff:
```python
import functools

import jax
import jax.numpy as jnp
from jax import lax
from jax.experimental import pallas as pl
from jax.experimental.pallas import tpu as pltpu
from jax.sharding import PartitionSpec as P

D = 3072
HD = 128
LAT = 16
CLIPS = 4
SIDE = 16
PSIDE = 8
CELLS = 256
GS = 16
HEADS = 2
ROWS = 256
FRAMES = 4
FEAT = 64
AUG = 80
EXT = 144
EPSILON = 1e-06
HIGHEST = lax.Precision.HIGHEST
LOG2E = 1.4426950408889634
OFF = -1e30
F32 = jnp.float32
BF16 = jnp.bfloat16
MIB = 1024 * 1024
PREPARE_UNROLL = 4
FWD_BLOCK = 1024
FWD_UNROLL = 1
BWD_BLOCK = 1024
BWD_UNROLL = 1


def nn(a, b):
    return lax.dot_general(a, b, (((1,), (0,)), ((), ())), preferred_element_type=F32)


def nt(a, b):
    return lax.dot_general(a, b, (((1,), (1,)), ((), ())), preferred_element_type=F32)


def tn(a, b):
    return lax.dot_general(a, b, (((0,), (0,)), ((), ())), preferred_element_type=F32)


def hi_lo(value):
    hi = value.astype(BF16)
    return hi, (value - hi.astype(F32)).astype(BF16)


def clip_number(frames, frame):
    one = frames[0]
    two = one + frames[1]
    three = two + frames[2]
    return (
        jnp.where(frame >= one, 1, 0) + jnp.where(frame >= two, 1, 0) + jnp.where(frame >= three, 1, 0)
    )


def frame_facts(frames, res, frame):
    clip = clip_number(frames, frame)
    one = frames[0]
    two = one + frames[1]
    three = two + frames[2]
    start = jnp.where(
        clip == 0, 0, jnp.where(clip == 1, one, jnp.where(clip == 2, two, three))
    )
    height, width = res[3:4, 0:1], res[3:4, 1:2]
    for c in range(CLIPS - 1):
        height = jnp.where(clip == c, res[c : c + 1, 0:1], height)
        width = jnp.where(clip == c, res[c : c + 1, 1:2], width)
    return clip, start, height, width


def column(row):
    return jnp.broadcast_to(row, (8, row.shape[1])).T[:, :1]


def turn_rows(width):
    feat = lax.broadcasted_iota(jnp.int32, (FEAT, width), 0)
    other = lax.broadcasted_iota(jnp.int32, (FEAT, width), 1)
    return jnp.where((feat & 3) * LAT + (feat >> 2) == other, 1.0, 0.0).astype(BF16)


def turn_back():
    feat = lax.broadcasted_iota(jnp.int32, (FEAT, FEAT), 0)
    other = lax.broadcasted_iota(jnp.int32, (FEAT, FEAT), 1)
    return jnp.where((feat & 15) * 4 + (feat >> 4) == other, 1.0, 0.0).astype(BF16)


def cell_order():
    cell = lax.broadcasted_iota(jnp.int32, (CELLS, CELLS), 0)
    place = lax.broadcasted_iota(jnp.int32, (CELLS, CELLS), 1)
    row, col = cell >> 4, cell & 15
    spot = ((row & 1) * 2 + (col & 1)) * 64 + (row >> 1) * PSIDE + (col >> 1)
    return jnp.where(spot == place, 1.0, 0.0).astype(BF16)


def cell_valid(height, width):
    cell = lax.broadcasted_iota(jnp.int32, (1, CELLS), 1)
    return ((cell >> 4) < height) & ((cell & 15) < width)


def stats_kernel(frames, res, enc, place, out):
    slab = lax.axis_index("slab")
    lane = lax.broadcasted_iota(jnp.int32, (FEAT, 128), 1)
    total = jnp.zeros((FEAT, 128), F32)
    for f in range(FRAMES):
        clip, _, height, width = frame_facts(frames, res, slab * FRAMES + f)
        kept = jnp.where(cell_valid(height, width), enc[f].astype(F32), 0.0)
        sums = jnp.sum(kept, axis=1, keepdims=True)
        squares = jnp.sum(kept * kept, axis=1, keepdims=True)
        total = total + jnp.where(lane == clip, sums, 0.0) + jnp.where(lane == clip + 4, squares, 0.0)
    groups = [jnp.sum(total[g * GS : (g + 1) * GS], axis=0, keepdims=True) for g in range(4)]
    payload = jnp.concatenate(groups + [place[...].astype(F32), jnp.zeros((2, 128), F32)], axis=0)
    for j in range(out.shape[0]):
        out[j] = payload


def conv_kernel(frames, res, enc, rim, sums, gain, bias, taps, out, proj):
    totals = jnp.sum(sums[...], axis=0)
    lane = lax.broadcasted_iota(jnp.int32, (8, 128), 1)
    first = lax.axis_index("slab") * FRAMES
    gain_c, bias_c = column(gain[...]), column(bias[...])
    taps_t = taps[...].astype(F32).T.astype(BF16)
    cell = lax.broadcasted_iota(jnp.int32, (1, CELLS), 1)
    row, col = cell >> 4, cell & 15
    for j in range(FRAMES + 2):
        clip, _, height, width = frame_facts(frames, res, jnp.maximum(first - 2 + j, 0))
        count = (frames[clip] * height * width * GS).astype(F32)
        mean = jnp.sum(jnp.where(lane == clip, totals, 0.0), axis=1, keepdims=True) / count
        square = jnp.sum(jnp.where(lane == clip + 4, totals, 0.0), axis=1, keepdims=True) / count
        rstd = lax.rsqrt(square - mean * mean + EPSILON)
        mean_c = jnp.concatenate([jnp.broadcast_to(mean[g : g + 1], (GS, 1)) for g in range(4)], axis=0)
        rstd_c = jnp.concatenate([jnp.broadcast_to(rstd[g : g + 1], (GS, 1)) for g in range(4)], axis=0)
        value = rim[j] if j < 2 else enc[j - 2]
        pre = (value.astype(F32) - mean_c) * rstd_c * gain_c + bias_c
        act = jnp.where(cell_valid(height, width), pre / (1.0 + jnp.exp(-pre)), 0.0)
        proj[j] = nn(taps_t, act.astype(BF16))
    results = []
    for f in range(FRAMES):
        _, start, _, _ = frame_facts(frames, res, first + f)
        source = [jnp.maximum(first + f - 2 + dt, start) - first + 2 for dt in range(3)]
        planes = [proj[source[dt], dt * 144 : (dt + 1) * 144, :] for dt in range(3)]
        joint = planes[0] + planes[1] + planes[2]
        result = jnp.zeros((LAT, CELLS), F32)
        for dx in range(3):
            part = jnp.zeros((LAT, CELLS), F32)
            for dy in range(3):
                tap = (dy * 3 + dx) * LAT
                piece = joint[tap : tap + LAT]
                if dy != 1:
                    piece = pltpu.roll(piece, (-(dy - 1) * SIDE) % CELLS, 1)
                    inside = (row >= 1) if dy == 0 else (row <= SIDE - 2)
                    piece = jnp.where(inside, piece, 0.0)
                part = part + piece
            if dx != 1:
                part = pltpu.roll(part, (-(dx - 1)) % CELLS, 1)
                inside = (col >= 1) if dx == 0 else (col <= SIDE - 2)
                part = jnp.where(inside, part, 0.0)
            result = result + part
        results.append(result.astype(BF16))
    sorted_cells = nn(jnp.concatenate(results, axis=0), cell_order()).astype(BF16)
    for ab in range(4):
        out[ab * LAT : (ab + 1) * LAT, :] = jnp.concatenate(
            [
                sorted_cells[f * LAT : (f + 1) * LAT, ab * 64 : (ab + 1) * 64]
                for f in range(FRAMES)
            ],
            axis=1,
        )


def shift_row(m_hi, m_lo, part):
    unit = jnp.where(lax.broadcasted_iota(jnp.int32, (16, AUG), 1) == FEAT + 1, 1.0, 0.0).astype(BF16)
    return (nt(unit, m_hi[part, :]) + nt(unit, m_lo[part, :]))[0:1]


def share_kernel(pair, one, two, three, out, total):
    value = (pair[...].astype(F32) + two[...].astype(F32)) + (one[...].astype(F32) + three[...].astype(F32))
    total[...] = value
    for j in range(out.shape[0]):
        out[j] = value.astype(BF16)


def cotangent_kernel(grad0, grad1, grad2, grad3, other0, other1, other2, other3, gate, w_out, lat_sorted, d_attn, d_out, latents):
    place = lax.axis_index("mp")
    core, level = lax.rem(place, 2), lax.div(place, 2)
    total = jnp.zeros((ROWS, HEADS * HD), F32)
    for k, grads in enumerate(((grad0, other0), (grad1, other1), (grad2, other2), (grad3, other3))):
        for side in range(2):
            m = lax.rem(level - k + 4, 4) * 2 + (core if side == 0 else 1 - core)
            cols = pl.ds(pl.multiple_of(m * 384, 128), 384)
            part = (grads[side][...].astype(F32) * gate[:, cols]).astype(BF16)
            d_attn[m] = part
            total = total + nt(part, w_out[:, cols])
    d_out[...] = total.astype(BF16)
    by_frame = jnp.concatenate(
        [
            jnp.concatenate(
                [lat_sorted[ab * LAT : (ab + 1) * LAT, f * 64 : (f + 1) * 64] for ab in range(4)], axis=1
            )
            for f in range(FRAMES)
        ],
        axis=0,
    )
    hi, lo = hi_lo(by_frame)
    order = cell_order()
    values = nt(hi, order) + nt(lo, order)
    for f in range(FRAMES):
        latents[f] = values[f * LAT : (f + 1) * LAT]


def prepare_kernel(
    embed_w,
    embed_b,
    shift,
    scale,
    w_hbm,
    gram_hi,
    gram_lo,
    m_hi,
    m_lo,
    m_k,
    centered_two,
    own_rows,
    window,
    w_qkv,
    arrived,
):
    fetch = pltpu.make_async_copy(w_hbm, w_qkv, arrived)
    fetch.start()
    row = lax.broadcasted_iota(jnp.int32, (16, D), 0)
    extra = jnp.where(row == 0, embed_b[...], 0.0)
    augmented = jnp.concatenate([nn(turn_back(), embed_w[...]), extra], axis=0)
    centered = augmented - jnp.mean(augmented, axis=1, keepdims=True)
    c_hi, c_lo = hi_lo(centered)
    centered_two[:AUG, :] = c_hi
    centered_two[AUG:, :] = c_lo
    gram = (nt(c_hi, c_hi) + nt(c_hi, c_lo) + nt(c_lo, c_hi)) * (1.0 / D)
    g_hi, g_lo = hi_lo(gram)
    gram_hi[...] = g_hi
    gram_lo[...] = g_lo
    row = lax.broadcasted_iota(jnp.int32, (AUG, D), 0)
    modulated = jnp.where(row == FEAT + 1, shift[...], centered * (1.0 + scale[...]))
    a_hi, a_lo = hi_lo(modulated)
    fetch.wait()
    both = nn(jnp.concatenate([a_hi, a_lo], axis=0), w_qkv[...])
    turned = (both[:AUG] + both[AUG:]).T
    t_hi, t_lo = hi_lo(turned)
    m_hi[...] = t_hi
    m_lo[...] = t_lo
    for h in range(HEADS):
        keys = slice(h * 384 + 128, h * 384 + 256)
        m_k[h * HD : (h + 1) * HD, :] = jnp.concatenate([t_hi[keys], t_hi[keys], t_lo[keys]], axis=1)
    window[...] = modulated.T
    slab = lax.axis_index("slab")
    o_hi, o_lo = hi_lo(window[pl.ds(pl.multiple_of(slab * 192, 64), 192), :])
    own_rows[...] = jnp.concatenate([o_hi, o_lo], axis=1)


def forward_kernel(
    frames,
    res,
    patches,
    place,
    gram_hi,
    gram_lo,
    m_k,
    m_hi,
    m_lo,
    d_out,
    q_gain,
    k_gain,
    grad_out,
    w_out,
    d_attn,
    embed_w,
    embed_b,
    attn_mine,
    attn_other,
    g_part0,
    g_part1,
    g_part2,
    g_part3,
    hidden_cols,
    early,
    g_own,
    s_sent,
    k_sent,
    rk_t,
    q_ext,
    q_norm,
    q_facts,
    u_cat,
    s_own,
):
    s_t, k_t = s_sent.buffer, k_sent.buffer
    blocks = patches.shape[0]
    row_aug = lax.broadcasted_iota(jnp.int32, (AUG, ROWS), 0)
    row16 = lax.broadcasted_iota(jnp.int32, (16, ROWS), 0)
    token = lax.broadcasted_iota(jnp.int32, (1, ROWS), 1)
    position = lax.broadcasted_iota(jnp.int32, (ROWS, ROWS), 0).astype(F32)
    base = (lax.axis_index("slab") * ROWS).astype(F32)
    k_gain_c = column(k_gain[...])
    one_row = jnp.where(row16 == 0, 1.0, 0.0).astype(BF16)

    def prepare(j, carry):
        x_q, clip_q = carry
        block = pl.ds(pl.multiple_of(j * ROWS, ROWS), ROWS)
        x_aug = jnp.concatenate([patches[j], one_row], axis=0)
        x_f = x_aug.astype(F32)
        gx = nn(gram_hi[...], x_aug) + nn(gram_lo[...], x_aug)
        rstd = lax.rsqrt(jnp.sum(gx * x_f, axis=0, keepdims=True) + EPSILON)
        s_hi, s_lo = hi_lo(jnp.where(row_aug == FEAT + 1, 1.0, x_f * rstd))
        s_t[:AUG, block] = s_hi
        s_t[AUG:, block] = s_lo
        clip = clip_number(frames, j * FRAMES + (token >> 6))
        height = jnp.zeros((1, ROWS), jnp.int32)
        width = jnp.zeros((1, ROWS), jnp.int32)
        for c in range(CLIPS):
            height = jnp.where(clip == c, res[c : c + 1, 0:1], height)
            width = jnp.where(clip == c, res[c : c + 1, 1:2], width)
        valid = (2 * ((token >> 3) & 7) < height) & (2 * (token & 7) < width)
        member = row16 == clip
        mask = jnp.where((row16 < CLIPS) & ~(member & valid), OFF, 0.0).astype(BF16)
        both = nn(m_k[...], jnp.concatenate([s_hi, s_lo, s_hi], axis=0))
        for h in range(HEADS):
            k = both[h * HD : (h + 1) * HD]
            rk = lax.rsqrt(jnp.mean(k * k, axis=0, keepdims=True) + EPSILON)
            rk_t[h, :, block] = jnp.broadcast_to(rk, (8, ROWS))
            k_t[h, :HD, block] = (k * rk * k_gain_c).astype(BF16)
            k_t[h, HD:, block] = mask
        spot = jnp.concatenate([place[j, 4:5, :], place[j, 5:6, :]], axis=1)
        chosen = jnp.where(spot == position + base, 1.0, 0.0).astype(BF16)
        x_q = x_q + nt(chosen, x_aug)
        clip_q = clip_q + nt(chosen, jnp.where(member, 1.0, 0.0).astype(BF16))
        return x_q, clip_q

    x_q, clip_q = lax.fori_loop(
        0, blocks, prepare, (jnp.zeros((ROWS, AUG), F32), jnp.zeros((ROWS, 16), F32)), unroll=PREPARE_UNROLL
    )
    s_sent.send()
    k_sent.send()
    x_qb = x_q.astype(BF16)
    own_cols = pl.ds(pl.multiple_of(lax.axis_index("mp") * 384, 128), 384)
    embed_cols = nn(turn_back(), embed_w.ready()[:, own_cols]).astype(BF16)
    hidden_cols[...] = (nn(x_qb[:, :FEAT], embed_cols) + embed_b[:, own_cols]).astype(BF16)
    g_own[...] = nn(turn_rows(AUG), tn(x_qb, grad_out.ready()[...]).astype(BF16))
    gx_q = nn(x_qb, gram_hi[...]) + nn(x_qb, gram_lo[...])
    rstd_q = lax.rsqrt(jnp.sum(gx_q * x_q, axis=1, keepdims=True) + EPSILON)
    lane_aug = lax.broadcasted_iota(jnp.int32, (ROWS, AUG), 1)
    s_q = jnp.where(lane_aug == FEAT + 1, 1.0, x_q * rstd_q)
    s_own[...] = s_q
    s_qhi, s_qlo = hi_lo(s_q)
    clip_qb = clip_q.astype(BF16)
    lane = lax.broadcasted_iota(jnp.int32, (ROWS, 128), 1)
    facts = jnp.zeros((ROWS, 128), F32)
    for h in range(HEADS):
        mine = slice(h * 384, h * 384 + 128)
        q = nt(s_qhi, m_hi[mine, :]) + nt(s_qlo, m_hi[mine, :]) + nt(s_qhi, m_lo[mine, :])
        rq = lax.rsqrt(jnp.mean(q * q, axis=1, keepdims=True) + EPSILON)
        qn = q * rq
        q_norm[h] = qn
        q_ext[h, :, :HD] = (qn * (q_gain[...] * (HD**-0.5 * LOG2E))).astype(BF16)
        q_ext[h, :, HD:] = clip_qb
        facts = jnp.where(lane == h, rq, facts)

    def forward(j, totals):
        block = pl.ds(pl.multiple_of(j * FWD_BLOCK, FWD_BLOCK), FWD_BLOCK)
        s_block = s_t[:, block]
        probs = [jnp.exp2(nn(q_ext[h], k_t[h, :, block])).astype(BF16) for h in range(HEADS)]
        return tuple(totals[h] + nt(probs[h], s_block) for h in range(HEADS))

    totals = lax.fori_loop(
        0, 4096 // FWD_BLOCK, forward, (jnp.zeros((ROWS, 2 * AUG), F32),) * HEADS, unroll=FWD_UNROLL
    )
    heads = []
    d_out = d_out.ready()
    for h in range(HEADS):
        inv_l = 1.0 / totals[h][:, FEAT + 1 : FEAT + 2]
        z_hi, z_lo = hi_lo((totals[h][:, :AUG] + totals[h][:, AUG:]) * inv_l)
        mine = slice(h * 384 + 256, h * 384 + 384)
        att = (nt(z_hi, m_hi[mine, :]) + nt(z_lo, m_hi[mine, :]) + nt(z_hi, m_lo[mine, :])).astype(BF16)
        heads.append(att)
        d_bf = d_out[:, h * HD : (h + 1) * HD]
        early[:, h * HD : (h + 1) * HD] = tn(z_hi, d_bf)
        do = d_bf.astype(F32)
        shift_v = shift_row(m_hi, m_lo, mine)
        weight = jnp.sum(do * (att.astype(F32) - shift_v), axis=1, keepdims=True) * inv_l
        facts = jnp.where(lane == 2 + h, weight, facts)
        u = (nn(d_bf, m_hi[mine, :]) + nn(d_bf, m_lo[mine, :])) * inv_l
        u_hi, u_lo = hi_lo(jnp.where(lane_aug == FEAT + 1, 0.0, u))
        u_cat[h] = jnp.concatenate([u_hi, u_lo, u_hi], axis=1)
    q_facts[...] = facts
    att_all = jnp.concatenate(heads, axis=1)
    place_mp, slab = lax.axis_index("mp"), lax.axis_index("slab")
    core, level = lax.rem(place_mp, 2), lax.div(place_mp, 2)
    y_pos, x_pos = lax.div(slab, 4), lax.rem(slab, 4)
    d_attn, w_out = d_attn.ready(), w_out.ready()
    for k, g_part in enumerate((g_part0, g_part1, g_part2, g_part3)):
        y_to = lax.rem(y_pos + k, 4)
        for half in range(2):
            both = tn(d_attn[2 * y_to + half], att_all).astype(BF16)
            for side in range(2):
                slot = lax.rem(2 * half + side - x_pos + 4, 4)
                g_part.buffer[slot] = both[side * 192 : (side + 1) * 192]
        g_part.send()
    for side, attn_part in enumerate((attn_other, attn_mine)):
        for k in range(4):
            m = 2 * lax.rem(level + k, 4) + (core if side == 1 else 1 - core)
            cols = pl.ds(pl.multiple_of(m * 384, 128), 384)
            attn_part.buffer[k] = nn(att_all, w_out[:, cols]).astype(BF16)
        attn_part.send()


def backward_kernel(
    s_hbm,
    k_hbm,
    rk_t,
    q_ext,
    q_norm,
    q_facts,
    u_cat,
    s_own,
    m_hi,
    m_lo,
    q_gain,
    k_gain,
    early,
    mod_scale,
    centered,
    w_hbm,
    sums,
    y_mine,
    y_other,
    q_t,
    w_qkv,
    arrived,
    s_t,
    k_t,
    s_sems,
    k_sems,
):
    def fetch_block(j):
        block = pl.ds(pl.multiple_of(j * BWD_BLOCK, BWD_BLOCK), BWD_BLOCK)
        return (
            pltpu.make_async_copy(s_hbm.at[:, block], s_t.at[:, block], s_sems.at[j]),
            pltpu.make_async_copy(k_hbm.at[:, :, block], k_t.at[:, :, block], k_sems.at[j]),
        )

    for j in range(4096 // BWD_BLOCK):
        for copy in fetch_block(j):
            copy.start()
    fetch = pltpu.make_async_copy(w_hbm, w_qkv, arrived)
    fetch.start()
    shift_k = []
    for h in range(HEADS):
        q_t[h] = q_ext[h, :, :HD].astype(F32).T.astype(BF16)
        mine = slice(h * 384 + 128, h * 384 + 256)
        shift_k.append(
            m_hi[mine, FEAT + 1 : FEAT + 2].astype(F32) + m_lo[mine, FEAT + 1 : FEAT + 2].astype(F32)
        )
    k_gain_c = column(k_gain[...])
    gain_back = k_gain_c * (1.0 / LOG2E)
    gain_inv = 1.0 / k_gain_c
    weights = [q_facts[:, 2 + h : 3 + h] for h in range(HEADS)]

    def backward(j, carry):
        grad_qs, p_k, quad = carry
        for copy in fetch_block(j):
            copy.wait()
        block = pl.ds(pl.multiple_of(j * BWD_BLOCK, BWD_BLOCK), BWD_BLOCK)
        s_hi = s_t[:AUG, block]
        s_cat = jnp.concatenate([s_hi, s_hi, s_t[AUG:, block]], axis=0)
        m2 = jnp.zeros((1, BWD_BLOCK), F32)
        new_q, dks = [], []
        for h in range(HEADS):
            keys = k_t[h, :HD, block]
            p = jnp.exp2(nn(q_ext[h], k_t[h, :, block]))
            raw = p * nn(u_cat[h], s_cat)
            m2 = m2 + jnp.sum(raw, axis=0, keepdims=True)
            d_score = (raw - p * weights[h]).astype(BF16)
            new_q.append(grad_qs[h] + nt(d_score, keys))
            scaled = nn(q_t[h], d_score) * gain_back
            kn = keys.astype(F32) * gain_inv
            rk = rk_t[h, 0:1, block]
            dk = rk * (scaled - kn * jnp.mean(scaled * kn, axis=0, keepdims=True))
            m2 = m2 + jnp.sum(dk * (kn * (1.0 / rk) - shift_k[h]), axis=0, keepdims=True)
            dks.append(dk.astype(BF16))
        p_k = p_k + nt(s_hi, jnp.concatenate(dks, axis=0))
        quad = quad + nt((s_hi.astype(F32) * m2).astype(BF16), s_hi)
        return tuple(new_q), p_k, quad

    grad_qs, p_k, quad = lax.fori_loop(
        0,
        4096 // BWD_BLOCK,
        backward,
        (
            (jnp.zeros((ROWS, HD), F32),) * HEADS,
            jnp.zeros((AUG, HEADS * HD), F32),
            jnp.zeros((AUG, AUG), F32),
        ),
        unroll=BWD_UNROLL,
    )
    s_q = s_own[...]
    s_qhi = s_q.astype(BF16)
    m2_q = jnp.zeros((ROWS, 1), F32)
    pieces = []
    for h in range(HEADS):
        mine = slice(h * 384, h * 384 + 128)
        rq = q_facts[:, h : h + 1]
        qn = q_norm[h]
        scaled = grad_qs[h] * (q_gain[...] * HD**-0.5)
        dq = rq * (scaled - qn * jnp.mean(scaled * qn, axis=1, keepdims=True))
        shift_q = shift_row(m_hi, m_lo, mine)
        m2_q = m2_q + jnp.sum(dq * (qn * (1.0 / rq) - shift_q), axis=1, keepdims=True)
        pieces += [tn(s_qhi, dq.astype(BF16)), p_k[:, h * HD : (h + 1) * HD], early[:, h * HD : (h + 1) * HD]]
    p_all = jnp.concatenate(pieces, axis=1).astype(BF16)
    sums[...] = p_all
    quad = ((quad + tn((s_q * m2_q).astype(BF16), s_qhi)) * (1.0 / D)).astype(BF16)
    turn = turn_rows(AUG)
    turned = nn(turn, p_all).astype(BF16)
    quad = nn(turn, quad).astype(BF16)
    fetch.wait()
    back = nt(turned, w_qkv[...]) * (1.0 + mod_scale[...])
    back = back - jnp.mean(back, axis=1, keepdims=True)
    back = (back - nn(jnp.concatenate([quad, quad], axis=1), centered[...])).astype(BF16)
    place = lax.axis_index("mp")
    core, level = lax.rem(place, 2), lax.div(place, 2)
    for z in range(4):
        slot = lax.rem(z - level + 4, 4)
        even = back[:, 2 * z * 384 : (2 * z + 1) * 384]
        odd = back[:, (2 * z + 1) * 384 : (2 * z + 2) * 384]
        y_mine[slot] = jnp.where(core == 0, even, odd)
        y_other[slot] = jnp.where(core == 0, odd, even)


def weights_kernel(own, one, two, three, own_rows, g_qkv, g_embed):
    total = (own[...].astype(F32) + two[...].astype(F32)) + (one[...].astype(F32) + three[...].astype(F32))
    p_all = total[:, :768].astype(BF16)
    g_qkv[...] = nn(own_rows[...], jnp.concatenate([p_all, p_all], axis=0))
    g_embed[...] = total[:FEAT, 768:]


VMEM = pl.BlockSpec(memory_space=pltpu.VMEM)
SMEM = pl.BlockSpec(memory_space=pltpu.SMEM)
ANY = pl.BlockSpec(memory_space=pl.ANY)


class Fetched:
    def __init__(self, source, buffer, sem):
        self.buffer, self.copy = buffer, pltpu.make_async_copy(source, buffer, sem)
        self.copy.start()

    def ready(self):
        self.copy.wait()
        return self.buffer


class Sent:
    def __init__(self, target, buffer, sem):
        self.buffer, self.copy = buffer, pltpu.make_async_copy(buffer, target, sem)

    def send(self):
        self.copy.start()


def call(kernel, inputs, outputs, scratch, flops, mib, places, out_places=None):
    single = not isinstance(outputs, tuple)
    outs = (outputs,) if single else outputs
    out_places = out_places or "v" * len(outs)
    staged = [
        (i, pltpu.VMEM(v.shape, v.dtype)) for i, (p, v) in enumerate(zip(places, inputs, strict=True)) if p == "l"
    ]
    sent = [(i, pltpu.VMEM(o.shape, o.dtype)) for i, (p, o) in enumerate(zip(out_places, outs, strict=True)) if p == "e"]
    n_in, n_out, n_stage, n_sent = len(inputs), len(outs), len(staged), len(sent)

    def wrapped(*refs):
        ins, results = list(refs[:n_in]), list(refs[n_in : n_in + n_out])
        rest = refs[n_in + n_out :]
        buffers, rest = rest[:n_stage], rest[n_stage:]
        holds, rest = rest[:n_sent], rest[n_sent:]
        sems, rest = rest[: n_stage + n_sent], rest[n_stage + n_sent :]
        for slot, (i, _) in enumerate(staged):
            ins[i] = Fetched(ins[i], buffers[slot], sems[slot])
        for slot, (i, _) in enumerate(sent):
            results[i] = Sent(results[i], holds[slot], sems[n_stage + slot])
        kernel(*ins, *results, *rest)
        for i, _ in sent:
            results[i].copy.wait()

    specs = {"v": VMEM, "e": ANY, "l": ANY, "r": ANY, "s": SMEM}
    result = pl.pallas_call(
        wrapped,
        out_shape=outs,
        in_specs=[specs[p] for p in places],
        out_specs=tuple(specs[p] for p in out_places),
        scratch_shapes=[b for _, b in staged]
        + [b for _, b in sent]
        + [pltpu.SemaphoreType.DMA] * (n_stage + n_sent)
        + scratch,
        compiler_params=pltpu.CompilerParams(vmem_limit_bytes=mib * MIB),
        cost_estimate=pl.CostEstimate(flops=flops, bytes_accessed=1 << 20, transcendentals=0),
    )(*inputs)
    return result[0] if single else result


def shift_by(value, axis, move):
    return lax.ppermute(value, axis, [(i, move(i)) for i in range(lax.axis_size(axis))])


def along_x(k):
    return lambda i: (i // 4) * 4 + (i % 4 + k) % 4


def along_y(k):
    return lambda i: ((i // 4 + k) % 4) * 4 + i % 4


def along_z(k):
    return lambda i: ((i // 2 + k) % 4) * 2 + i % 2


def sum_of_four(value, axis, move, kind):
    sent = value.astype(kind)
    one, two, three = (shift_by(sent, axis, move(k)).astype(F32) for k in (1, 2, 3))
    return (sent.astype(F32) + two) + (one + three)


def level_sum(pair):
    one, two, three = (shift_by(pair[k], "mp", along_z(k)).astype(F32) for k in (1, 2, 3))
    return (pair[0].astype(F32) + two) + (one + three)


def body(
    enc_feat,
    gn_gain,
    gn_bias,
    conv_w,
    clip_frames,
    clip_res,
    token_place,
    embed_w,
    embed_b,
    mod_shift,
    mod_scale,
    mod_gate,
    w_qkv,
    q_gain,
    k_gain,
    w_out,
    grad_out,
):
    slabs = lax.axis_size("slab")
    mp_size = lax.axis_size("mp")
    mp_pos = lax.axis_index("mp")
    cols_dev = D // mp_size
    row_cols = D // slabs

    clip_res = jnp.pad(clip_res, ((0, 4), (0, 126)))
    all_sent = call(
        stats_kernel,
        (clip_frames, clip_res, enc_feat, token_place.reshape(2, 128)),
        jax.ShapeDtypeStruct((slabs, 8, 128), F32),
        [],
        1 << 20,
        60,
        "svvv",
    )
    all_stats = lax.all_to_all(all_sent, "slab", split_axis=0, concat_axis=0, tiled=True)
    rim = shift_by(enc_feat[FRAMES - 2 :], "slab", lambda i: (i + 1) % slabs)
    rim, grad_sent = lax.optimization_barrier((rim, grad_out))
    grads = (grad_sent,) + tuple(shift_by(grad_sent, "mp", along_z(k)) for k in (1, 2, 3))
    embed_late, _ = lax.optimization_barrier((embed_b, all_sent))
    gram_hi, gram_lo, m_hi, m_lo, m_k, centered, own_rows = call(
        prepare_kernel,
        (embed_w, embed_late[None, :], mod_shift[None, :], mod_scale[None, :], w_qkv),
        (
            jax.ShapeDtypeStruct((AUG, AUG), BF16),
            jax.ShapeDtypeStruct((AUG, AUG), BF16),
            jax.ShapeDtypeStruct((768, AUG), BF16),
            jax.ShapeDtypeStruct((768, AUG), BF16),
            jax.ShapeDtypeStruct((HEADS * HD, 3 * AUG), BF16),
            jax.ShapeDtypeStruct((2 * AUG, D), BF16),
            jax.ShapeDtypeStruct((row_cols, 2 * AUG), BF16),
        ),
        [pltpu.VMEM((D, AUG), F32), pltpu.VMEM((D, 768), BF16), pltpu.SemaphoreType.DMA],
        1 << 33,
        60,
        "vvvvr",
    )
    gain, gram_hi = lax.optimization_barrier((gn_gain, gram_hi))
    partial = call(
        conv_kernel,
        (clip_frames, clip_res, enc_feat, rim, all_stats, gain[None, :], gn_bias[None, :], conv_w),
        jax.ShapeDtypeStruct((FEAT, CELLS), BF16),
        [pltpu.VMEM((FRAMES + 2, 432, CELLS), F32)],
        1 << 28,
        60,
        "svvvvvvv",
    )
    partial, grads = lax.optimization_barrier((partial, grads))
    pair = (partial.astype(F32) + shift_by(partial, "mp", lambda i: i ^ 1).astype(F32)).astype(BF16)
    patches_sent, lat_sorted = call(
        share_kernel,
        (pair,) + tuple(shift_by(pair, "mp", along_z(k)) for k in (1, 2, 3)),
        (
            jax.ShapeDtypeStruct((slabs, FEAT, CELLS), BF16),
            jax.ShapeDtypeStruct((FEAT, CELLS), F32),
        ),
        [],
        1 << 20,
        4,
        "vvvv",
    )
    all_patches = lax.all_to_all(patches_sent, "slab", split_axis=0, concat_axis=0, tiled=True)

    grads, lat_sorted = lax.optimization_barrier((grads, lat_sorted))
    others = tuple(shift_by(block, "mp", lambda i: i ^ 1) for block in grads)
    d_attn, d_out, latents = call(
        cotangent_kernel,
        (*grads, *others, mod_gate[None, :], w_out, lat_sorted),
        (
            jax.ShapeDtypeStruct((mp_size, ROWS, cols_dev), BF16),
            jax.ShapeDtypeStruct((ROWS, HEADS * HD), BF16),
            jax.ShapeDtypeStruct((FRAMES, LAT, CELLS), F32),
        ),
        [],
        1 << 32,
        60,
        "vvvvvvvvvvv",
    )

    (
        attn_mine,
        attn_other,
        *g_parts,
        hidden_cols,
        early,
        g_own,
        s_t,
        k_t,
        rk_t,
        q_ext,
        q_norm,
        q_facts,
        u_cat,
        s_own,
    ) = call(
        forward_kernel,
        (
            clip_frames,
            clip_res,
            all_patches,
            all_stats,
            gram_hi,
            gram_lo,
            m_k,
            m_hi,
            m_lo,
            d_out,
            q_gain[None, :],
            k_gain[None, :],
            grad_out,
            w_out,
            d_attn,
            embed_w,
            embed_b[None, :],
        ),
        (
            *(jax.ShapeDtypeStruct((4, ROWS, cols_dev), BF16),) * 2,
            *(jax.ShapeDtypeStruct((4, row_cols, HEADS * HD), BF16),) * 4,
            jax.ShapeDtypeStruct((ROWS, cols_dev), BF16),
            jax.ShapeDtypeStruct((AUG, 256), F32),
            jax.ShapeDtypeStruct((FEAT, cols_dev), F32),
            jax.ShapeDtypeStruct((2 * AUG, 4096), BF16),
            jax.ShapeDtypeStruct((HEADS, EXT, 4096), BF16),
            jax.ShapeDtypeStruct((HEADS, 8, 4096), F32),
            jax.ShapeDtypeStruct((HEADS, ROWS, EXT), BF16),
            jax.ShapeDtypeStruct((HEADS, ROWS, HD), F32),
            jax.ShapeDtypeStruct((ROWS, 128), F32),
            jax.ShapeDtypeStruct((HEADS, ROWS, 3 * AUG), BF16),
            jax.ShapeDtypeStruct((ROWS, AUG), F32),
        ),
        [],
        1 << 33,
        60,
        "svvvvvvvvlvvllllv",
        "eeeeeevvveevvvvvv",
    )
    attn_got = shift_by(attn_other, "mp", lambda i: i ^ 1)
    g_one = shift_by(g_parts[1], "slab", along_y(1))
    g_three = shift_by(g_parts[3], "slab", along_y(3))
    sums, y_mine, y_other = call(
        backward_kernel,
        (
            s_t,
            k_t,
            rk_t,
            q_ext,
            q_norm,
            q_facts,
            u_cat,
            s_own,
            m_hi,
            m_lo,
            q_gain[None, :],
            k_gain[None, :],
            early,
            mod_scale[None, :],
            centered,
            w_qkv,
        ),
        (
            jax.ShapeDtypeStruct((AUG, 768), BF16),
            jax.ShapeDtypeStruct((4, FEAT, cols_dev), BF16),
            jax.ShapeDtypeStruct((4, FEAT, cols_dev), BF16),
        ),
        [
            pltpu.VMEM((HEADS, HD, ROWS), BF16),
            pltpu.VMEM((D, 768), BF16),
            pltpu.SemaphoreType.DMA,
            pltpu.VMEM((2 * AUG, 4096), BF16),
            pltpu.VMEM((HEADS, EXT, 4096), BF16),
            pltpu.SemaphoreType.DMA((4096 // BWD_BLOCK,)),
            pltpu.SemaphoreType.DMA((4096 // BWD_BLOCK,)),
        ],
        1 << 34,
        60,
        "rrvvvvvvvvvvvvvr",
    )

    sums, y_mine, y_other, g_one, g_three, attn_got = lax.optimization_barrier(
        (sums, y_mine, y_other, g_one, g_three, attn_got)
    )
    y_got = shift_by(y_other, "mp", lambda i: i ^ 1)
    y_pair = (y_mine.astype(F32) + y_got.astype(F32)).astype(BF16)
    g_two = shift_by(g_parts[2], "slab", along_y(2))
    embed_part = level_sum(y_pair) + g_own
    payload = jnp.concatenate([sums, jnp.pad(embed_part, ((0, AUG - FEAT), (0, 0))).astype(BF16)], axis=1)
    payload, attn_mine = lax.optimization_barrier((payload, attn_mine))
    sent = tuple(shift_by(payload, "slab", along_x(k)) for k in (1, 2, 3))
    total = (
        (payload.astype(F32) + sent[1].astype(F32)) + (sent[0].astype(F32) + sent[2].astype(F32))
    ).astype(BF16)
    attn_pair = (attn_mine.astype(F32) + attn_got.astype(F32)).astype(BF16)
    attn_cols = level_sum(attn_pair)
    gate_cols = lax.dynamic_slice_in_dim(mod_gate, mp_pos * cols_dev, cols_dev, 0)
    block_out = (hidden_cols.astype(F32) + gate_cols * attn_cols).astype(BF16)
    received = tuple(shift_by(total, "slab", along_y(k)) for k in (1, 2, 3))
    total, g_two = lax.optimization_barrier((total, g_two))
    g_sum = (
        (g_parts[0].astype(F32) + g_two.astype(F32)) + (g_one.astype(F32) + g_three.astype(F32))
    ).astype(BF16)
    g_out = g_sum[0].astype(F32)
    for k in (1, 2, 3):
        g_out = g_out + shift_by(g_sum[k], "slab", along_x(k)).astype(F32)
    g_out = g_out.T
    g_qkv, g_embed = call(
        weights_kernel,
        (total, *received, own_rows),
        (
            jax.ShapeDtypeStruct((row_cols, 768), F32),
            jax.ShapeDtypeStruct((FEAT, cols_dev), F32),
        ),
        [],
        1 << 26,
        4,
        "vvvvv",
    )
    return (latents, block_out, g_qkv, g_out, g_embed)


def solution(mesh):
    in_specs = (
        P(("dp", "slab"), "mp", None),
        P("mp"),
        P("mp"),
        P("mp", None),
        P("dp"),
        P("dp", None),
        P(("dp", "slab")),
        P(),
        P(),
        P("dp"),
        P("dp"),
        P("dp"),
        P(None, "mp"),
        P(),
        P(),
        P("mp", None),
        P(("dp", "slab"), "mp"),
    )
    out_specs = (
        P(("dp", "slab"), None, None),
        P(("dp", "slab"), "mp"),
        P(("dp", "slab"), "mp"),
        P(("dp", "mp"), "slab"),
        P("dp", "mp"),
    )
    return jax.shard_map(body, mesh=mesh, in_specs=in_specs, out_specs=out_specs, check_vma=False)
```

time: 224 us -> 131 us (0.58)
  waiting for transfers between devices: 79 us -> 25.5 us
  matrix products: 18.7 us -> 0 us
  local copies, waits for them, and re-layouts: 20.6 us -> 5.98 us
  between operations: 14.4 us -> 1 us
  starting transfers between devices: 41.4 us -> 49.9 us
  other arithmetic: 7.65 us -> 4.75 us
  Pallas kernels: 41.3 us -> 43.7 us
    all_to_all x5 -> x2, waiting for transfers between devices: 41.1 us -> 6.86 us  [the longest x1 6.86 us: body(): lax.all_to_all(patches_sent, 'slab', split_axis=0, concat_axis=0, tiled=T...]
    ppermute x11 -> x32, starting transfers between devices: 16.2 us -> 36 us  [shift_by(): lax.ppermute(value, axis, [(i, move(i)) for i in range(lax.axis_size(axis...]
    ppermute x11 -> x32, waiting for transfers between devices: 37.4 us -> 18.6 us  [shift_by(): lax.ppermute(value, axis, [(i, move(i)) for i in range(lax.axis_size(axis...]
    dot_general x9 -> x0, matrix products: 18.7 us -> none  [the longest x2 6.83 us: nt(): lax.dot_general(a, b, (((1,), (1,)), ((), ())), preferred_element_type=F32)]
    all_to_all x5 -> x2, starting transfers between devices: 25.2 us -> 14 us  [the longest x1 7.22 us: body(): lax.all_to_all(patches_sent, 'slab', split_axis=0, concat_axis=0, tiled=T...]
    reshape x6 -> x0, local copies, waits for them, and re-layouts: 5.26 us -> none  [the longest x1 1.33 us: body(): attn_part.reshape(ROWS, mp_size, cols_dev).transpose(1, 0, 2)]
    unnamed x47 -> x37, local copies, waits for them, and re-layouts: 7.65 us -> 3.66 us
    reduce_sum x4 -> x0, other arithmetic: 3.76 us -> none  [the longest x1 1.66 us: body(): attn_cols = jnp.sum(attn_got.astype(F32), axis=0)]
  transfers between devices with their start and end apart: 17 -> 34, of which waited for: 12 -> 11; matrix products, arithmetic and copies ran while one was open for 15% -> 4% of each run, Pallas kernels for 1% -> 21%
where the time goes in v2:
time: 131 us
  starting transfers between devices  49.9 us (38%)
  Pallas kernels  43.7 us (33%)
  waiting for transfers between devices  25.5 us (19%)
  local copies, waits for them, and re-layouts  5.98 us (5%)
  other arithmetic  4.75 us (4%)
    pallas_call x8, Pallas kernels, call(): pl.pallas_call(wrapped, out_shape=outs, in_specs=[specs[p] for p in place...  43.7 us
    ppermute x32, starting transfers between devices, shift_by(): lax.ppermute(value, axis, [(i, move(i)) for i in range(lax.axis_size(axis...  36 us
    ppermute x32, waiting for transfers between devices, shift_by(): lax.ppermute(value, axis, [(i, move(i)) for i in range(lax.axis_size(axis...  18.6 us
    all_to_all x1, starting transfers between devices, body(): lax.all_to_all(patches_sent, 'slab', split_axis=0, concat_axis=0, tiled=T...  7.22 us
    all_to_all x1, waiting for transfers between devices, body(): lax.all_to_all(patches_sent, 'slab', split_axis=0, concat_axis=0, tiled=T...  6.86 us
    all_to_all x1, starting transfers between devices, body(): lax.all_to_all(all_sent, 'slab', split_axis=0, concat_axis=0, tiled=True)  6.74 us
    unnamed x37, local copies, waits for them, and re-layouts  3.66 us
  transfers between devices with their start and end apart: 34, of which 11 were waited for; matrix products, arithmetic and copies ran while one was open for 4% of the time, Pallas kernels for 21%

profile of v2, /device:TPU:0, one launch (start us, length us, event | category | flops | bytes accessed | tf_op | source)
XLA Modules:
  0.0 130.8 jit_solution(1226164270713502514)
XLA Ops:
  0.6 0.8 slice.39
  1.5 1.6 %collective-permute-start = (bf16[2,64,256]{2,1,0:T(8,128)(2,1)S(1)}, bf16[2,64,256]{2,1,0:T(8,128)(2,1)S(1)}, u32[]{:S(2)}, u32[]{:S(2)}) collective-permute-start(bf16[2,64,256]{2,1,0:T(8,128)(2,1)S(1)} %slice.39), channel_id=1, source_target_pairs={{0,8},{8,16},{16,24},{24,32},{32,40},{40,48},{48,56},{56,64},{64,7... | collective-permute-start | bytes 196616 | tf_op jit(solution)/shard_map/ppermute | solution.py:614
  3.1 0.8 copy.22
  4.4 1.8 %shard_map.200 = f32[16,8,128]{2,1,0:T(8,128)} custom-call(s32[4]{0:T(128)} %refs_0_.8, s32[8,128]{1,0:T(8,128)} %pad.9.refs_1_, bf16[4,64,256]{2,1,0:T(8,128)(2,1)} %refs_2_.3, s32[2,128]{1,0:T(2,128)} %bitcast.45), custom_call_target="tpu_custom_call" | custom-call | flops 1048576 | bytes 1048576 | tf_op jit(solution)/shard_map/pallas_call | solution.py:598
  6.2 6.7 %all-to-all-start = ((f32[16,8,128]{2,1,0:T(8,128)}), f32[16,8,128]{2,1,0:T(8,128)S(1)}, u32[]{:S(2)}, u32[]{:S(2)}) async-start(f32[16,8,128]{2,1,0:T(8,128)} %shard_map.200), calls=%async_computation | async-start | bytes 131072 | tf_op jit(solution)/shard_map/all_to_all | solution.py:675
  13.0 2.0 %collective-permute-start.1 = (bf16[256,384]{1,0:T(8,128)(2,1)}, bf16[256,384]{1,0:T(8,128)(2,1)S(1)}, u32[]{:S(2)}, u32[]{:S(2)}) collective-permute-start(bf16[256,384]{1,0:T(8,128)(2,1)} %refs_12_.1), channel_id=1, source_target_pairs={{0,2},{1,3},{2,4},{3,5},{4,6},{5,7},{6,0},{7,1},{8,10},{9,11},{10,... | collective-permute-start | bytes 589832 | tf_op jit(solution)/shard_map/ppermute | solution.py:614
  15.0 3.6 %collective-permute-start.2 = (bf16[256,384]{1,0:T(8,128)(2,1)}, bf16[256,384]{1,0:T(8,128)(2,1)S(1)}, u32[]{:S(2)}, u32[]{:S(2)}) collective-permute-start(bf16[256,384]{1,0:T(8,128)(2,1)} %refs_12_.1), channel_id=1, source_target_pairs={{0,4},{1,5},{2,6},{3,7},{4,0},{5,1},{6,2},{7,3},{8,12},{9,13},{10,... | collective-permute-start | bytes 589832 | tf_op jit(solution)/shard_map/ppermute | solution.py:614
  18.6 1.0 collective-permute-start.3
  19.6 5.6 %shard_map.201 = (bf16[80,80]{1,0:T(8,128)(2,1)}, bf16[80,80]{1,0:T(8,128)(2,1)}, bf16[768,80]{1,0:T(8,128)(2,1)}, bf16[768,80]{1,0:T(8,128)(2,1)}, bf16[256,240...) custom-call(bf16[64,3072]{1,0:T(8,128)(2,1)} %refs_15_.2, f32[1,3072]{1,0:T(1,128)} %bitcast.48, ...), custom_call_target="tpu_custom_call" | custom-call | flops 8589934592 | bytes 1048576 | tf_op jit(solution)/shard_map/pallas_call | solution.py:598
  25.8 3.0 %shard_map.202 = bf16[64,256]{1,0:T(8,128)(2,1)} custom-call(s32[4]{0:T(128)} %refs_0_.8, s32[8,128]{1,0:T(8,128)} %pad.9.refs_1_, bf16[4,64,256]{2,1,0:T(8,128)(2,1)} %refs_2_.3, bf16[2,64,256]{2,1,0:T(8,128)(2,1)} %copy-done.17, f32[16,8,128]{2,1,0:T(8,128)} %copy-done.7, f32[1,64]{1,0:T(1,128)} %bitcast.52, f32[1,64]{1,0:T(1,128)} %bitcast.53, ...), custom_call_target="tpu_custom_call" | custom-call | flops 268435456 | bytes 1048576 | tf_op jit(solution)/shard_map/pallas_call | solution.py:598
  28.9 1.4 %collective-permute-done.4 = bf16[64,256]{1,0:T(8,128)(2,1)S(1)} collective-permute-done((bf16[64,256]{1,0:T(8,128)(2,1)}, bf16[64,256]{1,0:T(8,128)(2,1)S(1)}, u32[]{:S(2)}, u32[]{:S(2)}) %collective-permute-start.4) | collective-permute-done | bytes 32800 | tf_op jit(solution)/shard_map/ppermute | solution.py:614
  30.3 0.8 add_convert_fusion.4.refs_0_
  31.1 1.1 collective-permute-start.5
  32.2 0.7 collective-permute-start.6
  32.9 2.0 %collective-permute-start.7 = (bf16[64,256]{1,0:T(8,128)(2,1)S(1)}, bf16[64,256]{1,0:T(8,128)(2,1)S(1)}, u32[]{:S(2)}, u32[]{:S(2)}) collective-permute-start(bf16[64,256]{1,0:T(8,128)(2,1)S(1)} %add_convert_fusion.4.refs_0_), channel_id=1, source_target_pairs={{0,6},{1,7},{2,0},{3,1},{4,2},{5,3},{6,4},{7,5},{8,14},{9,15},{10,... | collective-permute-start | bytes 98312 | tf_op jit(solution)/shard_map/ppermute | solution.py:614
  34.9 1.7 %collective-permute-done.5.refs_1_ = bf16[64,256]{1,0:T(8,128)(2,1)S(1)} collective-permute-done((bf16[64,256]{1,0:T(8,128)(2,1)S(1)}, bf16[64,256]{1,0:T(8,128)(2,1)S(1)}, u32[]{:S(2)}, u32[]{:S(2)}) %collective-permute-start.5) | collective-permute-done | bytes 32800 | tf_op jit(solution)/shard_map/ppermute | solution.py:614
  36.6 1.0 collective-permute-done.6.refs_2_
  37.6 0.9 shard_map.203
  38.5 0.6 copy-done.1
  40.1 7.2 %all-to-all-start.1 = ((bf16[16,64,256]{2,1,0:T(8,128)(2,1)}), bf16[16,64,256]{2,1,0:T(8,128)(2,1)S(1)}, u32[]{:S(2)}, u32[]{:S(2)}) async-start(bf16[16,64,256]{2,1,0:T(8,128)(2,1)} %get-tuple-element.81), calls=%async_computation.1 | async-start | bytes 1048576 | tf_op jit(solution)/shard_map/all_to_all | solution.py:721
  48.3 3.9 %shard_map.204 = (bf16[8,256,384]{2,1,0:T(8,128)(2,1)}, bf16[256,256]{1,0:T(8,128)(2,1)}, f32[4,16,256]{2,1,0:T(8,128)}) custom-call(bf16[256,384]{1,0:T(8,128)(2,1)} %refs_12_.1, bf16[256,384]{1,0:T(8,128)(2,1)} %copy-done.10, bf16[256,384]{1,0:T(8,128)(2,1)} %copy-done.11, bf16[256,384]{1,0:T(8,128)(2,1)} %copy-done.12, bf16[256,384]{1,0:T(8,128)(2,1)} %copy-done.13, ...), custom_call_target="tpu_custom_call" | custom-call | flops 4294967296 | bytes 1048576 | tf_op jit(solution)/shard_map/pallas_call | solution.py:598
  52.2 6.9 %all-to-all-done.1.refs_2_ = bf16[16,64,256]{2,1,0:T(8,128)(2,1)S(1)} async-done(((bf16[16,64,256]{2,1,0:T(8,128)(2,1)}), bf16[16,64,256]{2,1,0:T(8,128)(2,1)S(1)}, u32[]{:S(2)}, u32[]{:S(2)}) %all-to-all-start.1) | async-done | bytes 524320 | tf_op jit(solution)/shard_map/all_to_all | solution.py:721
  59.0 0.8 copy-done.3
  59.8 14.2 %shard_map.205 = (bf16[4,256,384]{2,1,0:T(8,128)(2,1)}, bf16[4,256,384]{2,1,0:T(8,128)(2,1)}, bf16[4,192,256]{2,1,0:T(8,128)(2,1)}, bf16[4,192,256]{2,1,0:T(8,12...) custom-call(s32[4]{0:T(128)} %refs_0_.8, ...), custom_call_target="tpu_custom_call" | custom-call | flops 8589934592 | bytes 1048576 | tf_op jit(solution)/shard_map/pallas_call | solution.py:598
  74.1 3.2 %collective-permute-start.13 = (bf16[4,192,256]{2,1,0:T(8,128)(2,1)}, bf16[4,192,256]{2,1,0:T(8,128)(2,1)S(1)}, u32[]{:S(2)}, u32[]{:S(2)}) collective-permute-start(bf16[4,192,256]{2,1,0:T(8,128)(2,1)} %get-tuple-element.104), channel_id=1, source_target_pairs={{0,96},{8,104},{16,112},{24,120},{32,0},{40,8},{48,16},{56,24},{64... | collective-permute-start | bytes 1179656 | tf_op jit(solution)/shard_map/ppermute | solution.py:614
  77.4 13.3 %shard_map.206 = (bf16[80,768]{1,0:T(8,128)(2,1)}, bf16[4,64,384]{2,1,0:T(8,128)(2,1)}, bf16[4,64,384]{2,1,0:T(8,128)(2,1)}) custom-call(bf16[160,4096]{1,0:T(8,128)(2,1)} %get-tuple-element.90.refs_0_, bf16[2,144,4096]{2,1,0:T(8,128)(2,1)} %get-tuple-element.91.refs_1_, f32[2,8,4096]{2,1,0:T(8,128)} %get-tuple-element.92.refs_2_, ...), custom_call_target="tpu_custom_call" | custom-call | flops 17179869184 | bytes 1048576 | tf_op jit(solution)/shard_map/pallas_call | solution.py:598
  91.3 1.3 collective-permute-done.15
  92.6 1.0 add_convert_fusion.2
  93.6 2.7 %collective-permute-start.18 = (bf16[64,384]{1,0:T(8,128)(2,1)S(1)}, bf16[64,384]{1,0:T(8,128)(2,1)S(1)}, u32[]{:S(2)}, u32[]{:S(2)}) collective-permute-start(bf16[64,384]{1,0:T(8,128)(2,1)S(1)} %get-tuple-element.130), channel_id=1, source_target_pairs={{0,6},{1,7},{2,0},{3,1},{4,2},{5,3},{6,4},{7,5},{8,14},{9,15},{10,... | collective-permute-start | bytes 147464 | tf_op jit(solution)/shard_map/ppermute | solution.py:614
  96.3 1.5 %collective-permute-start.16 = (bf16[64,384]{1,0:T(8,128)(2,1)S(1)}, bf16[64,384]{1,0:T(8,128)(2,1)S(1)}, u32[]{:S(2)}, u32[]{:S(2)}) collective-permute-start(bf16[64,384]{1,0:T(8,128)(2,1)S(1)} %get-tuple-element.129), channel_id=1, source_target_pairs={{0,4},{1,5},{2,6},{3,7},{4,0},{5,1},{6,2},{7,3},{8,12},{9,13},{10,... | collective-permute-start | bytes 147464 | tf_op jit(solution)/shard_map/ppermute | solution.py:614
  97.8 0.8 dynamic_slice.3
  98.6 3.7 %collective-permute-done.17 = bf16[64,384]{1,0:T(8,128)(2,1)S(1)} collective-permute-done((bf16[64,384]{1,0:T(8,128)(2,1)S(1)}, bf16[64,384]{1,0:T(8,128)(2,1)S(1)}, u32[]{:S(2)}, u32[]{:S(2)}) %collective-permute-start.17) | collective-permute-done | bytes 49184 | tf_op jit(solution)/shard_map/ppermute | solution.py:614
  102.3 0.9 fusion.8
  103.8 1.5 %collective-permute-start.23 = (bf16[80,1152]{1,0:T(8,128)(2,1)S(1)}, bf16[80,1152]{1,0:T(8,128)(2,1)S(1)}, u32[]{:S(2)}, u32[]{:S(2)}) collective-permute-start(bf16[80,1152]{1,0:T(8,128)(2,1)S(1)} %fusion.8), channel_id=1, source_target_pairs={{0,8},{8,16},{16,24},{24,0},{32,40},{40,48},{48,56},{56,32},{64,72... | collective-permute-start | bytes 552968 | tf_op jit(solution)/shard_map/ppermute | solution.py:614
  105.3 0.8 collective-permute-start.22
  106.4 2.9 %collective-permute-start.21 = (bf16[256,384]{1,0:T(8,128)(2,1)S(1)}, bf16[256,384]{1,0:T(8,128)(2,1)S(1)}, u32[]{:S(2)}, u32[]{:S(2)}) collective-permute-start(bf16[256,384]{1,0:T(8,128)(2,1)S(1)} %get-tuple-element.124), channel_id=1, source_target_pairs={{0,6},{1,7},{2,0},{3,1},{4,2},{5,3},{6,4},{7,5},{8,14},{9,15},{10,... | collective-permute-start | bytes 589832 | tf_op jit(solution)/shard_map/ppermute | solution.py:614
  109.3 1.5 %collective-permute-done.24 = bf16[80,1152]{1,0:T(8,128)(2,1)S(1)} collective-permute-done((bf16[80,1152]{1,0:T(8,128)(2,1)S(1)}, bf16[80,1152]{1,0:T(8,128)(2,1)S(1)}, u32[]{:S(2)}, u32[]{:S(2)}) %collective-permute-start.24) | collective-permute-done | bytes 184352 | tf_op jit(solution)/shard_map/ppermute | solution.py:614
  111.1 3.3 %collective-permute-done.23 = bf16[80,1152]{1,0:T(8,128)(2,1)S(1)} collective-permute-done((bf16[80,1152]{1,0:T(8,128)(2,1)S(1)}, bf16[80,1152]{1,0:T(8,128)(2,1)S(1)}, u32[]{:S(2)}, u32[]{:S(2)}) %collective-permute-start.23) | collective-permute-done | bytes 184352 | tf_op jit(solution)/shard_map/ppermute | solution.py:614
  114.5 0.8 collective-permute-start.19
  115.5 1.5 %collective-permute-start.27 = (bf16[80,1152]{1,0:T(8,128)(2,1)S(1)}, bf16[80,1152]{1,0:T(8,128)(2,1)S(1)}, u32[]{:S(2)}, u32[]{:S(2)}) collective-permute-start(bf16[80,1152]{1,0:T(8,128)(2,1)S(1)} %add_convert_fusion.3.refs_0_), channel_id=1, source_target_pairs={{0,64},{8,72},{16,80},{24,88},{32,96},{40,104},{48,112},{56,120},{... | collective-permute-start | bytes 552968 | tf_op jit(solution)/shard_map/ppermute | solution.py:614
  117.2 1.2 collective-permute-start.31
  118.4 3.2 %collective-permute-start.30 = (bf16[192,256]{1,0:T(8,128)(2,1)S(1)}, bf16[192,256]{1,0:T(8,128)(2,1)S(1)}, u32[]{:S(2)}, u32[]{:S(2)}) collective-permute-start(bf16[192,256]{1,0:T(8,128)(2,1)S(1)} %get-tuple-element.128), channel_id=1, source_target_pairs={{0,16},{8,24},{16,0},{24,8},{32,48},{40,56},{48,32},{56,40},{64,80... | collective-permute-start | bytes 294920 | tf_op jit(solution)/shard_map/ppermute | solution.py:614
  121.7 1.7 %collective-permute-start.29 = (bf16[192,256]{1,0:T(8,128)(2,1)S(1)}, bf16[192,256]{1,0:T(8,128)(2,1)S(1)}, u32[]{:S(2)}, u32[]{:S(2)}) collective-permute-start(bf16[192,256]{1,0:T(8,128)(2,1)S(1)} %get-tuple-element.126), channel_id=1, source_target_pairs={{0,8},{8,16},{16,24},{24,0},{32,40},{40,48},{48,56},{56,32},{64,72... | collective-permute-start | bytes 294920 | tf_op jit(solution)/shard_map/ppermute | solution.py:614
  123.4 0.8 fusion.3
  124.6 3.0 %collective-permute-done.29 = bf16[192,256]{1,0:T(8,128)(2,1)S(1)} collective-permute-done((bf16[192,256]{1,0:T(8,128)(2,1)S(1)}, bf16[192,256]{1,0:T(8,128)(2,1)S(1)}, u32[]{:S(2)}, u32[]{:S(2)}) %collective-permute-start.29) | collective-permute-done | bytes 98336 | tf_op jit(solution)/shard_map/ppermute | solution.py:614
  127.5 0.7 fusion.7
  128.3 1.5 %collective-permute-done.28.refs_3_ = bf16[80,1152]{1,0:T(8,128)(2,1)S(1)} collective-permute-done((bf16[80,1152]{1,0:T(8,128)(2,1)S(1)}, bf16[80,1152]{1,0:T(8,128)(2,1)S(1)}, u32[]{:S(2)}, u32[]{:S(2)}) %collective-permute-start.28) | collective-permute-done | bytes 184352 | tf_op jit(solution)/shard_map/ppermute | solution.py:614
  129.7 1.1 shard_map.207
  (80 shorter events, 5.8 us)
Async XLA Ops:
  1.5 11.5 %collective-permute-start = (bf16[2,64,256]{2,1,0:T(8,128)(2,1)S(1)}, bf16[2,64,256]{2,1,0:T(8,128)(2,1)S(1)}, u32[]{:S(2)}, u32[]{:S(2)}) collective-permute-start(bf16[2,64,256]{2,1,0:T(8,128)(2,1)S(1)} %slice.39), channel_id=1, source_target_pairs={{0,8},{8,16},{16,24},{24,32},{32,40},{40,48},{48,56},{56,64},{64,7... | collective-permute-start | bytes 196616 | tf_op jit(solution)/shard_map/ppermute | solution.py:614
  6.2 19.0 %all-to-all-start = ((f32[16,8,128]{2,1,0:T(8,128)}), f32[16,8,128]{2,1,0:T(8,128)S(1)}, u32[]{:S(2)}, u32[]{:S(2)}) async-start(f32[16,8,128]{2,1,0:T(8,128)} %shard_map.200), calls=%async_computation | async-start | bytes 131072 | tf_op jit(solution)/shard_map/all_to_all | solution.py:675
  13.0 12.2 %copy-start.17 = (bf16[2,64,256]{2,1,0:T(8,128)(2,1)}, bf16[2,64,256]{2,1,0:T(8,128)(2,1)S(1)}, u32[]{:S(2)}) copy-start(bf16[2,64,256]{2,1,0:T(8,128)(2,1)S(1)} %collective-permute-done.refs_3_) | copy-start | bytes 196612
  13.0 15.8 %collective-permute-start.1 = (bf16[256,384]{1,0:T(8,128)(2,1)}, bf16[256,384]{1,0:T(8,128)(2,1)S(1)}, u32[]{:S(2)}, u32[]{:S(2)}) collective-permute-start(bf16[256,384]{1,0:T(8,128)(2,1)} %refs_12_.1), channel_id=1, source_target_pairs={{0,2},{1,3},{2,4},{3,5},{4,6},{5,7},{6,0},{7,1},{8,10},{9,11},{10,... | collective-permute-start | bytes 589832 | tf_op jit(solution)/shard_map/ppermute | solution.py:614
  15.0 13.8 %collective-permute-start.2 = (bf16[256,384]{1,0:T(8,128)(2,1)}, bf16[256,384]{1,0:T(8,128)(2,1)S(1)}, u32[]{:S(2)}, u32[]{:S(2)}) collective-permute-start(bf16[256,384]{1,0:T(8,128)(2,1)} %refs_12_.1), channel_id=1, source_target_pairs={{0,4},{1,5},{2,6},{3,7},{4,0},{5,1},{6,2},{7,3},{8,12},{9,13},{10,... | collective-permute-start | bytes 589832 | tf_op jit(solution)/shard_map/ppermute | solution.py:614
  18.6 10.2 %collective-permute-start.3 = (bf16[256,384]{1,0:T(8,128)(2,1)}, bf16[256,384]{1,0:T(8,128)(2,1)S(1)}, u32[]{:S(2)}, u32[]{:S(2)}) collective-permute-start(bf16[256,384]{1,0:T(8,128)(2,1)} %refs_12_.1), channel_id=1, source_target_pairs={{0,6},{1,7},{2,0},{3,1},{4,2},{5,3},{6,4},{7,5},{8,14},{9,15},{10,... | collective-permute-start | bytes 589832 | tf_op jit(solution)/shard_map/ppermute | solution.py:614
  19.6 19.5 %copy-start.9 = (bf16[256,384]{1,0:T(8,128)(2,1)S(1)}, bf16[256,384]{1,0:T(8,128)(2,1)}, u32[]{:S(2)}) copy-start(bf16[256,384]{1,0:T(8,128)(2,1)} %refs_12_.1) | copy-start | bytes 589828
  28.8 18.6 %copy-start.10 = (bf16[256,384]{1,0:T(8,128)(2,1)}, bf16[256,384]{1,0:T(8,128)(2,1)S(1)}, u32[]{:S(2)}) copy-start(bf16[256,384]{1,0:T(8,128)(2,1)S(1)} %collective-permute-done.1.refs_1_) | copy-start | bytes 589828
  28.8 18.6 %copy-start.11 = (bf16[256,384]{1,0:T(8,128)(2,1)}, bf16[256,384]{1,0:T(8,128)(2,1)S(1)}, u32[]{:S(2)}) copy-start(bf16[256,384]{1,0:T(8,128)(2,1)S(1)} %collective-permute-done.2.refs_2_) | copy-start | bytes 589828
  28.8 18.6 %copy-start.12 = (bf16[256,384]{1,0:T(8,128)(2,1)}, bf16[256,384]{1,0:T(8,128)(2,1)S(1)}, u32[]{:S(2)}) copy-start(bf16[256,384]{1,0:T(8,128)(2,1)S(1)} %collective-permute-done.3.refs_3_) | copy-start | bytes 589828
  28.8 1.5 %collective-permute-start.4 = (bf16[64,256]{1,0:T(8,128)(2,1)}, bf16[64,256]{1,0:T(8,128)(2,1)S(1)}, u32[]{:S(2)}, u32[]{:S(2)}) collective-permute-start(bf16[64,256]{1,0:T(8,128)(2,1)} %shard_map.202), channel_id=1, source_target_pairs={{0,1},{1,0},{2,3},{3,2},{4,5},{5,4},{6,7},{7,6},{8,9},{9,8},{10,11... | collective-permute-start | bytes 98312 | tf_op jit(solution)/shard_map/ppermute | solution.py:614
  31.1 5.5 %collective-permute-start.5 = (bf16[64,256]{1,0:T(8,128)(2,1)S(1)}, bf16[64,256]{1,0:T(8,128)(2,1)S(1)}, u32[]{:S(2)}, u32[]{:S(2)}) collective-permute-start(bf16[64,256]{1,0:T(8,128)(2,1)S(1)} %add_convert_fusion.4.refs_0_), channel_id=1, source_target_pairs={{0,2},{1,3},{2,4},{3,5},{4,6},{5,7},{6,0},{7,1},{8,10},{9,11},{10,... | collective-permute-start | bytes 98312 | tf_op jit(solution)/shard_map/ppermute | solution.py:614
  32.2 5.4 %collective-permute-start.6 = (bf16[64,256]{1,0:T(8,128)(2,1)S(1)}, bf16[64,256]{1,0:T(8,128)(2,1)S(1)}, u32[]{:S(2)}, u32[]{:S(2)}) collective-permute-start(bf16[64,256]{1,0:T(8,128)(2,1)S(1)} %add_convert_fusion.4.refs_0_), channel_id=1, source_target_pairs={{0,4},{1,5},{2,6},{3,7},{4,0},{5,1},{6,2},{7,3},{8,12},{9,13},{10,... | collective-permute-start | bytes 98312 | tf_op jit(solution)/shard_map/ppermute | solution.py:614
  32.9 4.7 %collective-permute-start.7 = (bf16[64,256]{1,0:T(8,128)(2,1)S(1)}, bf16[64,256]{1,0:T(8,128)(2,1)S(1)}, u32[]{:S(2)}, u32[]{:S(2)}) collective-permute-start(bf16[64,256]{1,0:T(8,128)(2,1)S(1)} %add_convert_fusion.4.refs_0_), channel_id=1, source_target_pairs={{0,6},{1,7},{2,0},{3,1},{4,2},{5,3},{6,4},{7,5},{8,14},{9,15},{10,... | collective-permute-start | bytes 98312 | tf_op jit(solution)/shard_map/ppermute | solution.py:614
  39.1 8.3 %collective-permute-start.8 = (bf16[256,384]{1,0:T(8,128)(2,1)S(1)}, bf16[256,384]{1,0:T(8,128)(2,1)S(1)}, u32[]{:S(2)}, u32[]{:S(2)}) collective-permute-start(bf16[256,384]{1,0:T(8,128)(2,1)S(1)} %copy-done.9), channel_id=1, source_target_pairs={{0,1},{1,0},{2,3},{3,2},{4,5},{5,4},{6,7},{7,6},{8,9},{9,8},{10,11... | collective-permute-start | bytes 589832 | tf_op jit(solution)/shard_map/ppermute | solution.py:614
  39.1 8.3 %collective-permute-start.9 = (bf16[256,384]{1,0:T(8,128)(2,1)S(1)}, bf16[256,384]{1,0:T(8,128)(2,1)S(1)}, u32[]{:S(2)}, u32[]{:S(2)}) collective-permute-start(bf16[256,384]{1,0:T(8,128)(2,1)S(1)} %collective-permute-done.1.refs_1_), channel_id=1, source_target_pairs={{0,1},{1,0},{2,3},{3,2},{4,5},{5,4},{6,7},{7,6},{8,9},{9,8},{10,11... | collective-permute-start | bytes 589832 | tf_op jit(solution)/shard_map/ppermute | solution.py:614
  39.6 7.8 %collective-permute-start.10 = (bf16[256,384]{1,0:T(8,128)(2,1)S(1)}, bf16[256,384]{1,0:T(8,128)(2,1)S(1)}, u32[]{:S(2)}, u32[]{:S(2)}) collective-permute-start(bf16[256,384]{1,0:T(8,128)(2,1)S(1)} %collective-permute-done.2.refs_2_), channel_id=1, source_target_pairs={{0,1},{1,0},{2,3},{3,2},{4,5},{5,4},{6,7},{7,6},{8,9},{9,8},{10,11... | collective-permute-start | bytes 589832 | tf_op jit(solution)/shard_map/ppermute | solution.py:614
  39.6 7.8 %collective-permute-start.11 = (bf16[256,384]{1,0:T(8,128)(2,1)S(1)}, bf16[256,384]{1,0:T(8,128)(2,1)S(1)}, u32[]{:S(2)}, u32[]{:S(2)}) collective-permute-start(bf16[256,384]{1,0:T(8,128)(2,1)S(1)} %collective-permute-done.3.refs_3_), channel_id=1, source_target_pairs={{0,1},{1,0},{2,3},{3,2},{4,5},{5,4},{6,7},{7,6},{8,9},{9,8},{10,11... | collective-permute-start | bytes 589832 | tf_op jit(solution)/shard_map/ppermute | solution.py:614
  40.1 18.9 %all-to-all-start.1 = ((bf16[16,64,256]{2,1,0:T(8,128)(2,1)}), bf16[16,64,256]{2,1,0:T(8,128)(2,1)S(1)}, u32[]{:S(2)}, u32[]{:S(2)}) async-start(bf16[16,64,256]{2,1,0:T(8,128)(2,1)} %get-tuple-element.81), calls=%async_computation.1 | async-start | bytes 1048576 | tf_op jit(solution)/shard_map/all_to_all | solution.py:721
  47.4 0.8 copy-start.15
  47.4 0.9 copy-start.16
  59.0 0.8 copy-start.3
  74.0 16.7 %collective-permute-start.12 = (bf16[4,192,256]{2,1,0:T(8,128)(2,1)}, bf16[4,192,256]{2,1,0:T(8,128)(2,1)S(1)}, u32[]{:S(2)}, u32[]{:S(2)}) collective-permute-start(bf16[4,192,256]{2,1,0:T(8,128)(2,1)} %get-tuple-element.103), channel_id=1, source_target_pairs={{0,32},{8,40},{16,48},{24,56},{32,64},{40,72},{48,80},{56,88},{64,... | collective-permute-start | bytes 1179656 | tf_op jit(solution)/shard_map/ppermute | solution.py:614
  74.1 16.6 %collective-permute-start.13 = (bf16[4,192,256]{2,1,0:T(8,128)(2,1)}, bf16[4,192,256]{2,1,0:T(8,128)(2,1)S(1)}, u32[]{:S(2)}, u32[]{:S(2)}) collective-permute-start(bf16[4,192,256]{2,1,0:T(8,128)(2,1)} %get-tuple-element.104), channel_id=1, source_target_pairs={{0,96},{8,104},{16,112},{24,120},{32,0},{40,8},{48,16},{56,24},{64... | collective-permute-start | bytes 1179656 | tf_op jit(solution)/shard_map/ppermute | solution.py:614
  77.3 13.4 %collective-permute-start.14 = (bf16[4,256,384]{2,1,0:T(8,128)(2,1)}, bf16[4,256,384]{2,1,0:T(8,128)(2,1)S(1)}, u32[]{:S(2)}, u32[]{:S(2)}) collective-permute-start(bf16[4,256,384]{2,1,0:T(8,128)(2,1)} %get-tuple-element.105), channel_id=1, source_target_pairs={{0,1},{1,0},{2,3},{3,2},{4,5},{5,4},{6,7},{7,6},{8,9},{9,8},{10,11... | collective-permute-start | bytes 2359304 | tf_op jit(solution)/shard_map/ppermute | solution.py:614
  77.3 21.2 %copy-start.8 = (bf16[4,192,256]{2,1,0:T(8,128)(2,1)S(1)}, bf16[4,192,256]{2,1,0:T(8,128)(2,1)}, u32[]{:S(2)}) copy-start(bf16[4,192,256]{2,1,0:T(8,128)(2,1)} %get-tuple-element.114) | copy-start | bytes 1179652
  77.4 24.9 %copy-start.6 = (f32[64,384]{1,0:T(8,128)S(1)}, f32[64,384]{1,0:T(8,128)}, u32[]{:S(2)}) copy-start(f32[64,384]{1,0:T(8,128)} %get-tuple-element.109) | copy-start | bytes 294916
  90.7 15.4 %copy-start.2 = (bf16[4,256,384]{2,1,0:T(8,128)(2,1)S(1)}, bf16[4,256,384]{2,1,0:T(8,128)(2,1)}, u32[]{:S(2)}) copy-start(bf16[4,256,384]{2,1,0:T(8,128)(2,1)} %get-tuple-element.111) | copy-start | bytes 2359300
  90.7 1.9 %collective-permute-start.15 = (bf16[4,64,384]{2,1,0:T(8,128)(2,1)}, bf16[4,64,384]{2,1,0:T(8,128)(2,1)S(1)}, u32[]{:S(2)}, u32[]{:S(2)}) collective-permute-start(bf16[4,64,384]{2,1,0:T(8,128)(2,1)} %get-tuple-element.108), channel_id=1, source_target_pairs={{0,1},{1,0},{2,3},{3,2},{4,5},{5,4},{6,7},{7,6},{8,9},{9,8},{10,11... | collective-permute-start | bytes 589832 | tf_op jit(solution)/shard_map/ppermute | solution.py:614
  93.6 5.0 %collective-permute-start.18 = (bf16[64,384]{1,0:T(8,128)(2,1)S(1)}, bf16[64,384]{1,0:T(8,128)(2,1)S(1)}, u32[]{:S(2)}, u32[]{:S(2)}) collective-permute-start(bf16[64,384]{1,0:T(8,128)(2,1)S(1)} %get-tuple-element.130), channel_id=1, source_target_pairs={{0,6},{1,7},{2,0},{3,1},{4,2},{5,3},{6,4},{7,5},{8,14},{9,15},{10,... | collective-permute-start | bytes 147464 | tf_op jit(solution)/shard_map/ppermute | solution.py:614
  96.2 6.0 %collective-permute-start.17 = (bf16[64,384]{1,0:T(8,128)(2,1)S(1)}, bf16[64,384]{1,0:T(8,128)(2,1)S(1)}, u32[]{:S(2)}, u32[]{:S(2)}) collective-permute-start(bf16[64,384]{1,0:T(8,128)(2,1)S(1)} %get-tuple-element.131), channel_id=1, source_target_pairs={{0,2},{1,3},{2,4},{3,5},{4,6},{5,7},{6,0},{7,1},{8,10},{9,11},{10,... | collective-permute-start | bytes 147464 | tf_op jit(solution)/shard_map/ppermute | solution.py:614
  96.3 6.0 %collective-permute-start.16 = (bf16[64,384]{1,0:T(8,128)(2,1)S(1)}, bf16[64,384]{1,0:T(8,128)(2,1)S(1)}, u32[]{:S(2)}, u32[]{:S(2)}) collective-permute-start(bf16[64,384]{1,0:T(8,128)(2,1)S(1)} %get-tuple-element.129), channel_id=1, source_target_pairs={{0,4},{1,5},{2,6},{3,7},{4,0},{5,1},{6,2},{7,3},{8,12},{9,13},{10,... | collective-permute-start | bytes 147464 | tf_op jit(solution)/shard_map/ppermute | solution.py:614
  98.6 16.9 %collective-permute-start.25 = (bf16[4,192,256]{2,1,0:T(8,128)(2,1)S(1)}, bf16[4,192,256]{2,1,0:T(8,128)(2,1)S(1)}, u32[]{:S(2)}, u32[]{:S(2)}) collective-permute-start(bf16[4,192,256]{2,1,0:T(8,128)(2,1)S(1)} %copy-done.8), channel_id=1, source_target_pairs={{0,64},{8,72},{16,80},{24,88},{32,96},{40,104},{48,112},{56,120},{... | collective-permute-start | bytes 1179656 | tf_op jit(solution)/shard_map/ppermute | solution.py:614
  103.2 7.6 %collective-permute-start.24 = (bf16[80,1152]{1,0:T(8,128)(2,1)S(1)}, bf16[80,1152]{1,0:T(8,128)(2,1)S(1)}, u32[]{:S(2)}, u32[]{:S(2)}) collective-permute-start(bf16[80,1152]{1,0:T(8,128)(2,1)S(1)} %fusion.8), channel_id=1, source_target_pairs={{0,24},{8,0},{16,8},{24,16},{32,56},{40,32},{48,40},{56,48},{64,88... | collective-permute-start | bytes 552968 | tf_op jit(solution)/shard_map/ppermute | solution.py:614
  103.8 10.7 %collective-permute-start.23 = (bf16[80,1152]{1,0:T(8,128)(2,1)S(1)}, bf16[80,1152]{1,0:T(8,128)(2,1)S(1)}, u32[]{:S(2)}, u32[]{:S(2)}) collective-permute-start(bf16[80,1152]{1,0:T(8,128)(2,1)S(1)} %fusion.8), channel_id=1, source_target_pairs={{0,8},{8,16},{16,24},{24,0},{32,40},{40,48},{48,56},{56,32},{64,72... | collective-permute-start | bytes 552968 | tf_op jit(solution)/shard_map/ppermute | solution.py:614
  105.3 10.0 %collective-permute-start.22 = (bf16[80,1152]{1,0:T(8,128)(2,1)S(1)}, bf16[80,1152]{1,0:T(8,128)(2,1)S(1)}, u32[]{:S(2)}, u32[]{:S(2)}) collective-permute-start(bf16[80,1152]{1,0:T(8,128)(2,1)S(1)} %fusion.8), channel_id=1, source_target_pairs={{0,16},{8,24},{16,0},{24,8},{32,48},{40,56},{48,32},{56,40},{64,80... | collective-permute-start | bytes 552968 | tf_op jit(solution)/shard_map/ppermute | solution.py:614
  106.3 10.6 %copy-start.4 = (bf16[4,192,256]{2,1,0:T(8,128)(2,1)S(1)}, bf16[4,192,256]{2,1,0:T(8,128)(2,1)}, u32[]{:S(2)}) copy-start(bf16[4,192,256]{2,1,0:T(8,128)(2,1)} %get-tuple-element.118) | copy-start | bytes 1179652
  106.4 10.8 %collective-permute-start.21 = (bf16[256,384]{1,0:T(8,128)(2,1)S(1)}, bf16[256,384]{1,0:T(8,128)(2,1)S(1)}, u32[]{:S(2)}, u32[]{:S(2)}) collective-permute-start(bf16[256,384]{1,0:T(8,128)(2,1)S(1)} %get-tuple-element.124), channel_id=1, source_target_pairs={{0,6},{1,7},{2,0},{3,1},{4,2},{5,3},{6,4},{7,5},{8,14},{9,15},{10,... | collective-permute-start | bytes 589832 | tf_op jit(solution)/shard_map/ppermute | solution.py:614
  110.8 7.6 %collective-permute-start.20 = (bf16[256,384]{1,0:T(8,128)(2,1)S(1)}, bf16[256,384]{1,0:T(8,128)(2,1)S(1)}, u32[]{:S(2)}, u32[]{:S(2)}) collective-permute-start(bf16[256,384]{1,0:T(8,128)(2,1)S(1)} %get-tuple-element.125), channel_id=1, source_target_pairs={{0,2},{1,3},{2,4},{3,5},{4,6},{5,7},{6,0},{7,1},{8,10},{9,11},{10,... | collective-permute-start | bytes 589832 | tf_op jit(solution)/shard_map/ppermute | solution.py:614
  114.5 8.9 %copy-start.5 = (bf16[256,384]{1,0:T(8,128)(2,1)S(1)}, bf16[256,384]{1,0:T(8,128)(2,1)}, u32[]{:S(2)}) copy-start(bf16[256,384]{1,0:T(8,128)(2,1)} %get-tuple-element.89) | copy-start | bytes 589828
  114.5 7.2 %collective-permute-start.19 = (bf16[256,384]{1,0:T(8,128)(2,1)S(1)}, bf16[256,384]{1,0:T(8,128)(2,1)S(1)}, u32[]{:S(2)}, u32[]{:S(2)}) collective-permute-start(bf16[256,384]{1,0:T(8,128)(2,1)S(1)} %get-tuple-element.123), channel_id=1, source_target_pairs={{0,4},{1,5},{2,6},{3,7},{4,0},{5,1},{6,2},{7,3},{8,12},{9,13},{10,... | collective-permute-start | bytes 589832 | tf_op jit(solution)/shard_map/ppermute | solution.py:614
  115.4 12.9 %collective-permute-start.26 = (bf16[80,1152]{1,0:T(8,128)(2,1)S(1)}, bf16[80,1152]{1,0:T(8,128)(2,1)S(1)}, u32[]{:S(2)}, u32[]{:S(2)}) collective-permute-start(bf16[80,1152]{1,0:T(8,128)(2,1)S(1)} %add_convert_fusion.3.refs_0_), channel_id=1, source_target_pairs={{0,32},{8,40},{16,48},{24,56},{32,64},{40,72},{48,80},{56,88},{64,... | collective-permute-start | bytes 552968 | tf_op jit(solution)/shard_map/ppermute | solution.py:614
  115.5 12.8 %collective-permute-start.27 = (bf16[80,1152]{1,0:T(8,128)(2,1)S(1)}, bf16[80,1152]{1,0:T(8,128)(2,1)S(1)}, u32[]{:S(2)}, u32[]{:S(2)}) collective-permute-start(bf16[80,1152]{1,0:T(8,128)(2,1)S(1)} %add_convert_fusion.3.refs_0_), channel_id=1, source_target_pairs={{0,64},{8,72},{16,80},{24,88},{32,96},{40,104},{48,112},{56,120},{... | collective-permute-start | bytes 552968 | tf_op jit(solution)/shard_map/ppermute | solution.py:614
  117.2 12.6 %copy-start = (bf16[192,160]{1,0:T(8,128)(2,1)S(1)}, bf16[192,160]{1,0:T(8,128)(2,1)}, u32[]{:S(2)}) copy-start(bf16[192,160]{1,0:T(8,128)(2,1)} %get-tuple-element.116.refs_4_) | copy-start | bytes 184324
  117.2 7.0 %collective-permute-start.31 = (bf16[192,256]{1,0:T(8,128)(2,1)S(1)}, bf16[192,256]{1,0:T(8,128)(2,1)S(1)}, u32[]{:S(2)}, u32[]{:S(2)}) collective-permute-start(bf16[192,256]{1,0:T(8,128)(2,1)S(1)} %get-tuple-element.127), channel_id=1, source_target_pairs={{0,24},{8,0},{16,8},{24,16},{32,56},{40,32},{48,40},{56,48},{64,88... | collective-permute-start | bytes 294920 | tf_op jit(solution)/shard_map/ppermute | solution.py:614
  118.4 6.1 %collective-permute-start.30 = (bf16[192,256]{1,0:T(8,128)(2,1)S(1)}, bf16[192,256]{1,0:T(8,128)(2,1)S(1)}, u32[]{:S(2)}, u32[]{:S(2)}) collective-permute-start(bf16[192,256]{1,0:T(8,128)(2,1)S(1)} %get-tuple-element.128), channel_id=1, source_target_pairs={{0,16},{8,24},{16,0},{24,8},{32,48},{40,56},{48,32},{56,40},{64,80... | collective-permute-start | bytes 294920 | tf_op jit(solution)/shard_map/ppermute | solution.py:614
  121.7 5.8 %collective-permute-start.29 = (bf16[192,256]{1,0:T(8,128)(2,1)S(1)}, bf16[192,256]{1,0:T(8,128)(2,1)S(1)}, u32[]{:S(2)}, u32[]{:S(2)}) collective-permute-start(bf16[192,256]{1,0:T(8,128)(2,1)S(1)} %get-tuple-element.126), channel_id=1, source_target_pairs={{0,8},{8,16},{16,24},{24,0},{32,40},{40,48},{48,56},{56,32},{64,72... | collective-permute-start | bytes 294920 | tf_op jit(solution)/shard_map/ppermute | solution.py:614
  124.2 5.5 %collective-permute-start.28 = (bf16[80,1152]{1,0:T(8,128)(2,1)S(1)}, bf16[80,1152]{1,0:T(8,128)(2,1)S(1)}, u32[]{:S(2)}, u32[]{:S(2)}) collective-permute-start(bf16[80,1152]{1,0:T(8,128)(2,1)S(1)} %add_convert_fusion.3.refs_0_), channel_id=1, source_target_pairs={{0,96},{8,104},{16,112},{24,120},{32,0},{40,8},{48,16},{56,24},{64... | collective-permute-start | bytes 552968 | tf_op jit(solution)/shard_map/ppermute | solution.py:614
  (4 other events, 2.7 us)

commit v3 on v2

--- a/solution.py
+++ b/solution.py
@@ -121,12 +121,15 @@
         out[j] = payload
 
 
+def taps_kernel(taps, out):
+    out[...] = taps[...].astype(F32).T.astype(BF16)
+
+
 def conv_kernel(frames, res, enc, rim, sums, gain, bias, taps, out, proj):
     totals = jnp.sum(sums[...], axis=0)
     lane = lax.broadcasted_iota(jnp.int32, (8, 128), 1)
     first = lax.axis_index("slab") * FRAMES
     gain_c, bias_c = column(gain[...]), column(bias[...])
-    taps_t = taps[...].astype(F32).T.astype(BF16)
     cell = lax.broadcasted_iota(jnp.int32, (1, CELLS), 1)
     row, col = cell >> 4, cell & 15
     for j in range(FRAMES + 2):
@@ -140,7 +143,7 @@
         value = rim[j] if j < 2 else enc[j - 2]
         pre = (value.astype(F32) - mean_c) * rstd_c * gain_c + bias_c
         act = jnp.where(cell_valid(height, width), pre / (1.0 + jnp.exp(-pre)), 0.0)
-        proj[j] = nn(taps_t, act.astype(BF16))
+        proj[j] = nn(taps[...], act.astype(BF16))
     results = []
     for f in range(FRAMES):
         _, start, _, _ = frame_facts(frames, res, first + f)
@@ -178,6 +181,10 @@
 def shift_row(m_hi, m_lo, part):
     unit = jnp.where(lax.broadcasted_iota(jnp.int32, (16, AUG), 1) == FEAT + 1, 1.0, 0.0).astype(BF16)
     return (nt(unit, m_hi[part, :]) + nt(unit, m_lo[part, :]))[0:1]
+
+
+def stacked(value):
+    return jnp.concatenate([value[:, i : i + 128] for i in range(0, value.shape[1], 128)], axis=0)
 
 
 def share_kernel(pair, one, two, three, out, total):
@@ -281,6 +288,7 @@
     d_attn,
     embed_w,
     embed_b,
+    gate,
     attn_mine,
     attn_other,
     g_part0,
@@ -290,8 +298,9 @@
     hidden_cols,
     early,
     g_own,
-    s_sent,
-    k_sent,
+    gate_cols,
+    s_t,
+    k_t,
     rk_t,
     q_ext,
     q_norm,
@@ -299,7 +308,6 @@
     u_cat,
     s_own,
 ):
-    s_t, k_t = s_sent.buffer, k_sent.buffer
     blocks = patches.shape[0]
     row_aug = lax.broadcasted_iota(jnp.int32, (AUG, ROWS), 0)
     row16 = lax.broadcasted_iota(jnp.int32, (16, ROWS), 0)
@@ -344,13 +352,12 @@
     x_q, clip_q = lax.fori_loop(
         0, blocks, prepare, (jnp.zeros((ROWS, AUG), F32), jnp.zeros((ROWS, 16), F32)), unroll=PREPARE_UNROLL
     )
-    s_sent.send()
-    k_sent.send()
     x_qb = x_q.astype(BF16)
     own_cols = pl.ds(pl.multiple_of(lax.axis_index("mp") * 384, 128), 384)
+    gate_cols[...] = gate[:, own_cols]
     embed_cols = nn(turn_back(), embed_w.ready()[:, own_cols]).astype(BF16)
     hidden_cols[...] = (nn(x_qb[:, :FEAT], embed_cols) + embed_b[:, own_cols]).astype(BF16)
-    g_own[...] = nn(turn_rows(AUG), tn(x_qb, grad_out.ready()[...]).astype(BF16))
+    g_own[...] = stacked(nn(turn_rows(AUG), tn(x_qb, grad_out.ready()[...]).astype(BF16)))
     gx_q = nn(x_qb, gram_hi[...]) + nn(x_qb, gram_lo[...])
     rstd_q = lax.rsqrt(jnp.sum(gx_q * x_q, axis=1, keepdims=True) + EPSILON)
     lane_aug = lax.broadcasted_iota(jnp.int32, (ROWS, AUG), 1)
@@ -399,7 +406,7 @@
     q_facts[...] = facts
     att_all = jnp.concatenate(heads, axis=1)
     place_mp, slab = lax.axis_index("mp"), lax.axis_index("slab")
-    core, level = lax.rem(place_mp, 2), lax.div(place_mp, 2)
+    core = lax.rem(place_mp, 2)
     y_pos, x_pos = lax.div(slab, 4), lax.rem(slab, 4)
     d_attn, w_out = d_attn.ready(), w_out.ready()
     for k, g_part in enumerate((g_part0, g_part1, g_part2, g_part3)):
@@ -412,15 +419,15 @@
         g_part.send()
     for side, attn_part in enumerate((attn_other, attn_mine)):
         for k in range(4):
-            m = 2 * lax.rem(level + k, 4) + (core if side == 1 else 1 - core)
+            m = 2 * k + (core if side == 1 else 1 - core)
             cols = pl.ds(pl.multiple_of(m * 384, 128), 384)
             attn_part.buffer[k] = nn(att_all, w_out[:, cols]).astype(BF16)
         attn_part.send()
 
 
 def backward_kernel(
-    s_hbm,
-    k_hbm,
+    s_t,
+    k_t,
     rk_t,
     q_ext,
     q_norm,
@@ -434,30 +441,12 @@
     early,
     mod_scale,
     centered,
-    w_hbm,
+    w_qkv,
     sums,
     y_mine,
     y_other,
     q_t,
-    w_qkv,
-    arrived,
-    s_t,
-    k_t,
-    s_sems,
-    k_sems,
 ):
-    def fetch_block(j):
-        block = pl.ds(pl.multiple_of(j * BWD_BLOCK, BWD_BLOCK), BWD_BLOCK)
-        return (
-            pltpu.make_async_copy(s_hbm.at[:, block], s_t.at[:, block], s_sems.at[j]),
-            pltpu.make_async_copy(k_hbm.at[:, :, block], k_t.at[:, :, block], k_sems.at[j]),
-        )
-
-    for j in range(4096 // BWD_BLOCK):
-        for copy in fetch_block(j):
-            copy.start()
-    fetch = pltpu.make_async_copy(w_hbm, w_qkv, arrived)
-    fetch.start()
     shift_k = []
     for h in range(HEADS):
         q_t[h] = q_ext[h, :, :HD].astype(F32).T.astype(BF16)
@@ -472,8 +461,6 @@
 
     def backward(j, carry):
         grad_qs, p_k, quad = carry
-        for copy in fetch_block(j):
-            copy.wait()
         block = pl.ds(pl.multiple_of(j * BWD_BLOCK, BWD_BLOCK), BWD_BLOCK)
         s_hi = s_t[:AUG, block]
         s_cat = jnp.concatenate([s_hi, s_hi, s_t[AUG:, block]], axis=0)
@@ -520,13 +507,17 @@
         shift_q = shift_row(m_hi, m_lo, mine)
         m2_q = m2_q + jnp.sum(dq * (qn * (1.0 / rq) - shift_q), axis=1, keepdims=True)
         pieces += [tn(s_qhi, dq.astype(BF16)), p_k[:, h * HD : (h + 1) * HD], early[:, h * HD : (h + 1) * HD]]
-    p_all = jnp.concatenate(pieces, axis=1).astype(BF16)
-    sums[...] = p_all
+    p_rows = jnp.concatenate(pieces, axis=1)
+    p_all = p_rows.astype(BF16)
+    extra = [p_rows[FEAT + i : FEAT + 1 + i, g * 128 : (g + 1) * 128] for i in range(2) for g in range(6)]
+    extra = jnp.concatenate(extra + [jnp.zeros((4, 128), F32)], axis=0)
+    sums[:384, :] = stacked(p_all[:FEAT])
+    sums[384:, :] = extra.astype(BF16)
     quad = ((quad + tn((s_q * m2_q).astype(BF16), s_qhi)) * (1.0 / D)).astype(BF16)
     turn = turn_rows(AUG)
     turned = nn(turn, p_all).astype(BF16)
     quad = nn(turn, quad).astype(BF16)
-    fetch.wait()
+    w_qkv = w_qkv.ready()
     back = nt(turned, w_qkv[...]) * (1.0 + mod_scale[...])
     back = back - jnp.mean(back, axis=1, keepdims=True)
     back = (back - nn(jnp.concatenate([quad, quad], axis=1), centered[...])).astype(BF16)
@@ -536,15 +527,129 @@
         slot = lax.rem(z - level + 4, 4)
         even = back[:, 2 * z * 384 : (2 * z + 1) * 384]
         odd = back[:, (2 * z + 1) * 384 : (2 * z + 2) * 384]
-        y_mine[slot] = jnp.where(core == 0, even, odd)
-        y_other[slot] = jnp.where(core == 0, odd, even)
+        y_mine[slot] = stacked(jnp.where(core == 0, even, odd))
+        y_other[slot] = stacked(jnp.where(core == 0, odd, even))
+
+
+def attention_kernel(
+    frames,
+    res,
+    patches,
+    place,
+    gram_hi,
+    gram_lo,
+    m_k,
+    m_hi,
+    m_lo,
+    d_out,
+    q_gain,
+    k_gain,
+    grad_out,
+    w_out,
+    d_attn,
+    embed_w,
+    embed_b,
+    gate,
+    mod_scale,
+    centered,
+    w_qkv,
+    attn_mine,
+    attn_other,
+    g_part0,
+    g_part1,
+    g_part2,
+    g_part3,
+    hidden_cols,
+    g_own,
+    gate_cols,
+    sums,
+    y_mine,
+    y_other,
+    early,
+    s_t,
+    k_t,
+    rk_t,
+    q_ext,
+    q_norm,
+    q_facts,
+    u_cat,
+    s_own,
+    q_t,
+):
+    forward_kernel(
+        frames,
+        res,
+        patches,
+        place,
+        gram_hi,
+        gram_lo,
+        m_k,
+        m_hi,
+        m_lo,
+        d_out,
+        q_gain,
+        k_gain,
+        grad_out,
+        w_out,
+        d_attn,
+        embed_w,
+        embed_b,
+        gate,
+        attn_mine,
+        attn_other,
+        g_part0,
+        g_part1,
+        g_part2,
+        g_part3,
+        hidden_cols,
+        early,
+        g_own,
+        gate_cols,
+        s_t,
+        k_t,
+        rk_t,
+        q_ext,
+        q_norm,
+        q_facts,
+        u_cat,
+        s_own,
+    )
+    backward_kernel(
+        s_t,
+        k_t,
+        rk_t,
+        q_ext,
+        q_norm,
+        q_facts,
+        u_cat,
+        s_own,
+        m_hi,
+        m_lo,
+        q_gain,
+        k_gain,
+        early,
+        mod_scale,
+        centered.ready(),
+        w_qkv,
+        sums,
+        y_mine,
+        y_other,
+        q_t,
+    )
 
 
 def weights_kernel(own, one, two, three, own_rows, g_qkv, g_embed):
     total = (own[...].astype(F32) + two[...].astype(F32)) + (one[...].astype(F32) + three[...].astype(F32))
-    p_all = total[:, :768].astype(BF16)
+    row = lax.broadcasted_iota(jnp.int32, (AUG, 128), 0)
+    blocks = []
+    for g in range(6):
+        block = jnp.concatenate([total[g * 64 : (g + 1) * 64], jnp.zeros((AUG - FEAT, 128), F32)], axis=0)
+        block = jnp.where(row == FEAT, total[384 + g : 385 + g], block)
+        blocks.append(jnp.where(row == FEAT + 1, total[390 + g : 391 + g], block))
+    p_all = jnp.concatenate(blocks, axis=1).astype(BF16)
     g_qkv[...] = nn(own_rows[...], jnp.concatenate([p_all, p_all], axis=0))
-    g_embed[...] = total[:FEAT, 768:]
+    for g in range(3):
+        g_embed[:, g * 128 : (g + 1) * 128] = total[400 + g * 64 : 464 + g * 64]
 
 
 VMEM = pl.BlockSpec(memory_space=pltpu.VMEM)
@@ -630,6 +735,9 @@
     sent = value.astype(kind)
     one, two, three = (shift_by(sent, axis, move(k)).astype(F32) for k in (1, 2, 3))
     return (sent.astype(F32) + two) + (one + three)
+
+
+Z_GROUPS = [[0, 2, 4, 6], [1, 3, 5, 7]]
 
 
 def level_sum(pair):
@@ -658,7 +766,6 @@
 ):
     slabs = lax.axis_size("slab")
     mp_size = lax.axis_size("mp")
-    mp_pos = lax.axis_index("mp")
     cols_dev = D // mp_size
     row_cols = D // slabs
 
@@ -676,7 +783,41 @@
     rim = shift_by(enc_feat[FRAMES - 2 :], "slab", lambda i: (i + 1) % slabs)
     rim, grad_sent = lax.optimization_barrier((rim, grad_out))
     grads = (grad_sent,) + tuple(shift_by(grad_sent, "mp", along_z(k)) for k in (1, 2, 3))
-    embed_late, _ = lax.optimization_barrier((embed_b, all_sent))
+    taps = call(
+        taps_kernel,
+        (conv_w,),
+        jax.ShapeDtypeStruct((432, FEAT), BF16),
+        [],
+        1 << 33,
+        60,
+        "v",
+    )
+    partial = call(
+        conv_kernel,
+        (clip_frames, clip_res, enc_feat, rim, all_stats, gn_gain[None, :], gn_bias[None, :], taps),
+        jax.ShapeDtypeStruct((FEAT, CELLS), BF16),
+        [pltpu.VMEM((FRAMES + 2, 432, CELLS), F32)],
+        1 << 28,
+        60,
+        "svvvvvvv",
+    )
+    partial, grads = lax.optimization_barrier((partial, grads))
+    pair = (partial.astype(F32) + shift_by(partial, "mp", lambda i: i ^ 1).astype(F32)).astype(BF16)
+    patches_sent, lat_sorted = call(
+        share_kernel,
+        (pair,) + tuple(shift_by(pair, "mp", along_z(k)) for k in (1, 2, 3)),
+        (
+            jax.ShapeDtypeStruct((slabs, FEAT, CELLS), BF16),
+            jax.ShapeDtypeStruct((FEAT, CELLS), F32),
+        ),
+        [],
+        1 << 20,
+        4,
+        "vvvv",
+    )
+    all_patches = lax.all_to_all(patches_sent, "slab", split_axis=0, concat_axis=0, tiled=True)
+
+    embed_late, _ = lax.optimization_barrier((embed_b, patches_sent))
     gram_hi, gram_lo, m_hi, m_lo, m_k, centered, own_rows = call(
         prepare_kernel,
         (embed_w, embed_late[None, :], mod_shift[None, :], mod_scale[None, :], w_qkv),
@@ -690,35 +831,10 @@
             jax.ShapeDtypeStruct((row_cols, 2 * AUG), BF16),
         ),
         [pltpu.VMEM((D, AUG), F32), pltpu.VMEM((D, 768), BF16), pltpu.SemaphoreType.DMA],
-        1 << 33,
+        1 << 32,
         60,
         "vvvvr",
     )
-    gain, gram_hi = lax.optimization_barrier((gn_gain, gram_hi))
-    partial = call(
-        conv_kernel,
-        (clip_frames, clip_res, enc_feat, rim, all_stats, gain[None, :], gn_bias[None, :], conv_w),
-        jax.ShapeDtypeStruct((FEAT, CELLS), BF16),
-        [pltpu.VMEM((FRAMES + 2, 432, CELLS), F32)],
-        1 << 28,
-        60,
-        "svvvvvvv",
-    )
-    partial, grads = lax.optimization_barrier((partial, grads))
-    pair = (partial.astype(F32) + shift_by(partial, "mp", lambda i: i ^ 1).astype(F32)).astype(BF16)
-    patches_sent, lat_sorted = call(
-        share_kernel,
-        (pair,) + tuple(shift_by(pair, "mp", along_z(k)) for k in (1, 2, 3)),
-        (
-            jax.ShapeDtypeStruct((slabs, FEAT, CELLS), BF16),
-            jax.ShapeDtypeStruct((FEAT, CELLS), F32),
-        ),
-        [],
-        1 << 20,
-        4,
-        "vvvv",
-    )
-    all_patches = lax.all_to_all(patches_sent, "slab", split_axis=0, concat_axis=0, tiled=True)
 
     grads, lat_sorted = lax.optimization_barrier((grads, lat_sorted))
     others = tuple(shift_by(block, "mp", lambda i: i ^ 1) for block in grads)
@@ -736,23 +852,8 @@
         "vvvvvvvvvvv",
     )
 
-    (
-        attn_mine,
-        attn_other,
-        *g_parts,
-        hidden_cols,
-        early,
-        g_own,
-        s_t,
-        k_t,
-        rk_t,
-        q_ext,
-        q_norm,
-        q_facts,
-        u_cat,
-        s_own,
-    ) = call(
-        forward_kernel,
+    attn_mine, attn_other, *g_parts, hidden_cols, g_own, gate_cols, sums, y_mine, y_other = call(
+        attention_kernel,
         (
             clip_frames,
             clip_res,
@@ -771,96 +872,67 @@
             d_attn,
             embed_w,
             embed_b[None, :],
+            mod_gate[None, :],
+            mod_scale[None, :],
+            centered,
+            w_qkv,
         ),
         (
             *(jax.ShapeDtypeStruct((4, ROWS, cols_dev), BF16),) * 2,
             *(jax.ShapeDtypeStruct((4, row_cols, HEADS * HD), BF16),) * 4,
             jax.ShapeDtypeStruct((ROWS, cols_dev), BF16),
-            jax.ShapeDtypeStruct((AUG, 256), F32),
-            jax.ShapeDtypeStruct((FEAT, cols_dev), F32),
-            jax.ShapeDtypeStruct((2 * AUG, 4096), BF16),
-            jax.ShapeDtypeStruct((HEADS, EXT, 4096), BF16),
-            jax.ShapeDtypeStruct((HEADS, 8, 4096), F32),
-            jax.ShapeDtypeStruct((HEADS, ROWS, EXT), BF16),
-            jax.ShapeDtypeStruct((HEADS, ROWS, HD), F32),
-            jax.ShapeDtypeStruct((ROWS, 128), F32),
-            jax.ShapeDtypeStruct((HEADS, ROWS, 3 * AUG), BF16),
-            jax.ShapeDtypeStruct((ROWS, AUG), F32),
-        ),
-        [],
-        1 << 33,
-        60,
-        "svvvvvvvvlvvllllv",
-        "eeeeeevvveevvvvvv",
-    )
-    attn_got = shift_by(attn_other, "mp", lambda i: i ^ 1)
-    g_one = shift_by(g_parts[1], "slab", along_y(1))
-    g_three = shift_by(g_parts[3], "slab", along_y(3))
-    sums, y_mine, y_other = call(
-        backward_kernel,
-        (
-            s_t,
-            k_t,
-            rk_t,
-            q_ext,
-            q_norm,
-            q_facts,
-            u_cat,
-            s_own,
-            m_hi,
-            m_lo,
-            q_gain[None, :],
-            k_gain[None, :],
-            early,
-            mod_scale[None, :],
-            centered,
-            w_qkv,
-        ),
-        (
-            jax.ShapeDtypeStruct((AUG, 768), BF16),
-            jax.ShapeDtypeStruct((4, FEAT, cols_dev), BF16),
-            jax.ShapeDtypeStruct((4, FEAT, cols_dev), BF16),
+            jax.ShapeDtypeStruct((192, 128), F32),
+            jax.ShapeDtypeStruct((1, cols_dev), F32),
+            jax.ShapeDtypeStruct((400, 128), BF16),
+            jax.ShapeDtypeStruct((4, 192, 128), BF16),
+            jax.ShapeDtypeStruct((4, 192, 128), BF16),
         ),
         [
-            pltpu.VMEM((HEADS, HD, ROWS), BF16),
-            pltpu.VMEM((D, 768), BF16),
-            pltpu.SemaphoreType.DMA,
+            pltpu.VMEM((AUG, 256), F32),
             pltpu.VMEM((2 * AUG, 4096), BF16),
             pltpu.VMEM((HEADS, EXT, 4096), BF16),
-            pltpu.SemaphoreType.DMA((4096 // BWD_BLOCK,)),
-            pltpu.SemaphoreType.DMA((4096 // BWD_BLOCK,)),
+            pltpu.VMEM((HEADS, 8, 4096), F32),
+            pltpu.VMEM((HEADS, ROWS, EXT), BF16),
+            pltpu.VMEM((HEADS, ROWS, HD), F32),
+            pltpu.VMEM((ROWS, 128), F32),
+            pltpu.VMEM((HEADS, ROWS, 3 * AUG), BF16),
+            pltpu.VMEM((ROWS, AUG), F32),
+            pltpu.VMEM((HEADS, HD, ROWS), BF16),
         ],
         1 << 34,
         60,
-        "rrvvvvvvvvvvvvvr",
-    )
-
-    sums, y_mine, y_other, g_one, g_three, attn_got = lax.optimization_barrier(
-        (sums, y_mine, y_other, g_one, g_three, attn_got)
-    )
+        "svvvvvvvvlvvllllvvvll",
+        "eeeeeevvvvvv",
+    )
+
     y_got = shift_by(y_other, "mp", lambda i: i ^ 1)
     y_pair = (y_mine.astype(F32) + y_got.astype(F32)).astype(BF16)
-    g_two = shift_by(g_parts[2], "slab", along_y(2))
+    y_pair, attn_other, g_parts = lax.optimization_barrier((y_pair, attn_other, g_parts))
+    attn_got = shift_by(attn_other, "mp", lambda i: i ^ 1)
+    g_one, g_two, g_three = (shift_by(g_parts[k], "slab", along_y(k)) for k in (1, 2, 3))
     embed_part = level_sum(y_pair) + g_own
-    payload = jnp.concatenate([sums, jnp.pad(embed_part, ((0, AUG - FEAT), (0, 0))).astype(BF16)], axis=1)
+    payload = jnp.concatenate([sums, embed_part.astype(BF16)], axis=0)
     payload, attn_mine = lax.optimization_barrier((payload, attn_mine))
     sent = tuple(shift_by(payload, "slab", along_x(k)) for k in (1, 2, 3))
+    sent, g_one, g_two, g_three = lax.optimization_barrier((sent, g_one, g_two, g_three))
     total = (
         (payload.astype(F32) + sent[1].astype(F32)) + (sent[0].astype(F32) + sent[2].astype(F32))
     ).astype(BF16)
     attn_pair = (attn_mine.astype(F32) + attn_got.astype(F32)).astype(BF16)
-    attn_cols = level_sum(attn_pair)
-    gate_cols = lax.dynamic_slice_in_dim(mod_gate, mp_pos * cols_dev, cols_dev, 0)
-    block_out = (hidden_cols.astype(F32) + gate_cols * attn_cols).astype(BF16)
+    attn_got = lax.all_to_all(attn_pair, "mp", split_axis=0, concat_axis=0, tiled=True, axis_index_groups=Z_GROUPS)
+    total, attn_got = lax.optimization_barrier((total, attn_got))
     received = tuple(shift_by(total, "slab", along_y(k)) for k in (1, 2, 3))
     total, g_two = lax.optimization_barrier((total, g_two))
     g_sum = (
         (g_parts[0].astype(F32) + g_two.astype(F32)) + (g_one.astype(F32) + g_three.astype(F32))
     ).astype(BF16)
-    g_out = g_sum[0].astype(F32)
-    for k in (1, 2, 3):
-        g_out = g_out + shift_by(g_sum[k], "slab", along_x(k)).astype(F32)
-    g_out = g_out.T
+    g_got = tuple(shift_by(g_sum[k], "slab", along_x(k)) for k in (1, 2, 3))
+    received, g_late = lax.optimization_barrier((received, g_sum[0]))
+    attn_cols = jnp.sum(attn_got.astype(F32), axis=0)
+    block_out = (hidden_cols.astype(F32) + gate_cols * attn_cols).astype(BF16)
+    g_out = (
+        (g_late.astype(F32) + g_got[1].astype(F32)) + (g_got[0].astype(F32) + g_got[2].astype(F32))
+    ).T
     g_qkv, g_embed = call(
         weights_kernel,
         (total, *received, own_rows),

time: 131 us -> 129 us (0.985)
  Pallas kernels: 43.7 us -> 40.2 us
  other arithmetic: 4.75 us -> 6.56 us
    ppermute x32 -> x29, waiting for transfers between devices: 18.6 us -> 25.5 us  [shift_by(): lax.ppermute(value, axis, [(i, move(i)) for i in range(lax.axis_size(axis...]
    all_to_all x1, waiting for transfers between devices: 6.86 us -> 0.01 us  [body(): lax.all_to_all(patches_sent, 'slab', split_axis=0, concat_axis=0, tiled=T...]
    ppermute x32 -> x29, starting transfers between devices: 36 us -> 31.5 us  [shift_by(): lax.ppermute(value, axis, [(i, move(i)) for i in range(lax.axis_size(axis...]
    all_to_all x0 -> x1, starting transfers between devices: none -> 3.97 us  [body(): lax.all_to_all(attn_pair, 'mp', split_axis=0, concat_axis=0, tiled=True,...]
    pallas_call x8, Pallas kernels: 43.7 us -> 40.2 us  [call(): pl.pallas_call(wrapped, out_shape=outs, in_specs=[specs[p] for p in place...]
    unnamed x37 -> x35, local copies, waits for them, and re-layouts: 3.66 us -> 3.68 us
  transfers between devices with their start and end apart: 34 -> 32, of which waited for: 11 -> 15; matrix products, arithmetic and copies ran while one was open for 4% -> 4% of each run, Pallas kernels for 21% -> 13%
where the time goes in v3:
time: 129 us; the launch traced here: 128 us
  starting transfers between devices  49.1 us (38%)
  Pallas kernels  40.2 us (31%)
  waiting for transfers between devices  26.2 us (20%)
  other arithmetic  6.56 us (5%)
  local copies, waits for them, and re-layouts  5.16 us (4%)
    pallas_call x8, Pallas kernels, call(): pl.pallas_call(wrapped, out_shape=outs, in_specs=[specs[p] for p in place...  40.2 us
    ppermute x29, starting transfers between devices, shift_by(): lax.ppermute(value, axis, [(i, move(i)) for i in range(lax.axis_size(axis...  31.5 us
    ppermute x29, waiting for transfers between devices, shift_by(): lax.ppermute(value, axis, [(i, move(i)) for i in range(lax.axis_size(axis...  25.5 us
    all_to_all x1, starting transfers between devices, body(): lax.all_to_all(patches_sent, 'slab', split_axis=0, concat_axis=0, tiled=T...  6.93 us
    all_to_all x1, starting transfers between devices, body(): lax.all_to_all(all_sent, 'slab', split_axis=0, concat_axis=0, tiled=True)  6.74 us
    all_to_all x1, starting transfers between devices, body(): lax.all_to_all(attn_pair, 'mp', split_axis=0, concat_axis=0, tiled=True,...  3.97 us
    unnamed x35, local copies, waits for them, and re-layouts  3.68 us
  transfers between devices with their start and end apart: 32, of which 15 were waited for; matrix products, arithmetic and copies ran while one was open for 4% of the time, Pallas kernels for 13%

profile of v3, /device:TPU:0, one launch (start us, length us, event | category | flops | bytes accessed | tf_op | source)
XLA Modules:
  0.0 128.1 jit_solution(17146661380187968700)
XLA Ops:
  0.6 0.8 slice.27
  1.5 1.6 %collective-permute-start = (bf16[2,64,256]{2,1,0:T(8,128)(2,1)S(1)}, bf16[2,64,256]{2,1,0:T(8,128)(2,1)S(1)}, u32[]{:S(2)}, u32[]{:S(2)}) collective-permute-start(bf16[2,64,256]{2,1,0:T(8,128)(2,1)S(1)} %slice.27), channel_id=1, source_target_pairs={{0,8},{8,16},{16,24},{24,32},{32,40},{40,48},{48,56},{56,64},{64,7... | collective-permute-start | bytes 196616 | tf_op jit(solution)/shard_map/ppermute | solution.py:719
  3.1 0.8 copy.22
  4.4 1.8 %shard_map.200 = f32[16,8,128]{2,1,0:T(8,128)} custom-call(s32[4]{0:T(128)} %refs_0_.10, s32[8,128]{1,0:T(8,128)} %pad.4.refs_1_, bf16[4,64,256]{2,1,0:T(8,128)(2,1)} %refs_2_.3, s32[2,128]{1,0:T(2,128)} %bitcast.29), custom_call_target="tpu_custom_call" | custom-call | flops 1048576 | bytes 1048576 | tf_op jit(solution)/shard_map/pallas_call | solution.py:703
  6.2 6.7 %all-to-all-start = ((f32[16,8,128]{2,1,0:T(8,128)}), f32[16,8,128]{2,1,0:T(8,128)S(1)}, u32[]{:S(2)}, u32[]{:S(2)}) async-start(f32[16,8,128]{2,1,0:T(8,128)} %shard_map.200), calls=%async_computation | async-start | bytes 131072 | tf_op jit(solution)/shard_map/all_to_all | solution.py:782
  13.0 4.1 %collective-permute-start.3 = (bf16[256,384]{1,0:T(8,128)(2,1)}, bf16[256,384]{1,0:T(8,128)(2,1)S(1)}, u32[]{:S(2)}, u32[]{:S(2)}) collective-permute-start(bf16[256,384]{1,0:T(8,128)(2,1)} %refs_12_.1), channel_id=1, source_target_pairs={{0,6},{1,7},{2,0},{3,1},{4,2},{5,3},{6,4},{7,5},{8,14},{9,15},{10,... | collective-permute-start | bytes 589832 | tf_op jit(solution)/shard_map/ppermute | solution.py:719
  17.1 1.3 collective-permute-start.1
  18.4 1.6 %shard_map.201.refs_7_ = bf16[432,64]{1,0:T(8,128)(2,1)} custom-call(bf16[64,432]{1,0:T(8,128)(2,1)} %refs_0_.6), custom_call_target="tpu_custom_call" | custom-call | flops 8589934592 | bytes 1048576 | tf_op jit(solution)/shard_map/pallas_call | solution.py:703
  21.3 2.9 %shard_map.202 = bf16[64,256]{1,0:T(8,128)(2,1)} custom-call(s32[4]{0:T(128)} %refs_0_.10, s32[8,128]{1,0:T(8,128)} %pad.4.refs_1_, bf16[4,64,256]{2,1,0:T(8,128)(2,1)} %refs_2_.3, bf16[2,64,256]{2,1,0:T(8,128)(2,1)} %copy-done.16, f32[16,8,128]{2,1,0:T(8,128)} %copy-done.6, f32[1,64]{1,0:T(1,128)} %bitcast.37, f32[1,64]{1,0:T(1,128)} %bitcast.38, ...), custom_call_target="tpu_custom_call" | custom-call | flops 268435456 | bytes 1048576 | tf_op jit(solution)/shard_map/pallas_call | solution.py:703
  24.2 1.0 collective-permute-done.3.refs_3_
  25.2 1.4 %collective-permute-done.2.refs_2_ = bf16[256,384]{1,0:T(8,128)(2,1)S(1)} collective-permute-done((bf16[256,384]{1,0:T(8,128)(2,1)}, bf16[256,384]{1,0:T(8,128)(2,1)S(1)}, u32[]{:S(2)}, u32[]{:S(2)}) %collective-permute-start.2) | collective-permute-done | bytes 196640 | tf_op jit(solution)/shard_map/ppermute | solution.py:719
  26.7 1.9 %collective-permute-done.1.refs_1_ = bf16[256,384]{1,0:T(8,128)(2,1)S(1)} collective-permute-done((bf16[256,384]{1,0:T(8,128)(2,1)}, bf16[256,384]{1,0:T(8,128)(2,1)S(1)}, u32[]{:S(2)}, u32[]{:S(2)}) %collective-permute-start.1) | collective-permute-done | bytes 196640 | tf_op jit(solution)/shard_map/ppermute | solution.py:719
  28.5 1.4 %collective-permute-done.4 = bf16[64,256]{1,0:T(8,128)(2,1)S(1)} collective-permute-done((bf16[64,256]{1,0:T(8,128)(2,1)}, bf16[64,256]{1,0:T(8,128)(2,1)S(1)}, u32[]{:S(2)}, u32[]{:S(2)}) %collective-permute-start.4) | collective-permute-done | bytes 32800 | tf_op jit(solution)/shard_map/ppermute | solution.py:719
  30.0 0.8 add_convert_fusion.5.refs_0_
  30.7 1.0 collective-permute-start.7
  32.0 0.9 collective-permute-start.5
  32.8 1.9 %collective-permute-done.7.refs_3_ = bf16[64,256]{1,0:T(8,128)(2,1)S(1)} collective-permute-done((bf16[64,256]{1,0:T(8,128)(2,1)S(1)}, bf16[64,256]{1,0:T(8,128)(2,1)S(1)}, u32[]{:S(2)}, u32[]{:S(2)}) %collective-permute-start.7) | collective-permute-done | bytes 32800 | tf_op jit(solution)/shard_map/ppermute | solution.py:719
  34.7 2.4 %collective-permute-done.6.refs_2_ = bf16[64,256]{1,0:T(8,128)(2,1)S(1)} collective-permute-done((bf16[64,256]{1,0:T(8,128)(2,1)S(1)}, bf16[64,256]{1,0:T(8,128)(2,1)S(1)}, u32[]{:S(2)}, u32[]{:S(2)}) %collective-permute-start.6) | collective-permute-done | bytes 32800 | tf_op jit(solution)/shard_map/ppermute | solution.py:719
  37.5 0.9 shard_map.203
  38.9 6.9 %all-to-all-start.1 = ((bf16[16,64,256]{2,1,0:T(8,128)(2,1)}), bf16[16,64,256]{2,1,0:T(8,128)(2,1)S(1)}, u32[]{:S(2)}, u32[]{:S(2)}) async-start(bf16[16,64,256]{2,1,0:T(8,128)(2,1)} %get-tuple-element.80), calls=%async_computation.1 | async-start | bytes 1048576 | tf_op jit(solution)/shard_map/all_to_all | solution.py:818
  47.0 5.6 %shard_map.205 = (bf16[80,80]{1,0:T(8,128)(2,1)}, bf16[80,80]{1,0:T(8,128)(2,1)}, bf16[768,80]{1,0:T(8,128)(2,1)}, bf16[768,80]{1,0:T(8,128)(2,1)}, bf16[256,240...) custom-call(bf16[64,3072]{1,0:T(8,128)(2,1)} %refs_15_.1, f32[1,3072]{1,0:T(1,128)} %bitcast.33, ...), custom_call_target="tpu_custom_call" | custom-call | flops 4294967296 | bytes 1048576 | tf_op jit(solution)/shard_map/pallas_call | solution.py:703
  53.5 3.9 %shard_map.204 = (bf16[8,256,384]{2,1,0:T(8,128)(2,1)}, bf16[256,256]{1,0:T(8,128)(2,1)}, f32[4,16,256]{2,1,0:T(8,128)}) custom-call(bf16[256,384]{1,0:T(8,128)(2,1)} %refs_12_.1, bf16[256,384]{1,0:T(8,128)(2,1)} %copy-done.11, bf16[256,384]{1,0:T(8,128)(2,1)} %copy-done.10, bf16[256,384]{1,0:T(8,128)(2,1)} %copy-done.9, bf16[256,384]{1,0:T(8,128)(2,1)} %copy-done.12, ...), custom_call_target="tpu_custom_call" | custom-call | flops 4294967296 | bytes 1048576 | tf_op jit(solution)/shard_map/pallas_call | solution.py:703
  57.5 0.8 copy-done.3
  58.3 22.4 %shard_map.206 = (bf16[4,256,384]{2,1,0:T(8,128)(2,1)}, bf16[4,256,384]{2,1,0:T(8,128)(2,1)}, bf16[4,192,256]{2,1,0:T(8,128)(2,1)}, bf16[4,192,256]{2,1,0:T(8,12...) custom-call(s32[4]{0:T(128)} %refs_0_.10, ...), custom_call_target="tpu_custom_call" | custom-call | flops 17179869184 | bytes 1048576 | tf_op jit(solution)/shard_map/pallas_call | solution.py:703
  80.8 1.6 %collective-permute-done.12 = bf16[4,192,128]{2,1,0:T(8,128)(2,1)S(1)} collective-permute-done((bf16[4,192,128]{2,1,0:T(8,128)(2,1)}, bf16[4,192,128]{2,1,0:T(8,128)(2,1)S(1)}, u32[]{:S(2)}, u32[]{:S(2)}) %collective-permute-start.12) | collective-permute-done | bytes 196640 | tf_op jit(solution)/shard_map/ppermute | solution.py:719
  82.4 1.0 add_convert_fusion.3
  83.6 1.8 %collective-permute-start.13 = (bf16[192,128]{1,0:T(8,128)(2,1)S(1)}, bf16[192,128]{1,0:T(8,128)(2,1)S(1)}, u32[]{:S(2)}, u32[]{:S(2)}) collective-permute-start(bf16[192,128]{1,0:T(8,128)(2,1)S(1)} %get-tuple-element.131), channel_id=1, source_target_pairs={{0,4},{1,5},{2,6},{3,7},{4,0},{5,1},{6,2},{7,3},{8,12},{9,13},{10,... | collective-permute-start | bytes 147464 | tf_op jit(solution)/shard_map/ppermute | solution.py:719
  85.4 1.8 %collective-permute-start.15 = (bf16[192,128]{1,0:T(8,128)(2,1)S(1)}, bf16[192,128]{1,0:T(8,128)(2,1)S(1)}, u32[]{:S(2)}, u32[]{:S(2)}) collective-permute-start(bf16[192,128]{1,0:T(8,128)(2,1)S(1)} %get-tuple-element.132), channel_id=1, source_target_pairs={{0,6},{1,7},{2,0},{3,1},{4,2},{5,3},{6,4},{7,5},{8,14},{9,15},{10,... | collective-permute-start | bytes 147464 | tf_op jit(solution)/shard_map/ppermute | solution.py:719
  87.4 1.9 %collective-permute-start.19 = (bf16[4,192,256]{2,1,0:T(8,128)(2,1)}, bf16[4,192,256]{2,1,0:T(8,128)(2,1)S(1)}, u32[]{:S(2)}, u32[]{:S(2)}) collective-permute-start(bf16[4,192,256]{2,1,0:T(8,128)(2,1)} %get-tuple-element.104), channel_id=1, source_target_pairs={{0,32},{8,40},{16,48},{24,56},{32,64},{40,72},{48,80},{56,88},{64,... | collective-permute-start | bytes 1179656 | tf_op jit(solution)/shard_map/ppermute | solution.py:719
  89.3 3.4 %collective-permute-start.20 = (bf16[4,192,256]{2,1,0:T(8,128)(2,1)}, bf16[4,192,256]{2,1,0:T(8,128)(2,1)S(1)}, u32[]{:S(2)}, u32[]{:S(2)}) collective-permute-start(bf16[4,192,256]{2,1,0:T(8,128)(2,1)} %get-tuple-element.105), channel_id=1, source_target_pairs={{0,64},{8,72},{16,80},{24,88},{32,96},{40,104},{48,112},{56,120},{... | collective-permute-start | bytes 1179656 | tf_op jit(solution)/shard_map/ppermute | solution.py:719
  92.7 1.2 collective-permute-start.21
  93.9 0.9 fusion.2
  94.8 0.9 pad_maximum_fusion
  95.8 1.1 add_convert_fusion
  96.9 4.0 %all-to-all-start.2 = ((bf16[4,256,384]{2,1,0:T(8,128)(2,1)}), bf16[4,256,384]{2,1,0:T(8,128)(2,1)S(1)}, u32[]{:S(2)}, u32[]{:S(2)}) async-start(bf16[4,256,384]{2,1,0:T(8,128)(2,1)} %add_convert_fusion), calls=%async_computation.2 | async-start | bytes 1572864 | tf_op jit(solution)/shard_map/all_to_all | solution.py:922
  100.8 2.7 %collective-permute-start.18 = (bf16[592,128]{1,0:T(8,128)(2,1)S(1)}, bf16[592,128]{1,0:T(8,128)(2,1)S(1)}, u32[]{:S(2)}, u32[]{:S(2)}) collective-permute-start(bf16[592,128]{1,0:T(8,128)(2,1)S(1)} %pad_maximum_fusion), channel_id=1, source_target_pairs={{0,24},{8,0},{16,8},{24,16},{32,56},{40,32},{48,40},{56,48},{64,88... | collective-permute-start | bytes 454664 | tf_op jit(solution)/shard_map/ppermute | solution.py:719
  103.5 0.9 collective-permute-start.17
  104.4 4.2 %collective-permute-done.18 = bf16[592,128]{1,0:T(8,128)(2,1)S(1)} collective-permute-done((bf16[592,128]{1,0:T(8,128)(2,1)S(1)}, bf16[592,128]{1,0:T(8,128)(2,1)S(1)}, u32[]{:S(2)}, u32[]{:S(2)}) %collective-permute-start.18) | collective-permute-done | bytes 151584 | tf_op jit(solution)/shard_map/ppermute | solution.py:719
  109.1 1.2 collective-permute-done.17
  110.3 5.1 %collective-permute-done.16 = bf16[592,128]{1,0:T(8,128)(2,1)S(1)} collective-permute-done((bf16[592,128]{1,0:T(8,128)(2,1)S(1)}, bf16[592,128]{1,0:T(8,128)(2,1)S(1)}, u32[]{:S(2)}, u32[]{:S(2)}) %collective-permute-start.16) | collective-permute-done | bytes 151584 | tf_op jit(solution)/shard_map/ppermute | solution.py:719
  115.5 1.7 %collective-permute-start.25 = (bf16[592,128]{1,0:T(8,128)(2,1)S(1)}, bf16[592,128]{1,0:T(8,128)(2,1)S(1)}, u32[]{:S(2)}, u32[]{:S(2)}) collective-permute-start(bf16[592,128]{1,0:T(8,128)(2,1)S(1)} %add_convert_fusion.4.refs_0_), channel_id=1, source_target_pairs={{0,96},{8,104},{16,112},{24,120},{32,0},{40,8},{48,16},{56,24},{64... | collective-permute-start | bytes 454664 | tf_op jit(solution)/shard_map/ppermute | solution.py:719
  117.2 1.2 collective-permute-start.24
  119.2 1.1 collective-permute-start.26
  120.3 1.1 collective-permute-start.28
  121.5 1.0 collective-permute-start.27
  124.0 1.6 %collective-permute-done.23.refs_1_ = bf16[592,128]{1,0:T(8,128)(2,1)S(1)} collective-permute-done((bf16[592,128]{1,0:T(8,128)(2,1)S(1)}, bf16[592,128]{1,0:T(8,128)(2,1)S(1)}, u32[]{:S(2)}, u32[]{:S(2)}) %collective-permute-start.23) | collective-permute-done | bytes 151584 | tf_op jit(solution)/shard_map/ppermute | solution.py:719
  125.6 1.1 shard_map.207
  126.6 0.8 collective-permute-done.27
  (74 shorter events, 9.4 us)
Async XLA Ops:
  1.5 11.5 %collective-permute-start = (bf16[2,64,256]{2,1,0:T(8,128)(2,1)S(1)}, bf16[2,64,256]{2,1,0:T(8,128)(2,1)S(1)}, u32[]{:S(2)}, u32[]{:S(2)}) collective-permute-start(bf16[2,64,256]{2,1,0:T(8,128)(2,1)S(1)} %slice.27), channel_id=1, source_target_pairs={{0,8},{8,16},{16,24},{24,32},{32,40},{40,48},{48,56},{56,64},{64,7... | collective-permute-start | bytes 196616 | tf_op jit(solution)/shard_map/ppermute | solution.py:719
  6.2 14.4 %all-to-all-start = ((f32[16,8,128]{2,1,0:T(8,128)}), f32[16,8,128]{2,1,0:T(8,128)S(1)}, u32[]{:S(2)}, u32[]{:S(2)}) async-start(f32[16,8,128]{2,1,0:T(8,128)} %shard_map.200), calls=%async_computation | async-start | bytes 131072 | tf_op jit(solution)/shard_map/all_to_all | solution.py:782
  13.0 7.0 %copy-start.16 = (bf16[2,64,256]{2,1,0:T(8,128)(2,1)}, bf16[2,64,256]{2,1,0:T(8,128)(2,1)S(1)}, u32[]{:S(2)}) copy-start(bf16[2,64,256]{2,1,0:T(8,128)(2,1)S(1)} %collective-permute-done.refs_3_) | copy-start | bytes 196612
  13.0 12.2 %collective-permute-start.3 = (bf16[256,384]{1,0:T(8,128)(2,1)}, bf16[256,384]{1,0:T(8,128)(2,1)S(1)}, u32[]{:S(2)}, u32[]{:S(2)}) collective-permute-start(bf16[256,384]{1,0:T(8,128)(2,1)} %refs_12_.1), channel_id=1, source_target_pairs={{0,6},{1,7},{2,0},{3,1},{4,2},{5,3},{6,4},{7,5},{8,14},{9,15},{10,... | collective-permute-start | bytes 589832 | tf_op jit(solution)/shard_map/ppermute | solution.py:719
  17.1 9.6 %collective-permute-start.2 = (bf16[256,384]{1,0:T(8,128)(2,1)}, bf16[256,384]{1,0:T(8,128)(2,1)S(1)}, u32[]{:S(2)}, u32[]{:S(2)}) collective-permute-start(bf16[256,384]{1,0:T(8,128)(2,1)} %refs_12_.1), channel_id=1, source_target_pairs={{0,4},{1,5},{2,6},{3,7},{4,0},{5,1},{6,2},{7,3},{8,12},{9,13},{10,... | collective-permute-start | bytes 589832 | tf_op jit(solution)/shard_map/ppermute | solution.py:719
  17.1 11.4 %collective-permute-start.1 = (bf16[256,384]{1,0:T(8,128)(2,1)}, bf16[256,384]{1,0:T(8,128)(2,1)S(1)}, u32[]{:S(2)}, u32[]{:S(2)}) collective-permute-start(bf16[256,384]{1,0:T(8,128)(2,1)} %refs_12_.1), channel_id=1, source_target_pairs={{0,2},{1,3},{2,4},{3,5},{4,6},{5,7},{6,0},{7,1},{8,10},{9,11},{10,... | collective-permute-start | bytes 589832 | tf_op jit(solution)/shard_map/ppermute | solution.py:719
  20.0 25.9 %copy-start.8 = (bf16[256,384]{1,0:T(8,128)(2,1)S(1)}, bf16[256,384]{1,0:T(8,128)(2,1)}, u32[]{:S(2)}) copy-start(bf16[256,384]{1,0:T(8,128)(2,1)} %refs_12_.1) | copy-start | bytes 589828
  20.6 0.6 copy-start.6
  25.2 27.4 %copy-start.9 = (bf16[256,384]{1,0:T(8,128)(2,1)}, bf16[256,384]{1,0:T(8,128)(2,1)S(1)}, u32[]{:S(2)}) copy-start(bf16[256,384]{1,0:T(8,128)(2,1)S(1)} %collective-permute-done.3.refs_3_) | copy-start | bytes 589828
  26.7 25.9 %copy-start.10 = (bf16[256,384]{1,0:T(8,128)(2,1)}, bf16[256,384]{1,0:T(8,128)(2,1)S(1)}, u32[]{:S(2)}) copy-start(bf16[256,384]{1,0:T(8,128)(2,1)S(1)} %collective-permute-done.2.refs_2_) | copy-start | bytes 589828
  28.5 24.1 %copy-start.11 = (bf16[256,384]{1,0:T(8,128)(2,1)}, bf16[256,384]{1,0:T(8,128)(2,1)S(1)}, u32[]{:S(2)}) copy-start(bf16[256,384]{1,0:T(8,128)(2,1)S(1)} %collective-permute-done.1.refs_1_) | copy-start | bytes 589828
  28.5 1.4 %collective-permute-start.4 = (bf16[64,256]{1,0:T(8,128)(2,1)}, bf16[64,256]{1,0:T(8,128)(2,1)S(1)}, u32[]{:S(2)}, u32[]{:S(2)}) collective-permute-start(bf16[64,256]{1,0:T(8,128)(2,1)} %shard_map.202), channel_id=1, source_target_pairs={{0,1},{1,0},{2,3},{3,2},{4,5},{5,4},{6,7},{7,6},{8,9},{9,8},{10,11... | collective-permute-start | bytes 98312 | tf_op jit(solution)/shard_map/ppermute | solution.py:719
  30.7 4.0 %collective-permute-start.7 = (bf16[64,256]{1,0:T(8,128)(2,1)S(1)}, bf16[64,256]{1,0:T(8,128)(2,1)S(1)}, u32[]{:S(2)}, u32[]{:S(2)}) collective-permute-start(bf16[64,256]{1,0:T(8,128)(2,1)S(1)} %add_convert_fusion.5.refs_0_), channel_id=1, source_target_pairs={{0,6},{1,7},{2,0},{3,1},{4,2},{5,3},{6,4},{7,5},{8,14},{9,15},{10,... | collective-permute-start | bytes 98312 | tf_op jit(solution)/shard_map/ppermute | solution.py:719
  31.7 5.4 %collective-permute-start.6 = (bf16[64,256]{1,0:T(8,128)(2,1)S(1)}, bf16[64,256]{1,0:T(8,128)(2,1)S(1)}, u32[]{:S(2)}, u32[]{:S(2)}) collective-permute-start(bf16[64,256]{1,0:T(8,128)(2,1)S(1)} %add_convert_fusion.5.refs_0_), channel_id=1, source_target_pairs={{0,4},{1,5},{2,6},{3,7},{4,0},{5,1},{6,2},{7,3},{8,12},{9,13},{10,... | collective-permute-start | bytes 98312 | tf_op jit(solution)/shard_map/ppermute | solution.py:719
  32.0 5.5 %collective-permute-start.5 = (bf16[64,256]{1,0:T(8,128)(2,1)S(1)}, bf16[64,256]{1,0:T(8,128)(2,1)S(1)}, u32[]{:S(2)}, u32[]{:S(2)}) collective-permute-start(bf16[64,256]{1,0:T(8,128)(2,1)S(1)} %add_convert_fusion.5.refs_0_), channel_id=1, source_target_pairs={{0,2},{1,3},{2,4},{3,5},{4,6},{5,7},{6,0},{7,1},{8,10},{9,11},{10,... | collective-permute-start | bytes 98312 | tf_op jit(solution)/shard_map/ppermute | solution.py:719
  38.9 18.5 %all-to-all-start.1 = ((bf16[16,64,256]{2,1,0:T(8,128)(2,1)}), bf16[16,64,256]{2,1,0:T(8,128)(2,1)S(1)}, u32[]{:S(2)}, u32[]{:S(2)}) async-start(bf16[16,64,256]{2,1,0:T(8,128)(2,1)} %get-tuple-element.80), calls=%async_computation.1 | async-start | bytes 1048576 | tf_op jit(solution)/shard_map/all_to_all | solution.py:818
  45.9 6.7 %collective-permute-start.8 = (bf16[256,384]{1,0:T(8,128)(2,1)S(1)}, bf16[256,384]{1,0:T(8,128)(2,1)S(1)}, u32[]{:S(2)}, u32[]{:S(2)}) collective-permute-start(bf16[256,384]{1,0:T(8,128)(2,1)S(1)} %copy-done.8), channel_id=1, source_target_pairs={{0,1},{1,0},{2,3},{3,2},{4,5},{5,4},{6,7},{7,6},{8,9},{9,8},{10,11... | collective-permute-start | bytes 589832 | tf_op jit(solution)/shard_map/ppermute | solution.py:719
  46.0 6.7 %collective-permute-start.9 = (bf16[256,384]{1,0:T(8,128)(2,1)S(1)}, bf16[256,384]{1,0:T(8,128)(2,1)S(1)}, u32[]{:S(2)}, u32[]{:S(2)}) collective-permute-start(bf16[256,384]{1,0:T(8,128)(2,1)S(1)} %collective-permute-done.1.refs_1_), channel_id=1, source_target_pairs={{0,1},{1,0},{2,3},{3,2},{4,5},{5,4},{6,7},{7,6},{8,9},{9,8},{10,11... | collective-permute-start | bytes 589832 | tf_op jit(solution)/shard_map/ppermute | solution.py:719
  46.5 6.2 %collective-permute-start.10 = (bf16[256,384]{1,0:T(8,128)(2,1)S(1)}, bf16[256,384]{1,0:T(8,128)(2,1)S(1)}, u32[]{:S(2)}, u32[]{:S(2)}) collective-permute-start(bf16[256,384]{1,0:T(8,128)(2,1)S(1)} %collective-permute-done.2.refs_2_), channel_id=1, source_target_pairs={{0,1},{1,0},{2,3},{3,2},{4,5},{5,4},{6,7},{7,6},{8,9},{9,8},{10,11... | collective-permute-start | bytes 589832 | tf_op jit(solution)/shard_map/ppermute | solution.py:719
  46.6 6.1 %collective-permute-start.11 = (bf16[256,384]{1,0:T(8,128)(2,1)S(1)}, bf16[256,384]{1,0:T(8,128)(2,1)S(1)}, u32[]{:S(2)}, u32[]{:S(2)}) collective-permute-start(bf16[256,384]{1,0:T(8,128)(2,1)S(1)} %collective-permute-done.3.refs_3_), channel_id=1, source_target_pairs={{0,1},{1,0},{2,3},{3,2},{4,5},{5,4},{6,7},{7,6},{8,9},{9,8},{10,11... | collective-permute-start | bytes 589832 | tf_op jit(solution)/shard_map/ppermute | solution.py:719
  52.6 0.7 copy-start.12
  52.6 0.7 copy-start.13
  52.7 0.8 copy-start.14
  52.7 0.8 copy-start.15
  57.5 0.8 copy-start.3
  80.7 15.1 %copy-start.2 = (bf16[4,256,384]{2,1,0:T(8,128)(2,1)S(1)}, bf16[4,256,384]{2,1,0:T(8,128)(2,1)}, u32[]{:S(2)}) copy-start(bf16[4,256,384]{2,1,0:T(8,128)(2,1)} %get-tuple-element.110) | copy-start | bytes 2359300
  80.7 1.7 %collective-permute-start.12 = (bf16[4,192,128]{2,1,0:T(8,128)(2,1)}, bf16[4,192,128]{2,1,0:T(8,128)(2,1)S(1)}, u32[]{:S(2)}, u32[]{:S(2)}) collective-permute-start(bf16[4,192,128]{2,1,0:T(8,128)(2,1)} %get-tuple-element.94), channel_id=1, source_target_pairs={{0,1},{1,0},{2,3},{3,2},{4,5},{5,4},{6,7},{7,6},{8,9},{9,8},{10,11... | collective-permute-start | bytes 589832 | tf_op jit(solution)/shard_map/ppermute | solution.py:719
  83.4 12.4 %collective-permute-start.22 = (bf16[4,256,384]{2,1,0:T(8,128)(2,1)}, bf16[4,256,384]{2,1,0:T(8,128)(2,1)S(1)}, u32[]{:S(2)}, u32[]{:S(2)}) collective-permute-start(bf16[4,256,384]{2,1,0:T(8,128)(2,1)} %get-tuple-element.111), channel_id=1, source_target_pairs={{0,1},{1,0},{2,3},{3,2},{4,5},{5,4},{6,7},{7,6},{8,9},{9,8},{10,11... | collective-permute-start | bytes 2359304 | tf_op jit(solution)/shard_map/ppermute | solution.py:719
  83.6 5.7 %collective-permute-start.13 = (bf16[192,128]{1,0:T(8,128)(2,1)S(1)}, bf16[192,128]{1,0:T(8,128)(2,1)S(1)}, u32[]{:S(2)}, u32[]{:S(2)}) collective-permute-start(bf16[192,128]{1,0:T(8,128)(2,1)S(1)} %get-tuple-element.131), channel_id=1, source_target_pairs={{0,4},{1,5},{2,6},{3,7},{4,0},{5,1},{6,2},{7,3},{8,12},{9,13},{10,... | collective-permute-start | bytes 147464 | tf_op jit(solution)/shard_map/ppermute | solution.py:719
  85.4 7.4 %collective-permute-start.15 = (bf16[192,128]{1,0:T(8,128)(2,1)S(1)}, bf16[192,128]{1,0:T(8,128)(2,1)S(1)}, u32[]{:S(2)}, u32[]{:S(2)}) collective-permute-start(bf16[192,128]{1,0:T(8,128)(2,1)S(1)} %get-tuple-element.132), channel_id=1, source_target_pairs={{0,6},{1,7},{2,0},{3,1},{4,2},{5,3},{6,4},{7,5},{8,14},{9,15},{10,... | collective-permute-start | bytes 147464 | tf_op jit(solution)/shard_map/ppermute | solution.py:719
  87.2 6.7 %collective-permute-start.14 = (bf16[192,128]{1,0:T(8,128)(2,1)S(1)}, bf16[192,128]{1,0:T(8,128)(2,1)S(1)}, u32[]{:S(2)}, u32[]{:S(2)}) collective-permute-start(bf16[192,128]{1,0:T(8,128)(2,1)S(1)} %get-tuple-element.133), channel_id=1, source_target_pairs={{0,2},{1,3},{2,4},{3,5},{4,6},{5,7},{6,0},{7,1},{8,10},{9,11},{10,... | collective-permute-start | bytes 147464 | tf_op jit(solution)/shard_map/ppermute | solution.py:719
  87.4 28.0 %collective-permute-start.19 = (bf16[4,192,256]{2,1,0:T(8,128)(2,1)}, bf16[4,192,256]{2,1,0:T(8,128)(2,1)S(1)}, u32[]{:S(2)}, u32[]{:S(2)}) collective-permute-start(bf16[4,192,256]{2,1,0:T(8,128)(2,1)} %get-tuple-element.104), channel_id=1, source_target_pairs={{0,32},{8,40},{16,48},{24,56},{32,64},{40,72},{48,80},{56,88},{64,... | collective-permute-start | bytes 1179656 | tf_op jit(solution)/shard_map/ppermute | solution.py:719
  89.3 26.0 %collective-permute-start.20 = (bf16[4,192,256]{2,1,0:T(8,128)(2,1)}, bf16[4,192,256]{2,1,0:T(8,128)(2,1)S(1)}, u32[]{:S(2)}, u32[]{:S(2)}) collective-permute-start(bf16[4,192,256]{2,1,0:T(8,128)(2,1)} %get-tuple-element.105), channel_id=1, source_target_pairs={{0,64},{8,72},{16,80},{24,88},{32,96},{40,104},{48,112},{56,120},{... | collective-permute-start | bytes 1179656 | tf_op jit(solution)/shard_map/ppermute | solution.py:719
  92.7 22.6 %collective-permute-start.21 = (bf16[4,192,256]{2,1,0:T(8,128)(2,1)}, bf16[4,192,256]{2,1,0:T(8,128)(2,1)S(1)}, u32[]{:S(2)}, u32[]{:S(2)}) collective-permute-start(bf16[4,192,256]{2,1,0:T(8,128)(2,1)} %get-tuple-element.106), channel_id=1, source_target_pairs={{0,96},{8,104},{16,112},{24,120},{32,0},{40,8},{48,16},{56,24},{64... | collective-permute-start | bytes 1179656 | tf_op jit(solution)/shard_map/ppermute | solution.py:719
  95.7 13.3 %copy-start.7 = (f32[1,384]{1,0:T(1,128)S(1)}, f32[1,384]{1,0:T(1,128)}, u32[]{:S(2)}) copy-start(f32[1,384]{1,0:T(1,128)} %get-tuple-element.91) | copy-start | bytes 4612
  96.9 22.1 %copy-start.4 = (bf16[4,192,256]{2,1,0:T(8,128)(2,1)S(1)}, bf16[4,192,256]{2,1,0:T(8,128)(2,1)}, u32[]{:S(2)}) copy-start(bf16[4,192,256]{2,1,0:T(8,128)(2,1)} %get-tuple-element.116) | copy-start | bytes 1179652
  96.9 18.6 %all-to-all-start.2 = ((bf16[4,256,384]{2,1,0:T(8,128)(2,1)}), bf16[4,256,384]{2,1,0:T(8,128)(2,1)S(1)}, u32[]{:S(2)}, u32[]{:S(2)}) async-start(bf16[4,256,384]{2,1,0:T(8,128)(2,1)} %add_convert_fusion), calls=%async_computation.2 | async-start | bytes 1572864 | tf_op jit(solution)/shard_map/all_to_all | solution.py:922
  100.8 7.7 %collective-permute-start.18 = (bf16[592,128]{1,0:T(8,128)(2,1)S(1)}, bf16[592,128]{1,0:T(8,128)(2,1)S(1)}, u32[]{:S(2)}, u32[]{:S(2)}) collective-permute-start(bf16[592,128]{1,0:T(8,128)(2,1)S(1)} %pad_maximum_fusion), channel_id=1, source_target_pairs={{0,24},{8,0},{16,8},{24,16},{32,56},{40,32},{48,40},{56,48},{64,88... | collective-permute-start | bytes 454664 | tf_op jit(solution)/shard_map/ppermute | solution.py:719
  103.5 6.8 %collective-permute-start.17 = (bf16[592,128]{1,0:T(8,128)(2,1)S(1)}, bf16[592,128]{1,0:T(8,128)(2,1)S(1)}, u32[]{:S(2)}, u32[]{:S(2)}) collective-permute-start(bf16[592,128]{1,0:T(8,128)(2,1)S(1)} %pad_maximum_fusion), channel_id=1, source_target_pairs={{0,16},{8,24},{16,0},{24,8},{32,48},{40,56},{48,32},{56,40},{64,80... | collective-permute-start | bytes 454664 | tf_op jit(solution)/shard_map/ppermute | solution.py:719
  108.5 6.8 %collective-permute-start.16 = (bf16[592,128]{1,0:T(8,128)(2,1)S(1)}, bf16[592,128]{1,0:T(8,128)(2,1)S(1)}, u32[]{:S(2)}, u32[]{:S(2)}) collective-permute-start(bf16[592,128]{1,0:T(8,128)(2,1)S(1)} %pad_maximum_fusion), channel_id=1, source_target_pairs={{0,8},{8,16},{16,24},{24,0},{32,40},{40,48},{48,56},{56,32},{64,72... | collective-permute-start | bytes 454664 | tf_op jit(solution)/shard_map/ppermute | solution.py:719
  115.5 7.1 %copy-start.5 = (bf16[256,384]{1,0:T(8,128)(2,1)S(1)}, bf16[256,384]{1,0:T(8,128)(2,1)}, u32[]{:S(2)}) copy-start(bf16[256,384]{1,0:T(8,128)(2,1)} %get-tuple-element.90) | copy-start | bytes 589828
  115.5 6.0 %collective-permute-start.25 = (bf16[592,128]{1,0:T(8,128)(2,1)S(1)}, bf16[592,128]{1,0:T(8,128)(2,1)S(1)}, u32[]{:S(2)}, u32[]{:S(2)}) collective-permute-start(bf16[592,128]{1,0:T(8,128)(2,1)S(1)} %add_convert_fusion.4.refs_0_), channel_id=1, source_target_pairs={{0,96},{8,104},{16,112},{24,120},{32,0},{40,8},{48,16},{56,24},{64... | collective-permute-start | bytes 454664 | tf_op jit(solution)/shard_map/ppermute | solution.py:719
  117.2 6.8 %collective-permute-start.24 = (bf16[592,128]{1,0:T(8,128)(2,1)S(1)}, bf16[592,128]{1,0:T(8,128)(2,1)S(1)}, u32[]{:S(2)}, u32[]{:S(2)}) collective-permute-start(bf16[592,128]{1,0:T(8,128)(2,1)S(1)} %add_convert_fusion.4.refs_0_), channel_id=1, source_target_pairs={{0,64},{8,72},{16,80},{24,88},{32,96},{40,104},{48,112},{56,120},{... | collective-permute-start | bytes 454664 | tf_op jit(solution)/shard_map/ppermute | solution.py:719
  118.5 7.1 %collective-permute-start.23 = (bf16[592,128]{1,0:T(8,128)(2,1)S(1)}, bf16[592,128]{1,0:T(8,128)(2,1)S(1)}, u32[]{:S(2)}, u32[]{:S(2)}) collective-permute-start(bf16[592,128]{1,0:T(8,128)(2,1)S(1)} %add_convert_fusion.4.refs_0_), channel_id=1, source_target_pairs={{0,32},{8,40},{16,48},{24,56},{32,64},{40,72},{48,80},{56,88},{64,... | collective-permute-start | bytes 454664 | tf_op jit(solution)/shard_map/ppermute | solution.py:719
  119.2 6.4 %copy-start = (bf16[192,160]{1,0:T(8,128)(2,1)S(1)}, bf16[192,160]{1,0:T(8,128)(2,1)}, u32[]{:S(2)}) copy-start(bf16[192,160]{1,0:T(8,128)(2,1)} %get-tuple-element.123.refs_4_) | copy-start | bytes 184324
  119.2 7.4 %collective-permute-start.26 = (bf16[192,256]{1,0:T(8,128)(2,1)S(1)}, bf16[192,256]{1,0:T(8,128)(2,1)S(1)}, u32[]{:S(2)}, u32[]{:S(2)}) collective-permute-start(bf16[192,256]{1,0:T(8,128)(2,1)S(1)} %get-tuple-element.127), channel_id=1, source_target_pairs={{0,16},{8,24},{16,0},{24,8},{32,48},{40,56},{48,32},{56,40},{64,80... | collective-permute-start | bytes 294920 | tf_op jit(solution)/shard_map/ppermute | solution.py:719
  120.3 6.3 %collective-permute-start.28 = (bf16[192,256]{1,0:T(8,128)(2,1)S(1)}, bf16[192,256]{1,0:T(8,128)(2,1)S(1)}, u32[]{:S(2)}, u32[]{:S(2)}) collective-permute-start(bf16[192,256]{1,0:T(8,128)(2,1)S(1)} %get-tuple-element.128), channel_id=1, source_target_pairs={{0,24},{8,0},{16,8},{24,16},{32,56},{40,32},{48,40},{56,48},{64,88... | collective-permute-start | bytes 294920 | tf_op jit(solution)/shard_map/ppermute | solution.py:719
  121.5 5.9 %collective-permute-start.27 = (bf16[192,256]{1,0:T(8,128)(2,1)S(1)}, bf16[192,256]{1,0:T(8,128)(2,1)S(1)}, u32[]{:S(2)}, u32[]{:S(2)}) collective-permute-start(bf16[192,256]{1,0:T(8,128)(2,1)S(1)} %get-tuple-element.129), channel_id=1, source_target_pairs={{0,8},{8,16},{16,24},{24,0},{32,40},{40,48},{48,56},{56,32},{64,72... | collective-permute-start | bytes 294920 | tf_op jit(solution)/shard_map/ppermute | solution.py:719
  (1 other events, 0.6 us)

commit v4 on v3

--- a/solution.py
+++ b/solution.py
@@ -32,7 +32,7 @@
 FWD_BLOCK = 1024
 FWD_UNROLL = 1
 BWD_BLOCK = 1024
-BWD_UNROLL = 1
+BWD_UNROLL = 2
 
 
 def nn(a, b):
@@ -913,8 +913,9 @@
     embed_part = level_sum(y_pair) + g_own
     payload = jnp.concatenate([sums, embed_part.astype(BF16)], axis=0)
     payload, attn_mine = lax.optimization_barrier((payload, attn_mine))
+    payload, g_one = lax.optimization_barrier((payload, g_one))
     sent = tuple(shift_by(payload, "slab", along_x(k)) for k in (1, 2, 3))
-    sent, g_one, g_two, g_three = lax.optimization_barrier((sent, g_one, g_two, g_three))
+    sent, g_two, g_three = lax.optimization_barrier((sent, g_two, g_three))
     total = (
         (payload.astype(F32) + sent[1].astype(F32)) + (sent[0].astype(F32) + sent[2].astype(F32))
     ).astype(BF16)

time: 129 us -> 127 us (0.984)
  waiting for transfers between devices: 26.2 us -> 22.4 us
  starting transfers between devices: 49.1 us -> 51.5 us
    ppermute x29, waiting for transfers between devices: 25.5 us -> 21.7 us  [shift_by(): lax.ppermute(value, axis, [(i, move(i)) for i in range(lax.axis_size(axis...]
    ppermute x29, starting transfers between devices: 31.5 us -> 33.8 us  [shift_by(): lax.ppermute(value, axis, [(i, move(i)) for i in range(lax.axis_size(axis...]
where the time goes in v4:
time: 127 us; the launch traced here: 126 us
  starting transfers between devices  51.5 us (41%)
  Pallas kernels  39.8 us (31%)
  waiting for transfers between devices  22.4 us (18%)
  other arithmetic  6.56 us (5%)
  local copies, waits for them, and re-layouts  5.16 us (4%)
    pallas_call x8, Pallas kernels, call(): pl.pallas_call(wrapped, out_shape=outs, in_specs=[specs[p] for p in place...  39.8 us
    ppermute x29, starting transfers between devices, shift_by(): lax.ppermute(value, axis, [(i, move(i)) for i in range(lax.axis_size(axis...  33.8 us
    ppermute x29, waiting for transfers between devices, shift_by(): lax.ppermute(value, axis, [(i, move(i)) for i in range(lax.axis_size(axis...  21.7 us
    all_to_all x1, starting transfers between devices, body(): lax.all_to_all(patches_sent, 'slab', split_axis=0, concat_axis=0, tiled=T...  6.93 us
    all_to_all x1, starting transfers between devices, body(): lax.all_to_all(all_sent, 'slab', split_axis=0, concat_axis=0, tiled=True)  6.74 us
    all_to_all x1, starting transfers between devices, body(): lax.all_to_all(attn_pair, 'mp', split_axis=0, concat_axis=0, tiled=True,...  3.97 us
    unnamed x35, local copies, waits for them, and re-layouts  3.68 us
  transfers between devices with their start and end apart: 32, of which 15 were waited for; matrix products, arithmetic and copies ran while one was open for 4% of the time, Pallas kernels for 13%

profile of v4, /device:TPU:0, one launch (start us, length us, event | category | flops | bytes accessed | tf_op | source)
XLA Modules:
  0.0 126.3 jit_solution(11359430256460557663)
XLA Ops:
  0.6 0.8 slice.27
  1.5 1.6 %collective-permute-start = (bf16[2,64,256]{2,1,0:T(8,128)(2,1)S(1)}, bf16[2,64,256]{2,1,0:T(8,128)(2,1)S(1)}, u32[]{:S(2)}, u32[]{:S(2)}) collective-permute-start(bf16[2,64,256]{2,1,0:T(8,128)(2,1)S(1)} %slice.27), channel_id=1, source_target_pairs={{0,8},{8,16},{16,24},{24,32},{32,40},{40,48},{48,56},{56,64},{64,7... | collective-permute-start | bytes 196616 | tf_op jit(solution)/shard_map/ppermute | solution.py:719
  4.4 1.8 %shard_map.200 = f32[16,8,128]{2,1,0:T(8,128)} custom-call(s32[4]{0:T(128)} %refs_0_.10, s32[8,128]{1,0:T(8,128)} %pad.4.refs_1_, bf16[4,64,256]{2,1,0:T(8,128)(2,1)} %refs_2_.3, s32[2,128]{1,0:T(2,128)} %bitcast.29), custom_call_target="tpu_custom_call" | custom-call | flops 1048576 | bytes 1048576 | tf_op jit(solution)/shard_map/pallas_call | solution.py:703
  6.2 6.7 %all-to-all-start = ((f32[16,8,128]{2,1,0:T(8,128)}), f32[16,8,128]{2,1,0:T(8,128)S(1)}, u32[]{:S(2)}, u32[]{:S(2)}) async-start(f32[16,8,128]{2,1,0:T(8,128)} %shard_map.200), calls=%async_computation | async-start | bytes 131072 | tf_op jit(solution)/shard_map/all_to_all | solution.py:782
  13.0 4.1 %collective-permute-start.3 = (bf16[256,384]{1,0:T(8,128)(2,1)}, bf16[256,384]{1,0:T(8,128)(2,1)S(1)}, u32[]{:S(2)}, u32[]{:S(2)}) collective-permute-start(bf16[256,384]{1,0:T(8,128)(2,1)} %refs_12_.1), channel_id=1, source_target_pairs={{0,6},{1,7},{2,0},{3,1},{4,2},{5,3},{6,4},{7,5},{8,14},{9,15},{10,... | collective-permute-start | bytes 589832 | tf_op jit(solution)/shard_map/ppermute | solution.py:719
  17.1 1.3 collective-permute-start.1
  18.4 1.6 %shard_map.201.refs_7_ = bf16[432,64]{1,0:T(8,128)(2,1)} custom-call(bf16[64,432]{1,0:T(8,128)(2,1)} %refs_0_.6), custom_call_target="tpu_custom_call" | custom-call | flops 8589934592 | bytes 1048576 | tf_op jit(solution)/shard_map/pallas_call | solution.py:703
  21.3 2.9 %shard_map.202 = bf16[64,256]{1,0:T(8,128)(2,1)} custom-call(s32[4]{0:T(128)} %refs_0_.10, s32[8,128]{1,0:T(8,128)} %pad.4.refs_1_, bf16[4,64,256]{2,1,0:T(8,128)(2,1)} %refs_2_.3, bf16[2,64,256]{2,1,0:T(8,128)(2,1)} %copy-done.16, f32[16,8,128]{2,1,0:T(8,128)} %copy-done.6, f32[1,64]{1,0:T(1,128)} %bitcast.37, f32[1,64]{1,0:T(1,128)} %bitcast.38, ...), custom_call_target="tpu_custom_call" | custom-call | flops 268435456 | bytes 1048576 | tf_op jit(solution)/shard_map/pallas_call | solution.py:703
  24.2 1.0 collective-permute-done.3.refs_3_
  25.2 1.4 %collective-permute-done.2.refs_2_ = bf16[256,384]{1,0:T(8,128)(2,1)S(1)} collective-permute-done((bf16[256,384]{1,0:T(8,128)(2,1)}, bf16[256,384]{1,0:T(8,128)(2,1)S(1)}, u32[]{:S(2)}, u32[]{:S(2)}) %collective-permute-start.2) | collective-permute-done | bytes 196640 | tf_op jit(solution)/shard_map/ppermute | solution.py:719
  26.7 1.9 %collective-permute-done.1.refs_1_ = bf16[256,384]{1,0:T(8,128)(2,1)S(1)} collective-permute-done((bf16[256,384]{1,0:T(8,128)(2,1)}, bf16[256,384]{1,0:T(8,128)(2,1)S(1)}, u32[]{:S(2)}, u32[]{:S(2)}) %collective-permute-start.1) | collective-permute-done | bytes 196640 | tf_op jit(solution)/shard_map/ppermute | solution.py:719
  28.5 1.4 %collective-permute-done.4 = bf16[64,256]{1,0:T(8,128)(2,1)S(1)} collective-permute-done((bf16[64,256]{1,0:T(8,128)(2,1)}, bf16[64,256]{1,0:T(8,128)(2,1)S(1)}, u32[]{:S(2)}, u32[]{:S(2)}) %collective-permute-start.4) | collective-permute-done | bytes 32800 | tf_op jit(solution)/shard_map/ppermute | solution.py:719
  30.0 0.8 add_convert_fusion.5.refs_0_
  30.7 1.0 collective-permute-start.7
  32.0 0.9 collective-permute-start.5
  32.8 1.9 %collective-permute-done.7.refs_3_ = bf16[64,256]{1,0:T(8,128)(2,1)S(1)} collective-permute-done((bf16[64,256]{1,0:T(8,128)(2,1)S(1)}, bf16[64,256]{1,0:T(8,128)(2,1)S(1)}, u32[]{:S(2)}, u32[]{:S(2)}) %collective-permute-start.7) | collective-permute-done | bytes 32800 | tf_op jit(solution)/shard_map/ppermute | solution.py:719
  34.7 2.4 %collective-permute-done.6.refs_2_ = bf16[64,256]{1,0:T(8,128)(2,1)S(1)} collective-permute-done((bf16[64,256]{1,0:T(8,128)(2,1)S(1)}, bf16[64,256]{1,0:T(8,128)(2,1)S(1)}, u32[]{:S(2)}, u32[]{:S(2)}) %collective-permute-start.6) | collective-permute-done | bytes 32800 | tf_op jit(solution)/shard_map/ppermute | solution.py:719
  37.5 0.9 shard_map.203
  38.9 6.9 %all-to-all-start.1 = ((bf16[16,64,256]{2,1,0:T(8,128)(2,1)}), bf16[16,64,256]{2,1,0:T(8,128)(2,1)S(1)}, u32[]{:S(2)}, u32[]{:S(2)}) async-start(bf16[16,64,256]{2,1,0:T(8,128)(2,1)} %get-tuple-element.81), calls=%async_computation.1 | async-start | bytes 1048576 | tf_op jit(solution)/shard_map/all_to_all | solution.py:818
  47.0 5.6 %shard_map.205 = (bf16[80,80]{1,0:T(8,128)(2,1)}, bf16[80,80]{1,0:T(8,128)(2,1)}, bf16[768,80]{1,0:T(8,128)(2,1)}, bf16[768,80]{1,0:T(8,128)(2,1)}, bf16[256,240...) custom-call(bf16[64,3072]{1,0:T(8,128)(2,1)} %refs_15_.1, f32[1,3072]{1,0:T(1,128)} %bitcast.33, ...), custom_call_target="tpu_custom_call" | custom-call | flops 4294967296 | bytes 1048576 | tf_op jit(solution)/shard_map/pallas_call | solution.py:703
  53.5 3.9 %shard_map.204 = (bf16[8,256,384]{2,1,0:T(8,128)(2,1)}, bf16[256,256]{1,0:T(8,128)(2,1)}, f32[4,16,256]{2,1,0:T(8,128)}) custom-call(bf16[256,384]{1,0:T(8,128)(2,1)} %refs_12_.1, bf16[256,384]{1,0:T(8,128)(2,1)} %copy-done.11, bf16[256,384]{1,0:T(8,128)(2,1)} %copy-done.10, bf16[256,384]{1,0:T(8,128)(2,1)} %copy-done.9, bf16[256,384]{1,0:T(8,128)(2,1)} %copy-done.12, ...), custom_call_target="tpu_custom_call" | custom-call | flops 4294967296 | bytes 1048576 | tf_op jit(solution)/shard_map/pallas_call | solution.py:703
  57.5 0.8 copy-done.3
  58.3 22.0 %shard_map.206 = (bf16[4,256,384]{2,1,0:T(8,128)(2,1)}, bf16[4,256,384]{2,1,0:T(8,128)(2,1)}, bf16[4,192,256]{2,1,0:T(8,128)(2,1)}, bf16[4,192,256]{2,1,0:T(8,12...) custom-call(s32[4]{0:T(128)} %refs_0_.10, ...), custom_call_target="tpu_custom_call" | custom-call | flops 17179869184 | bytes 1048576 | tf_op jit(solution)/shard_map/pallas_call | solution.py:703
  80.4 1.6 %collective-permute-done.12 = bf16[4,192,128]{2,1,0:T(8,128)(2,1)S(1)} collective-permute-done((bf16[4,192,128]{2,1,0:T(8,128)(2,1)}, bf16[4,192,128]{2,1,0:T(8,128)(2,1)S(1)}, u32[]{:S(2)}, u32[]{:S(2)}) %collective-permute-start.12) | collective-permute-done | bytes 196640 | tf_op jit(solution)/shard_map/ppermute | solution.py:719
  82.0 1.0 add_convert_fusion.3
  83.4 1.8 %collective-permute-start.13 = (bf16[192,128]{1,0:T(8,128)(2,1)S(1)}, bf16[192,128]{1,0:T(8,128)(2,1)S(1)}, u32[]{:S(2)}, u32[]{:S(2)}) collective-permute-start(bf16[192,128]{1,0:T(8,128)(2,1)S(1)} %get-tuple-element.133), channel_id=1, source_target_pairs={{0,4},{1,5},{2,6},{3,7},{4,0},{5,1},{6,2},{7,3},{8,12},{9,13},{10,... | collective-permute-start | bytes 147464 | tf_op jit(solution)/shard_map/ppermute | solution.py:719
  85.2 1.8 %collective-permute-start.15 = (bf16[192,128]{1,0:T(8,128)(2,1)S(1)}, bf16[192,128]{1,0:T(8,128)(2,1)S(1)}, u32[]{:S(2)}, u32[]{:S(2)}) collective-permute-start(bf16[192,128]{1,0:T(8,128)(2,1)S(1)} %get-tuple-element.134), channel_id=1, source_target_pairs={{0,6},{1,7},{2,0},{3,1},{4,2},{5,3},{6,4},{7,5},{8,14},{9,15},{10,... | collective-permute-start | bytes 147464 | tf_op jit(solution)/shard_map/ppermute | solution.py:719
  87.2 1.9 %collective-permute-start.16 = (bf16[4,192,256]{2,1,0:T(8,128)(2,1)}, bf16[4,192,256]{2,1,0:T(8,128)(2,1)S(1)}, u32[]{:S(2)}, u32[]{:S(2)}) collective-permute-start(bf16[4,192,256]{2,1,0:T(8,128)(2,1)} %get-tuple-element.105), channel_id=1, source_target_pairs={{0,32},{8,40},{16,48},{24,56},{32,64},{40,72},{48,80},{56,88},{64,... | collective-permute-start | bytes 1179656 | tf_op jit(solution)/shard_map/ppermute | solution.py:719
  89.2 3.4 %collective-permute-start.20 = (bf16[4,192,256]{2,1,0:T(8,128)(2,1)}, bf16[4,192,256]{2,1,0:T(8,128)(2,1)S(1)}, u32[]{:S(2)}, u32[]{:S(2)}) collective-permute-start(bf16[4,192,256]{2,1,0:T(8,128)(2,1)} %get-tuple-element.107), channel_id=1, source_target_pairs={{0,64},{8,72},{16,80},{24,88},{32,96},{40,104},{48,112},{56,120},{... | collective-permute-start | bytes 1179656 | tf_op jit(solution)/shard_map/ppermute | solution.py:719
  92.6 1.2 collective-permute-start.21
  93.7 0.9 fusion.2
  94.7 0.9 pad_maximum_fusion
  95.6 1.1 add_convert_fusion
  96.7 4.0 %all-to-all-start.2 = ((bf16[4,256,384]{2,1,0:T(8,128)(2,1)}), bf16[4,256,384]{2,1,0:T(8,128)(2,1)S(1)}, u32[]{:S(2)}, u32[]{:S(2)}) async-start(bf16[4,256,384]{2,1,0:T(8,128)(2,1)} %add_convert_fusion), calls=%async_computation.2 | async-start | bytes 1572864 | tf_op jit(solution)/shard_map/all_to_all | solution.py:923
  100.7 2.7 %collective-permute-start.19 = (bf16[592,128]{1,0:T(8,128)(2,1)S(1)}, bf16[592,128]{1,0:T(8,128)(2,1)S(1)}, u32[]{:S(2)}, u32[]{:S(2)}) collective-permute-start(bf16[592,128]{1,0:T(8,128)(2,1)S(1)} %pad_maximum_fusion), channel_id=1, source_target_pairs={{0,24},{8,0},{16,8},{24,16},{32,56},{40,32},{48,40},{56,48},{64,88... | collective-permute-start | bytes 454664 | tf_op jit(solution)/shard_map/ppermute | solution.py:719
  103.3 0.9 collective-permute-start.18
  104.2 0.9 collective-permute-start.17
  105.1 3.9 %collective-permute-done.20 = bf16[4,192,256]{2,1,0:T(8,128)(2,1)S(1)} collective-permute-done((bf16[4,192,256]{2,1,0:T(8,128)(2,1)}, bf16[4,192,256]{2,1,0:T(8,128)(2,1)S(1)}, u32[]{:S(2)}, u32[]{:S(2)}) %collective-permute-start.20) | collective-permute-done | bytes 393248 | tf_op jit(solution)/shard_map/ppermute | solution.py:719
  109.0 1.0 collective-permute-done.21
  110.5 1.5 %collective-permute-done.17 = bf16[592,128]{1,0:T(8,128)(2,1)S(1)} collective-permute-done((bf16[592,128]{1,0:T(8,128)(2,1)S(1)}, bf16[592,128]{1,0:T(8,128)(2,1)S(1)}, u32[]{:S(2)}, u32[]{:S(2)}) %collective-permute-start.17) | collective-permute-done | bytes 151584 | tf_op jit(solution)/shard_map/ppermute | solution.py:719
  112.2 1.7 %collective-permute-start.25 = (bf16[592,128]{1,0:T(8,128)(2,1)S(1)}, bf16[592,128]{1,0:T(8,128)(2,1)S(1)}, u32[]{:S(2)}, u32[]{:S(2)}) collective-permute-start(bf16[592,128]{1,0:T(8,128)(2,1)S(1)} %add_convert_fusion.4.refs_0_), channel_id=1, source_target_pairs={{0,96},{8,104},{16,112},{24,120},{32,0},{40,8},{48,16},{56,24},{64... | collective-permute-start | bytes 454664 | tf_op jit(solution)/shard_map/ppermute | solution.py:719
  113.9 1.2 collective-permute-start.24
  115.9 2.5 %collective-permute-start.26 = (bf16[192,256]{1,0:T(8,128)(2,1)S(1)}, bf16[192,256]{1,0:T(8,128)(2,1)S(1)}, u32[]{:S(2)}, u32[]{:S(2)}) collective-permute-start(bf16[192,256]{1,0:T(8,128)(2,1)S(1)} %get-tuple-element.129), channel_id=1, source_target_pairs={{0,16},{8,24},{16,0},{24,8},{32,48},{40,56},{48,32},{56,40},{64,80... | collective-permute-start | bytes 294920 | tf_op jit(solution)/shard_map/ppermute | solution.py:719
  118.4 1.2 collective-permute-start.28
  119.7 1.3 %collective-permute-start.27 = (bf16[192,256]{1,0:T(8,128)(2,1)S(1)}, bf16[192,256]{1,0:T(8,128)(2,1)S(1)}, u32[]{:S(2)}, u32[]{:S(2)}) collective-permute-start(bf16[192,256]{1,0:T(8,128)(2,1)S(1)} %get-tuple-element.131), channel_id=1, source_target_pairs={{0,8},{8,16},{16,24},{24,0},{32,40},{40,48},{48,56},{56,32},{64,72... | collective-permute-start | bytes 294920 | tf_op jit(solution)/shard_map/ppermute | solution.py:719
  121.7 1.5 %collective-permute-done.23.refs_1_ = bf16[592,128]{1,0:T(8,128)(2,1)S(1)} collective-permute-done((bf16[592,128]{1,0:T(8,128)(2,1)S(1)}, bf16[592,128]{1,0:T(8,128)(2,1)S(1)}, u32[]{:S(2)}, u32[]{:S(2)}) %collective-permute-start.23) | collective-permute-done | bytes 151584 | tf_op jit(solution)/shard_map/ppermute | solution.py:719
  123.2 1.1 shard_map.207
  124.2 1.3 %collective-permute-done.27 = bf16[192,256]{1,0:T(8,128)(2,1)S(1)} collective-permute-done((bf16[192,256]{1,0:T(8,128)(2,1)S(1)}, bf16[192,256]{1,0:T(8,128)(2,1)S(1)}, u32[]{:S(2)}, u32[]{:S(2)}) %collective-permute-start.27) | collective-permute-done | bytes 98336 | tf_op jit(solution)/shard_map/ppermute | solution.py:719
  (74 shorter events, 9.7 us)
Async XLA Ops:
  1.5 11.5 %collective-permute-start = (bf16[2,64,256]{2,1,0:T(8,128)(2,1)S(1)}, bf16[2,64,256]{2,1,0:T(8,128)(2,1)S(1)}, u32[]{:S(2)}, u32[]{:S(2)}) collective-permute-start(bf16[2,64,256]{2,1,0:T(8,128)(2,1)S(1)} %slice.27), channel_id=1, source_target_pairs={{0,8},{8,16},{16,24},{24,32},{32,40},{40,48},{48,56},{56,64},{64,7... | collective-permute-start | bytes 196616 | tf_op jit(solution)/shard_map/ppermute | solution.py:719
  6.2 14.4 %all-to-all-start = ((f32[16,8,128]{2,1,0:T(8,128)}), f32[16,8,128]{2,1,0:T(8,128)S(1)}, u32[]{:S(2)}, u32[]{:S(2)}) async-start(f32[16,8,128]{2,1,0:T(8,128)} %shard_map.200), calls=%async_computation | async-start | bytes 131072 | tf_op jit(solution)/shard_map/all_to_all | solution.py:782
  13.0 7.0 %copy-start.16 = (bf16[2,64,256]{2,1,0:T(8,128)(2,1)}, bf16[2,64,256]{2,1,0:T(8,128)(2,1)S(1)}, u32[]{:S(2)}) copy-start(bf16[2,64,256]{2,1,0:T(8,128)(2,1)S(1)} %collective-permute-done.refs_3_) | copy-start | bytes 196612
  13.0 12.2 %collective-permute-start.3 = (bf16[256,384]{1,0:T(8,128)(2,1)}, bf16[256,384]{1,0:T(8,128)(2,1)S(1)}, u32[]{:S(2)}, u32[]{:S(2)}) collective-permute-start(bf16[256,384]{1,0:T(8,128)(2,1)} %refs_12_.1), channel_id=1, source_target_pairs={{0,6},{1,7},{2,0},{3,1},{4,2},{5,3},{6,4},{7,5},{8,14},{9,15},{10,... | collective-permute-start | bytes 589832 | tf_op jit(solution)/shard_map/ppermute | solution.py:719
  17.1 9.6 %collective-permute-start.2 = (bf16[256,384]{1,0:T(8,128)(2,1)}, bf16[256,384]{1,0:T(8,128)(2,1)S(1)}, u32[]{:S(2)}, u32[]{:S(2)}) collective-permute-start(bf16[256,384]{1,0:T(8,128)(2,1)} %refs_12_.1), channel_id=1, source_target_pairs={{0,4},{1,5},{2,6},{3,7},{4,0},{5,1},{6,2},{7,3},{8,12},{9,13},{10,... | collective-permute-start | bytes 589832 | tf_op jit(solution)/shard_map/ppermute | solution.py:719
  17.1 11.4 %collective-permute-start.1 = (bf16[256,384]{1,0:T(8,128)(2,1)}, bf16[256,384]{1,0:T(8,128)(2,1)S(1)}, u32[]{:S(2)}, u32[]{:S(2)}) collective-permute-start(bf16[256,384]{1,0:T(8,128)(2,1)} %refs_12_.1), channel_id=1, source_target_pairs={{0,2},{1,3},{2,4},{3,5},{4,6},{5,7},{6,0},{7,1},{8,10},{9,11},{10,... | collective-permute-start | bytes 589832 | tf_op jit(solution)/shard_map/ppermute | solution.py:719
  20.0 25.9 %copy-start.8 = (bf16[256,384]{1,0:T(8,128)(2,1)S(1)}, bf16[256,384]{1,0:T(8,128)(2,1)}, u32[]{:S(2)}) copy-start(bf16[256,384]{1,0:T(8,128)(2,1)} %refs_12_.1) | copy-start | bytes 589828
  20.6 0.6 copy-start.6
  25.2 27.4 %copy-start.9 = (bf16[256,384]{1,0:T(8,128)(2,1)}, bf16[256,384]{1,0:T(8,128)(2,1)S(1)}, u32[]{:S(2)}) copy-start(bf16[256,384]{1,0:T(8,128)(2,1)S(1)} %collective-permute-done.3.refs_3_) | copy-start | bytes 589828
  26.7 25.9 %copy-start.10 = (bf16[256,384]{1,0:T(8,128)(2,1)}, bf16[256,384]{1,0:T(8,128)(2,1)S(1)}, u32[]{:S(2)}) copy-start(bf16[256,384]{1,0:T(8,128)(2,1)S(1)} %collective-permute-done.2.refs_2_) | copy-start | bytes 589828
  28.5 24.1 %copy-start.11 = (bf16[256,384]{1,0:T(8,128)(2,1)}, bf16[256,384]{1,0:T(8,128)(2,1)S(1)}, u32[]{:S(2)}) copy-start(bf16[256,384]{1,0:T(8,128)(2,1)S(1)} %collective-permute-done.1.refs_1_) | copy-start | bytes 589828
  28.5 1.4 %collective-permute-start.4 = (bf16[64,256]{1,0:T(8,128)(2,1)}, bf16[64,256]{1,0:T(8,128)(2,1)S(1)}, u32[]{:S(2)}, u32[]{:S(2)}) collective-permute-start(bf16[64,256]{1,0:T(8,128)(2,1)} %shard_map.202), channel_id=1, source_target_pairs={{0,1},{1,0},{2,3},{3,2},{4,5},{5,4},{6,7},{7,6},{8,9},{9,8},{10,11... | collective-permute-start | bytes 98312 | tf_op jit(solution)/shard_map/ppermute | solution.py:719
  30.7 4.0 %collective-permute-start.7 = (bf16[64,256]{1,0:T(8,128)(2,1)S(1)}, bf16[64,256]{1,0:T(8,128)(2,1)S(1)}, u32[]{:S(2)}, u32[]{:S(2)}) collective-permute-start(bf16[64,256]{1,0:T(8,128)(2,1)S(1)} %add_convert_fusion.5.refs_0_), channel_id=1, source_target_pairs={{0,6},{1,7},{2,0},{3,1},{4,2},{5,3},{6,4},{7,5},{8,14},{9,15},{10,... | collective-permute-start | bytes 98312 | tf_op jit(solution)/shard_map/ppermute | solution.py:719
  31.7 5.4 %collective-permute-start.6 = (bf16[64,256]{1,0:T(8,128)(2,1)S(1)}, bf16[64,256]{1,0:T(8,128)(2,1)S(1)}, u32[]{:S(2)}, u32[]{:S(2)}) collective-permute-start(bf16[64,256]{1,0:T(8,128)(2,1)S(1)} %add_convert_fusion.5.refs_0_), channel_id=1, source_target_pairs={{0,4},{1,5},{2,6},{3,7},{4,0},{5,1},{6,2},{7,3},{8,12},{9,13},{10,... | collective-permute-start | bytes 98312 | tf_op jit(solution)/shard_map/ppermute | solution.py:719
  32.0 5.5 %collective-permute-start.5 = (bf16[64,256]{1,0:T(8,128)(2,1)S(1)}, bf16[64,256]{1,0:T(8,128)(2,1)S(1)}, u32[]{:S(2)}, u32[]{:S(2)}) collective-permute-start(bf16[64,256]{1,0:T(8,128)(2,1)S(1)} %add_convert_fusion.5.refs_0_), channel_id=1, source_target_pairs={{0,2},{1,3},{2,4},{3,5},{4,6},{5,7},{6,0},{7,1},{8,10},{9,11},{10,... | collective-permute-start | bytes 98312 | tf_op jit(solution)/shard_map/ppermute | solution.py:719
  38.9 18.5 %all-to-all-start.1 = ((bf16[16,64,256]{2,1,0:T(8,128)(2,1)}), bf16[16,64,256]{2,1,0:T(8,128)(2,1)S(1)}, u32[]{:S(2)}, u32[]{:S(2)}) async-start(bf16[16,64,256]{2,1,0:T(8,128)(2,1)} %get-tuple-element.81), calls=%async_computation.1 | async-start | bytes 1048576 | tf_op jit(solution)/shard_map/all_to_all | solution.py:818
  45.9 6.7 %collective-permute-start.8 = (bf16[256,384]{1,0:T(8,128)(2,1)S(1)}, bf16[256,384]{1,0:T(8,128)(2,1)S(1)}, u32[]{:S(2)}, u32[]{:S(2)}) collective-permute-start(bf16[256,384]{1,0:T(8,128)(2,1)S(1)} %copy-done.8), channel_id=1, source_target_pairs={{0,1},{1,0},{2,3},{3,2},{4,5},{5,4},{6,7},{7,6},{8,9},{9,8},{10,11... | collective-permute-start | bytes 589832 | tf_op jit(solution)/shard_map/ppermute | solution.py:719
  46.0 6.7 %collective-permute-start.9 = (bf16[256,384]{1,0:T(8,128)(2,1)S(1)}, bf16[256,384]{1,0:T(8,128)(2,1)S(1)}, u32[]{:S(2)}, u32[]{:S(2)}) collective-permute-start(bf16[256,384]{1,0:T(8,128)(2,1)S(1)} %collective-permute-done.1.refs_1_), channel_id=1, source_target_pairs={{0,1},{1,0},{2,3},{3,2},{4,5},{5,4},{6,7},{7,6},{8,9},{9,8},{10,11... | collective-permute-start | bytes 589832 | tf_op jit(solution)/shard_map/ppermute | solution.py:719
  46.5 6.2 %collective-permute-start.10 = (bf16[256,384]{1,0:T(8,128)(2,1)S(1)}, bf16[256,384]{1,0:T(8,128)(2,1)S(1)}, u32[]{:S(2)}, u32[]{:S(2)}) collective-permute-start(bf16[256,384]{1,0:T(8,128)(2,1)S(1)} %collective-permute-done.2.refs_2_), channel_id=1, source_target_pairs={{0,1},{1,0},{2,3},{3,2},{4,5},{5,4},{6,7},{7,6},{8,9},{9,8},{10,11... | collective-permute-start | bytes 589832 | tf_op jit(solution)/shard_map/ppermute | solution.py:719
  46.6 6.1 %collective-permute-start.11 = (bf16[256,384]{1,0:T(8,128)(2,1)S(1)}, bf16[256,384]{1,0:T(8,128)(2,1)S(1)}, u32[]{:S(2)}, u32[]{:S(2)}) collective-permute-start(bf16[256,384]{1,0:T(8,128)(2,1)S(1)} %collective-permute-done.3.refs_3_), channel_id=1, source_target_pairs={{0,1},{1,0},{2,3},{3,2},{4,5},{5,4},{6,7},{7,6},{8,9},{9,8},{10,11... | collective-permute-start | bytes 589832 | tf_op jit(solution)/shard_map/ppermute | solution.py:719
  52.6 0.7 copy-start.12
  52.6 0.7 copy-start.13
  52.7 0.8 copy-start.14
  52.7 0.8 copy-start.15
  57.5 0.8 copy-start.3
  80.3 15.3 %copy-start.2 = (bf16[4,256,384]{2,1,0:T(8,128)(2,1)S(1)}, bf16[4,256,384]{2,1,0:T(8,128)(2,1)}, u32[]{:S(2)}) copy-start(bf16[4,256,384]{2,1,0:T(8,128)(2,1)} %get-tuple-element.112) | copy-start | bytes 2359300
  80.3 1.7 %collective-permute-start.12 = (bf16[4,192,128]{2,1,0:T(8,128)(2,1)}, bf16[4,192,128]{2,1,0:T(8,128)(2,1)S(1)}, u32[]{:S(2)}, u32[]{:S(2)}) collective-permute-start(bf16[4,192,128]{2,1,0:T(8,128)(2,1)} %get-tuple-element.95), channel_id=1, source_target_pairs={{0,1},{1,0},{2,3},{3,2},{4,5},{5,4},{6,7},{7,6},{8,9},{9,8},{10,11... | collective-permute-start | bytes 589832 | tf_op jit(solution)/shard_map/ppermute | solution.py:719
  83.0 12.6 %collective-permute-start.22 = (bf16[4,256,384]{2,1,0:T(8,128)(2,1)}, bf16[4,256,384]{2,1,0:T(8,128)(2,1)S(1)}, u32[]{:S(2)}, u32[]{:S(2)}) collective-permute-start(bf16[4,256,384]{2,1,0:T(8,128)(2,1)} %get-tuple-element.113), channel_id=1, source_target_pairs={{0,1},{1,0},{2,3},{3,2},{4,5},{5,4},{6,7},{7,6},{8,9},{9,8},{10,11... | collective-permute-start | bytes 2359304 | tf_op jit(solution)/shard_map/ppermute | solution.py:719
  83.4 5.7 %collective-permute-start.13 = (bf16[192,128]{1,0:T(8,128)(2,1)S(1)}, bf16[192,128]{1,0:T(8,128)(2,1)S(1)}, u32[]{:S(2)}, u32[]{:S(2)}) collective-permute-start(bf16[192,128]{1,0:T(8,128)(2,1)S(1)} %get-tuple-element.133), channel_id=1, source_target_pairs={{0,4},{1,5},{2,6},{3,7},{4,0},{5,1},{6,2},{7,3},{8,12},{9,13},{10,... | collective-permute-start | bytes 147464 | tf_op jit(solution)/shard_map/ppermute | solution.py:719
  85.2 7.4 %collective-permute-start.15 = (bf16[192,128]{1,0:T(8,128)(2,1)S(1)}, bf16[192,128]{1,0:T(8,128)(2,1)S(1)}, u32[]{:S(2)}, u32[]{:S(2)}) collective-permute-start(bf16[192,128]{1,0:T(8,128)(2,1)S(1)} %get-tuple-element.134), channel_id=1, source_target_pairs={{0,6},{1,7},{2,0},{3,1},{4,2},{5,3},{6,4},{7,5},{8,14},{9,15},{10,... | collective-permute-start | bytes 147464 | tf_op jit(solution)/shard_map/ppermute | solution.py:719
  87.0 6.7 %collective-permute-start.14 = (bf16[192,128]{1,0:T(8,128)(2,1)S(1)}, bf16[192,128]{1,0:T(8,128)(2,1)S(1)}, u32[]{:S(2)}, u32[]{:S(2)}) collective-permute-start(bf16[192,128]{1,0:T(8,128)(2,1)S(1)} %get-tuple-element.135), channel_id=1, source_target_pairs={{0,2},{1,3},{2,4},{3,5},{4,6},{5,7},{6,0},{7,1},{8,10},{9,11},{10,... | collective-permute-start | bytes 147464 | tf_op jit(solution)/shard_map/ppermute | solution.py:719
  87.2 13.4 %collective-permute-start.16 = (bf16[4,192,256]{2,1,0:T(8,128)(2,1)}, bf16[4,192,256]{2,1,0:T(8,128)(2,1)S(1)}, u32[]{:S(2)}, u32[]{:S(2)}) collective-permute-start(bf16[4,192,256]{2,1,0:T(8,128)(2,1)} %get-tuple-element.105), channel_id=1, source_target_pairs={{0,32},{8,40},{16,48},{24,56},{32,64},{40,72},{48,80},{56,88},{64,... | collective-permute-start | bytes 1179656 | tf_op jit(solution)/shard_map/ppermute | solution.py:719
  89.2 19.9 %collective-permute-start.20 = (bf16[4,192,256]{2,1,0:T(8,128)(2,1)}, bf16[4,192,256]{2,1,0:T(8,128)(2,1)S(1)}, u32[]{:S(2)}, u32[]{:S(2)}) collective-permute-start(bf16[4,192,256]{2,1,0:T(8,128)(2,1)} %get-tuple-element.107), channel_id=1, source_target_pairs={{0,64},{8,72},{16,80},{24,88},{32,96},{40,104},{48,112},{56,120},{... | collective-permute-start | bytes 1179656 | tf_op jit(solution)/shard_map/ppermute | solution.py:719
  92.6 17.4 %collective-permute-start.21 = (bf16[4,192,256]{2,1,0:T(8,128)(2,1)}, bf16[4,192,256]{2,1,0:T(8,128)(2,1)S(1)}, u32[]{:S(2)}, u32[]{:S(2)}) collective-permute-start(bf16[4,192,256]{2,1,0:T(8,128)(2,1)} %get-tuple-element.108), channel_id=1, source_target_pairs={{0,96},{8,104},{16,112},{24,120},{32,0},{40,8},{48,16},{56,24},{64... | collective-permute-start | bytes 1179656 | tf_op jit(solution)/shard_map/ppermute | solution.py:719
  95.6 9.5 %copy-start.7 = (f32[1,384]{1,0:T(1,128)S(1)}, f32[1,384]{1,0:T(1,128)}, u32[]{:S(2)}) copy-start(f32[1,384]{1,0:T(1,128)} %get-tuple-element.92) | copy-start | bytes 4612
  96.7 18.9 %copy-start.4 = (bf16[4,192,256]{2,1,0:T(8,128)(2,1)S(1)}, bf16[4,192,256]{2,1,0:T(8,128)(2,1)}, u32[]{:S(2)}) copy-start(bf16[4,192,256]{2,1,0:T(8,128)(2,1)} %get-tuple-element.118) | copy-start | bytes 1179652
  96.7 15.5 %all-to-all-start.2 = ((bf16[4,256,384]{2,1,0:T(8,128)(2,1)}), bf16[4,256,384]{2,1,0:T(8,128)(2,1)S(1)}, u32[]{:S(2)}, u32[]{:S(2)}) async-start(bf16[4,256,384]{2,1,0:T(8,128)(2,1)} %add_convert_fusion), calls=%async_computation.2 | async-start | bytes 1572864 | tf_op jit(solution)/shard_map/all_to_all | solution.py:923
  100.7 9.3 %collective-permute-start.19 = (bf16[592,128]{1,0:T(8,128)(2,1)S(1)}, bf16[592,128]{1,0:T(8,128)(2,1)S(1)}, u32[]{:S(2)}, u32[]{:S(2)}) collective-permute-start(bf16[592,128]{1,0:T(8,128)(2,1)S(1)} %pad_maximum_fusion), channel_id=1, source_target_pairs={{0,24},{8,0},{16,8},{24,16},{32,56},{40,32},{48,40},{56,48},{64,88... | collective-permute-start | bytes 454664 | tf_op jit(solution)/shard_map/ppermute | solution.py:719
  103.3 7.2 %collective-permute-start.18 = (bf16[592,128]{1,0:T(8,128)(2,1)S(1)}, bf16[592,128]{1,0:T(8,128)(2,1)S(1)}, u32[]{:S(2)}, u32[]{:S(2)}) collective-permute-start(bf16[592,128]{1,0:T(8,128)(2,1)S(1)} %pad_maximum_fusion), channel_id=1, source_target_pairs={{0,16},{8,24},{16,0},{24,8},{32,48},{40,56},{48,32},{56,40},{64,80... | collective-permute-start | bytes 454664 | tf_op jit(solution)/shard_map/ppermute | solution.py:719
  104.2 7.9 %collective-permute-start.17 = (bf16[592,128]{1,0:T(8,128)(2,1)S(1)}, bf16[592,128]{1,0:T(8,128)(2,1)S(1)}, u32[]{:S(2)}, u32[]{:S(2)}) collective-permute-start(bf16[592,128]{1,0:T(8,128)(2,1)S(1)} %pad_maximum_fusion), channel_id=1, source_target_pairs={{0,8},{8,16},{16,24},{24,0},{32,40},{40,48},{48,56},{56,32},{64,72... | collective-permute-start | bytes 454664 | tf_op jit(solution)/shard_map/ppermute | solution.py:719
  112.1 8.8 %copy-start.5 = (bf16[256,384]{1,0:T(8,128)(2,1)S(1)}, bf16[256,384]{1,0:T(8,128)(2,1)}, u32[]{:S(2)}) copy-start(bf16[256,384]{1,0:T(8,128)(2,1)} %get-tuple-element.91) | copy-start | bytes 589828
  112.2 7.5 %collective-permute-start.25 = (bf16[592,128]{1,0:T(8,128)(2,1)S(1)}, bf16[592,128]{1,0:T(8,128)(2,1)S(1)}, u32[]{:S(2)}, u32[]{:S(2)}) collective-permute-start(bf16[592,128]{1,0:T(8,128)(2,1)S(1)} %add_convert_fusion.4.refs_0_), channel_id=1, source_target_pairs={{0,96},{8,104},{16,112},{24,120},{32,0},{40,8},{48,16},{56,24},{64... | collective-permute-start | bytes 454664 | tf_op jit(solution)/shard_map/ppermute | solution.py:719
  113.9 7.8 %collective-permute-start.24 = (bf16[592,128]{1,0:T(8,128)(2,1)S(1)}, bf16[592,128]{1,0:T(8,128)(2,1)S(1)}, u32[]{:S(2)}, u32[]{:S(2)}) collective-permute-start(bf16[592,128]{1,0:T(8,128)(2,1)S(1)} %add_convert_fusion.4.refs_0_), channel_id=1, source_target_pairs={{0,64},{8,72},{16,80},{24,88},{32,96},{40,104},{48,112},{56,120},{... | collective-permute-start | bytes 454664 | tf_op jit(solution)/shard_map/ppermute | solution.py:719
  115.1 8.0 %collective-permute-start.23 = (bf16[592,128]{1,0:T(8,128)(2,1)S(1)}, bf16[592,128]{1,0:T(8,128)(2,1)S(1)}, u32[]{:S(2)}, u32[]{:S(2)}) collective-permute-start(bf16[592,128]{1,0:T(8,128)(2,1)S(1)} %add_convert_fusion.4.refs_0_), channel_id=1, source_target_pairs={{0,32},{8,40},{16,48},{24,56},{32,64},{40,72},{48,80},{56,88},{64,... | collective-permute-start | bytes 454664 | tf_op jit(solution)/shard_map/ppermute | solution.py:719
  115.8 7.3 %copy-start = (bf16[192,160]{1,0:T(8,128)(2,1)S(1)}, bf16[192,160]{1,0:T(8,128)(2,1)}, u32[]{:S(2)}) copy-start(bf16[192,160]{1,0:T(8,128)(2,1)} %get-tuple-element.125.refs_4_) | copy-start | bytes 184324
  115.9 8.3 %collective-permute-start.26 = (bf16[192,256]{1,0:T(8,128)(2,1)S(1)}, bf16[192,256]{1,0:T(8,128)(2,1)S(1)}, u32[]{:S(2)}, u32[]{:S(2)}) collective-permute-start(bf16[192,256]{1,0:T(8,128)(2,1)S(1)} %get-tuple-element.129), channel_id=1, source_target_pairs={{0,16},{8,24},{16,0},{24,8},{32,48},{40,56},{48,32},{56,40},{64,80... | collective-permute-start | bytes 294920 | tf_op jit(solution)/shard_map/ppermute | solution.py:719
  118.4 5.8 %collective-permute-start.28 = (bf16[192,256]{1,0:T(8,128)(2,1)S(1)}, bf16[192,256]{1,0:T(8,128)(2,1)S(1)}, u32[]{:S(2)}, u32[]{:S(2)}) collective-permute-start(bf16[192,256]{1,0:T(8,128)(2,1)S(1)} %get-tuple-element.130), channel_id=1, source_target_pairs={{0,24},{8,0},{16,8},{24,16},{32,56},{40,32},{48,40},{56,48},{64,88... | collective-permute-start | bytes 294920 | tf_op jit(solution)/shard_map/ppermute | solution.py:719
  119.7 5.9 %collective-permute-start.27 = (bf16[192,256]{1,0:T(8,128)(2,1)S(1)}, bf16[192,256]{1,0:T(8,128)(2,1)S(1)}, u32[]{:S(2)}, u32[]{:S(2)}) collective-permute-start(bf16[192,256]{1,0:T(8,128)(2,1)S(1)} %get-tuple-element.131), channel_id=1, source_target_pairs={{0,8},{8,16},{16,24},{24,0},{32,40},{40,48},{48,56},{56,32},{64,72... | collective-permute-start | bytes 294920 | tf_op jit(solution)/shard_map/ppermute | solution.py:719
  (1 other events, 0.6 us)
